TPU v7x, 32 devices: a whole 2x2x4 slice. The times are simulated.
32 devices in a mesh: dp: 4 (over z), row: 4 (over y, core), col: 2 (over x).
Axes of the slice: x: 2, y: 2, z: 4, core: 2. Of those that a mesh axis runs over, the one named last changes fastest.
Arguments:
- tokens: bfloat16 [768, 4096], P('row', ('dp', 'col')), may hold values from -6 to 6
- condition: bfloat16 [16, 768], P(('dp', 'row'), 'col'), may hold values from -6 to 6
- w_mod: bfloat16 [6, 768, 768], P(None, 'row', 'col'), may hold values from -0.21875 to 0.21875
- b_mod: bfloat16 [6, 768], P(None, 'row'), may hold values from -3 to 3
- w_query: bfloat16 [768, 768], P('row', 'col'), may hold values from -0.21875 to 0.21875
- w_key: bfloat16 [768, 768], P('row', 'col'), may hold values from -0.21875 to 0.21875
- w_value: bfloat16 [768, 768], P('row', 'col'), may hold values from -0.21875 to 0.21875
- b_query: bfloat16 [768], P('col'), may hold values from -3 to 3
- b_value: bfloat16 [768], P('col'), may hold values from -3 to 3
- w_out: bfloat16 [768, 768], P('row', 'col'), may hold values from -0.875 to 0.875
- b_out: bfloat16 [768], P('row'), may hold values from -2 to 2
- w_up: bfloat16 [768, 3072], P('row', 'col'), may hold values from -0.21875 to 0.21875
- b_up: bfloat16 [3072], P('col'), may hold values from -3 to 3
- w_down: bfloat16 [768, 3072], P('row', 'col'), may hold values from -0.109375 to 0.109375
- b_down: bfloat16 [768], P('row'), may hold values from -2 to 2
- cotangent: bfloat16 [768, 4096], P('row', ('dp', 'col')), may hold values from -6 to 6
Outputs:
- output: bfloat16 [768, 4096], P('row', ('dp', 'col'))
- grad_tokens: float32 [768, 4096], P('row', ('dp', 'col'))
- grad_condition: float32 [16, 768], P(('dp', 'row'), 'col')
- grad_w_mod: float32 [6, 768, 768], P(None, 'row', 'col')
- grad_b_mod: float32 [6, 768], P(None, 'row')
- grad_w_query: float32 [768, 768], P('row', 'col')
- grad_w_key: float32 [768, 768], P('row', 'col')
- grad_w_value: float32 [768, 768], P('row', 'col')
- grad_b_query: float32 [768], P('col')
- grad_b_value: float32 [768], P('col')
- grad_w_out: float32 [768, 768], P('row', 'col')
- grad_b_out: float32 [768], P('row')
- grad_w_up: float32 [768, 3072], P('row', 'col')
- grad_b_up: float32 [3072], P('col')
- grad_w_down: float32 [768, 3072], P('row', 'col')
- grad_b_down: float32 [768], P('row')
All inputs are finite; a program needn't handle non-finite values.
Results may differ from a plain program's by a relative error of at most 0.02.
Values may be sent and summed in bfloat16 or wider, within the bound.
A program may use at most 128 MiB of HBM per device.

v0:
```python
from functools import partial

import jax
import jax.numpy as jnp
from jax import lax
from jax.sharding import PartitionSpec as P

D = 768
HEAD_DIM = 64
LEN = 256


def product(left_side, right_side):
    return jnp.dot(left_side, right_side, preferred_element_type=jnp.float32)


def product_transposed(left_side, right_side):
    return lax.dot_general(
        left_side, right_side, (((1,), (1,)), ((), ())), preferred_element_type=jnp.float32
    )


def weight_product(inputs, gradients):
    return lax.dot_general(
        inputs, gradients, (((0,), (0,)), ((), ())), preferred_element_type=jnp.float32
    )


def forward_rows(local_part, weight):
    gathered = lax.all_gather(local_part, "col", axis=0, tiled=True)
    share_rows = gathered.shape[0] // lax.axis_size("row")

    def row_term(first_row, row_count):
        return product(gathered, weight)

    return (
        gathered,
        lax.psum_scatter(
            row_term(jnp.int32(0), share_rows * lax.axis_size("row")),
            "row",
            scatter_dimension=0,
            tiled=True,
        ),
    )


def forward_cols(local_part, weight):
    gathered = lax.all_gather(local_part, "row", axis=0, tiled=True)
    share_rows = gathered.shape[0] // lax.axis_size("col")

    def row_term(first_row, row_count):
        return product_transposed(gathered, weight)

    return (
        gathered,
        lax.psum_scatter(
            row_term(jnp.int32(0), share_rows * lax.axis_size("col")),
            "col",
            scatter_dimension=0,
            tiled=True,
        ),
    )


def backward_rows(grad_part, weight):
    gathered = lax.all_gather(grad_part, "row", axis=0, tiled=True)
    share_rows = gathered.shape[0] // lax.axis_size("col")

    def row_term(first_row, row_count):
        return product_transposed(gathered, weight)

    return (
        gathered,
        lax.psum_scatter(
            row_term(jnp.int32(0), lax.axis_size("col") * share_rows).astype(jnp.bfloat16),
            "col",
            scatter_dimension=0,
            tiled=True,
        ).astype(jnp.float32),
    )


def backward_cols(grad_part, weight):
    gathered = lax.all_gather(grad_part, "col", axis=0, tiled=True)
    share_rows = gathered.shape[0] // lax.axis_size("row")

    def row_term(first_row, row_count):
        return product(gathered, weight)

    return (
        gathered,
        lax.psum_scatter(
            row_term(jnp.int32(0), lax.axis_size("row") * share_rows).astype(jnp.bfloat16),
            "row",
            scatter_dimension=0,
            tiled=True,
        ).astype(jnp.float32),
    )


def row_totals(first_term, second_term):
    return lax.psum((jnp.sum(first_term, axis=-1), jnp.sum(second_term, axis=-1)), "row")


def normalize(values):
    row_total, squares = row_totals(values, values * values)
    centre = row_total / D
    spread = squares / D - centre * centre
    inverse = lax.rsqrt(spread + 1e-06)
    return ((values - centre[:, None]) * inverse[:, None], inverse)


def normalize_back(grad_normed, normed, inverse):
    row_total, mixed_total = row_totals(grad_normed, grad_normed * normed)
    return inverse[:, None] * (
        grad_normed - row_total[:, None] / D - normed * (mixed_total[:, None] / D)
    )


def per_latent(matrix, latents):
    return matrix.reshape(latents, LEN, matrix.shape[-1])


def body(
    tokens,
    condition,
    w_mod,
    b_mod,
    w_query,
    w_key,
    w_value,
    b_query,
    b_value,
    w_out,
    b_out,
    w_up,
    b_up,
    w_down,
    b_down,
    cotangent,
):
    width_row = tokens.shape[0]
    width_col = w_query.shape[1]
    latents = tokens.shape[1] // LEN
    input_float = tokens.astype(jnp.float32).T
    condition_float = condition.astype(jnp.float32)
    silu_cond = jax.nn.silu(condition_float).astype(jnp.bfloat16)
    mod_flat = w_mod.reshape(-1, w_mod.shape[2])
    cond_gathered, mod_terms = forward_cols(silu_cond, mod_flat)
    modulation = mod_terms.reshape(latents, 6, width_row) + b_mod.astype(jnp.float32)[None]
    shift_attn = modulation[:, 0][:, None, :]
    scale_attn = modulation[:, 1][:, None, :]
    gate_attn = modulation[:, 2][:, None, :]
    shift_mlp = modulation[:, 3][:, None, :]
    scale_mlp = modulation[:, 4][:, None, :]
    gate_mlp = modulation[:, 5][:, None, :]
    normed_attn, inverse_attn = normalize(input_float)
    hidden_attn = (
        (per_latent(normed_attn, latents) * (1.0 + scale_attn) + shift_attn)
        .reshape(-1, width_row)
        .astype(jnp.bfloat16)
    )
    w_joined = jnp.concatenate([w_query, w_key, w_value], axis=1)
    attn_gathered, joined = forward_rows(hidden_attn, w_joined)
    queries = (joined[:, :width_col] + b_query.astype(jnp.float32)).astype(jnp.bfloat16)
    keys_all = joined[:, width_col : 2 * width_col].astype(jnp.bfloat16)
    values_all = (joined[:, 2 * width_col :] + b_value.astype(jnp.float32)).astype(jnp.bfloat16)
    local_seqs = queries.shape[0] // LEN
    local_heads = width_col // HEAD_DIM
    scale_factor = HEAD_DIM ** (-0.5)

    def split_heads(matrix):
        return matrix.reshape(local_seqs, LEN, local_heads, HEAD_DIM)

    def score_block():
        return (
            jnp.einsum(
                "bqhe,bkhe->bhqk",
                split_heads(queries),
                split_heads(keys_all),
                preferred_element_type=jnp.float32,
            )
            * scale_factor
        )

    scores = score_block()
    row_peak = jnp.max(scores, axis=-1, keepdims=True)
    exponent = jnp.exp(scores - row_peak)
    denominator = jnp.sum(exponent, axis=-1, keepdims=True)
    probabilities = (exponent / denominator).astype(jnp.bfloat16)
    log_total = row_peak + jnp.log(denominator)
    attended = jnp.einsum(
        "bhqk,bkhe->bqhe",
        probabilities,
        split_heads(values_all),
        preferred_element_type=jnp.float32,
    )
    attended = attended.reshape(-1, width_col).astype(jnp.bfloat16)
    out_gathered, projected = forward_cols(attended, w_out)
    projected = projected + b_out.astype(jnp.float32)
    residual = per_latent(input_float, latents) + gate_attn * per_latent(projected, latents)
    residual_flat = residual.reshape(-1, width_row)
    normed_mlp, inverse_mlp = normalize(residual_flat)
    hidden_mlp = (
        (per_latent(normed_mlp, latents) * (1.0 + scale_mlp) + shift_mlp)
        .reshape(-1, width_row)
        .astype(jnp.bfloat16)
    )
    mlp_gathered, upward = forward_rows(hidden_mlp, w_up)
    upward = upward + b_up.astype(jnp.float32)
    activated = jax.nn.gelu(upward, approximate=True).astype(jnp.bfloat16)
    act_gathered, downward = forward_cols(activated, w_down)
    downward = downward + b_down.astype(jnp.float32)
    final_state = residual + gate_mlp * per_latent(downward, latents)
    output = final_state.reshape(-1, width_row).T.astype(jnp.bfloat16)
    grad_final = per_latent(cotangent.astype(jnp.float32).T, latents)
    grad_gate_mlp = jnp.sum(grad_final * per_latent(downward, latents), axis=1)
    grad_down = (grad_final * gate_mlp).reshape(-1, width_row).astype(jnp.bfloat16)
    gelu_value, gelu_back = jax.vjp(partial(jax.nn.gelu, approximate=True), upward)
    down_gathered, grad_activated = backward_cols(grad_down, w_down)
    grad_w_down = weight_product(down_gathered, act_gathered)
    grad_b_down = jnp.sum(down_gathered, axis=0, dtype=jnp.float32)
    grad_upward = gelu_back(grad_activated)[0].astype(jnp.bfloat16)
    up_gathered, grad_hidden_mlp = backward_rows(grad_upward, w_up)
    grad_w_up = weight_product(mlp_gathered, up_gathered)
    grad_b_up = jnp.sum(up_gathered, axis=0, dtype=jnp.float32)
    grad_hidden = per_latent(grad_hidden_mlp, latents)
    grad_scale_mlp = jnp.sum(grad_hidden * per_latent(normed_mlp, latents), axis=1)
    grad_shift_mlp = jnp.sum(grad_hidden, axis=1)
    grad_normed = (grad_hidden * (1.0 + scale_mlp)).reshape(-1, width_row)
    grad_residual = grad_final.reshape(-1, width_row) + normalize_back(
        grad_normed, normed_mlp, inverse_mlp
    )
    grad_res_latent = per_latent(grad_residual, latents)
    grad_gate_attn = jnp.sum(grad_res_latent * per_latent(projected, latents), axis=1)
    grad_projected = (grad_res_latent * gate_attn).reshape(-1, width_row).astype(jnp.bfloat16)
    proj_gathered, grad_attended = backward_cols(grad_projected, w_out)
    grad_w_out = weight_product(proj_gathered, out_gathered)
    grad_b_out = jnp.sum(proj_gathered, axis=0, dtype=jnp.float32)
    grad_heads = split_heads(grad_attended.astype(jnp.bfloat16))
    full_probs = jnp.exp(score_block() - log_total)
    grad_probs = jnp.einsum(
        "bqhe,bkhe->bhqk", grad_heads, split_heads(values_all), preferred_element_type=jnp.float32
    )
    grad_values = jnp.einsum(
        "bhqk,bqhe->bkhe",
        full_probs.astype(jnp.bfloat16),
        grad_heads,
        preferred_element_type=jnp.float32,
    )
    inner = jnp.sum(full_probs * grad_probs, axis=-1, keepdims=True)
    grad_scores = (full_probs * (grad_probs - inner)).astype(jnp.bfloat16)
    grad_queries = (
        jnp.einsum(
            "bhqk,bkhe->bqhe",
            grad_scores,
            split_heads(keys_all),
            preferred_element_type=jnp.float32,
        )
        * scale_factor
    )
    grad_keys = (
        jnp.einsum(
            "bhqk,bqhe->bkhe", grad_scores, split_heads(queries), preferred_element_type=jnp.float32
        )
        * scale_factor
    )
    grad_joined = jnp.concatenate(
        [
            grad_queries.reshape(-1, width_col),
            grad_keys.reshape(-1, width_col),
            grad_values.reshape(-1, width_col),
        ],
        axis=1,
    ).astype(jnp.bfloat16)
    joined_gathered, grad_hidden_attn = backward_rows(grad_joined, w_joined)
    grad_w_joined = weight_product(attn_gathered, joined_gathered)
    grad_b_joined = jnp.sum(joined_gathered, axis=0, dtype=jnp.float32)
    grad_w_query = grad_w_joined[:, :width_col]
    grad_w_key = grad_w_joined[:, width_col : 2 * width_col]
    grad_w_value = grad_w_joined[:, 2 * width_col :]
    grad_b_query = grad_b_joined[:width_col]
    grad_b_value = grad_b_joined[2 * width_col :]
    grad_hidden = per_latent(grad_hidden_attn, latents)
    grad_scale_attn = jnp.sum(grad_hidden * per_latent(normed_attn, latents), axis=1)
    grad_shift_attn = jnp.sum(grad_hidden, axis=1)
    grad_normed = (grad_hidden * (1.0 + scale_attn)).reshape(-1, width_row)
    grad_tokens = (grad_residual + normalize_back(grad_normed, normed_attn, inverse_attn)).T
    grad_modulation = jnp.stack(
        [
            grad_shift_attn,
            grad_scale_attn,
            grad_gate_attn,
            grad_shift_mlp,
            grad_scale_mlp,
            grad_gate_mlp,
        ],
        axis=1,
    )
    grad_modulation = grad_modulation.reshape(latents, -1).astype(jnp.bfloat16)
    modgrad_gathered, grad_silu = backward_cols(grad_modulation, mod_flat)
    grad_w_mod = weight_product(modgrad_gathered, cond_gathered).reshape(w_mod.shape)
    grad_b_mod = jnp.sum(modgrad_gathered, axis=0, dtype=jnp.float32).reshape(b_mod.shape)
    silu_value, silu_back = jax.vjp(jax.nn.silu, condition_float)
    grad_condition = silu_back(grad_silu)[0]
    (
        grad_w_mod,
        grad_b_mod,
        grad_w_query,
        grad_w_key,
        grad_w_value,
        grad_b_query,
        grad_b_value,
        grad_w_out,
        grad_b_out,
        grad_w_up,
        grad_b_up,
        grad_w_down,
        grad_b_down,
    ) = (
        lax.psum(grad_w_mod.astype(jnp.bfloat16), "dp").astype(jnp.float32),
        lax.psum(grad_b_mod.astype(jnp.bfloat16), "dp").astype(jnp.float32),
        lax.psum(grad_w_query.astype(jnp.bfloat16), "dp").astype(jnp.float32),
        lax.psum(grad_w_key.astype(jnp.bfloat16), "dp").astype(jnp.float32),
        lax.psum(grad_w_value.astype(jnp.bfloat16), "dp").astype(jnp.float32),
        lax.psum(grad_b_query.astype(jnp.bfloat16), "dp").astype(jnp.float32),
        lax.psum(grad_b_value.astype(jnp.bfloat16), "dp").astype(jnp.float32),
        lax.psum(grad_w_out.astype(jnp.bfloat16), "dp").astype(jnp.float32),
        lax.psum(grad_b_out.astype(jnp.bfloat16), "dp").astype(jnp.float32),
        lax.psum(grad_w_up.astype(jnp.bfloat16), "dp").astype(jnp.float32),
        lax.psum(grad_b_up.astype(jnp.bfloat16), "dp").astype(jnp.float32),
        lax.psum(grad_w_down.astype(jnp.bfloat16), "dp").astype(jnp.float32),
        lax.psum(grad_b_down.astype(jnp.bfloat16), "dp").astype(jnp.float32),
    )
    return (
        output,
        grad_tokens,
        grad_condition,
        grad_w_mod,
        grad_b_mod,
        grad_w_query,
        grad_w_key,
        grad_w_value,
        grad_b_query,
        grad_b_value,
        grad_w_out,
        grad_b_out,
        grad_w_up,
        grad_b_up,
        grad_w_down,
        grad_b_down,
    )


def solution(mesh):
    placed = (
        P("row", ("dp", "col")),
        P(("dp", "row"), "col"),
        P(None, "row", "col"),
        P(None, "row"),
        P("row", "col"),
        P("row", "col"),
        P("row", "col"),
        P("col"),
        P("col"),
        P("row", "col"),
        P("row"),
        P("row", "col"),
        P("col"),
        P("row", "col"),
        P("row"),
        P("row", ("dp", "col")),
    )
    return jax.shard_map(
        body,
        mesh=mesh,
        in_specs=placed,
        out_specs=(
            P("row", ("dp", "col")),
            P("row", ("dp", "col")),
            P(("dp", "row"), "col"),
            P(None, "row", "col"),
            P(None, "row"),
            P("row", "col"),
            P("row", "col"),
            P("row", "col"),
            P("col"),
            P("col"),
            P("row", "col"),
            P("row"),
            P("row", "col"),
            P("col"),
            P("row", "col"),
            P("row"),
        ),
        check_vma=False,
    )
```

profile of v0, /device:TPU:0, one launch (start us, length us, event | category | flops | bytes accessed | tf_op | source)
XLA Modules:
  0.0 552.6 jit_solution(15931967011914610268)
XLA Ops:
  10.5 6.1 %all-gather = bf16[4,1,384]{2,1,0:T(2,128)(2,1)S(1)} all-gather(bf16[1,1,384]{2,1,0:T(2,128)(2,1)S(1)} %get-tuple-element.52), channel_id=1, replica_groups=mesh['dp'=4,'row'=4,'col'=2] {'row'}, dimensions={0}, use_global_device_ids=true | all-gather | bytes 3840 | tf_op jit(solution)/shard_map/all_gather | solution.py:48
  17.6 8.9 %all-reduce = f32[4,1152]{1,0:T(4,128)S(1)} all-reduce(f32[4,1152]{1,0:T(4,128)S(1)} %fusion.28), channel_id=2, replica_groups=mesh['dp'=4,'row'=4,'col'=2] {'col'}, use_global_device_ids=true, to_apply=%region_0.1.clone | all-reduce | flops 4608 | bytes 36864
  30.7 5.8 %all-reduce.5 = (f32[512]{0:T(512)S(1)}, f32[512]{0:T(512)S(1)}) all-reduce(f32[512]{0:T(512)S(1)} %fusion.20, f32[512]{0:T(512)S(1)} %convert_reduce_fusion), channel_id=1, replica_groups=mesh['dp'=4,'row'=4,'col'=2] {'row'}, use_global_device_ids=true, to_apply=%region_4.5 | all-reduce | flops 1024 | bytes 8192 | tf_op jit(solution)/shard_map/psum | solution.py:102
  37.3 7.3 %all_gather.31 = bf16[1024,192]{0,1:T(8,128)(2,1)S(1)} all-gather(bf16[512,192]{0,1:T(8,128)(2,1)S(1)} %get-tuple-element.64), channel_id=1, replica_groups=mesh['dp'=4,'row'=4,'col'=2] {'col'}, dimensions={0}, use_global_device_ids=true | all-gather | bytes 589824 | tf_op jit(solution)/shard_map/all_gather | solution.py:30
  50.0 47.6 %reduce-scatter.9.cloned.1.call-done = f32[256,1152]{1,0:T(8,128)} async-done(((f32[1024,1152]{1,0:T(8,128)}), f32[256,1152]{1,0:T(8,128)}) %reduce-scatter.9.cloned.1.call-update) | async-done | bytes 1179664 | tf_op jit(solution)/shard_map/reduce_scatter | solution.py:38
  101.7 8.2 %all_gather.32 = bf16[1024,384]{0,1:T(8,128)(2,1)S(1)} all-gather(bf16[256,384]{0,1:T(8,128)(2,1)S(1)} %bitcast.195), channel_id=1, replica_groups=mesh['dp'=4,'row'=4,'col'=2] {'row'}, dimensions={0}, use_global_device_ids=true | all-gather | bytes 983040 | tf_op jit(solution)/shard_map/all_gather | solution.py:48
  113.4 9.0 %all_gather.35 = bf16[1024,192]{0,1:T(8,128)(2,1)S(1)} all-gather(bf16[512,192]{0,1:T(8,128)(2,1)S(1)} %fusion.23), channel_id=1, replica_groups=mesh['dp'=4,'row'=4,'col'=2] {'col'}, dimensions={0}, use_global_device_ids=true | all-gather | bytes 589824 | tf_op jit(solution)/shard_map/all_gather | solution.py:84
  122.4 3.9 convolution_convert_fusion
  133.2 5.7 %all-reduce.4 = (f32[512]{0:T(512)S(1)}, f32[512]{0:T(512)S(1)}) all-reduce(f32[512]{0:T(512)S(1)} %get-tuple-element.25, f32[512]{0:T(512)S(1)} %get-tuple-element.24), channel_id=1, replica_groups=mesh['dp'=4,'row'=4,'col'=2] {'row'}, use_global_device_ids=true, to_apply=%region_12.13 | all-reduce | flops 1024 | bytes 8192 | tf_op jit(solution)/shard_map/psum | solution.py:102
  140.4 8.0 %all_gather.33 = bf16[1024,192]{0,1:T(8,128)(2,1)S(1)} all-gather(bf16[512,192]{0,1:T(8,128)(2,1)S(1)} %get-tuple-element.49), channel_id=1, replica_groups=mesh['dp'=4,'row'=4,'col'=2] {'col'}, dimensions={0}, use_global_device_ids=true | all-gather | bytes 589824 | tf_op jit(solution)/shard_map/all_gather | solution.py:30
  149.1 3.7 fusion.40
  153.5 18.1 %reduce-scatter.17.cloned.1.call-done = bf16[256,1536]{1,0:T(8,128)(2,1)} async-done(((bf16[1024,1536]{1,0:T(8,128)(2,1)}), bf16[256,1536]{1,0:T(8,128)(2,1)}) %reduce-scatter.17.cloned.1.call-update) | async-done | bytes 786448 | tf_op jit(solution)/shard_map/reduce_scatter | solution.py:92
  171.6 61.0 %reduce-scatter.13.cloned.1.call-done = f32[256,1536]{1,0:T(8,128)} async-done(((f32[1024,1536]{1,0:T(8,128)}), f32[256,1536]{1,0:T(8,128)}) %reduce-scatter.13.cloned.1.call-update) | async-done | bytes 1572880 | tf_op jit(solution)/shard_map/reduce_scatter | solution.py:38
  232.5 4.0 fusion.2
  237.2 28.1 %all-gather.8.cloned.1.call-done = bf16[1024,1536]{1,0:T(8,128)(2,1)} async-done(((bf16[256,1536]{1,0:T(8,128)(2,1)}), bf16[1024,1536]{1,0:T(8,128)(2,1)}) %all-gather.8.cloned.1.call-update) | async-done | bytes 3145744 | tf_op jit(solution)/shard_map/all_gather | solution.py:66
  265.3 3.9 convolution_convert_fusion.7
  269.3 26.5 %all-gather.6.cloned.1.call-done = bf16[1024,1536]{1,0:T(8,128)(2,1)} async-done(((bf16[256,1536]{1,0:T(8,128)(2,1)}), bf16[1024,1536]{1,0:T(8,128)(2,1)}) %all-gather.6.cloned.1.call-update) | async-done | bytes 3145744 | tf_op jit(solution)/shard_map/all_gather | solution.py:48
  295.8 4.1 fusion.41
  300.0 11.8 %reduce-scatter.19.cloned.1.call-done = bf16[512,192]{0,1:T(8,128)(2,1)} async-done(((bf16[1024,192]{0,1:T(8,128)(2,1)}), bf16[512,192]{0,1:T(8,128)(2,1)}) %reduce-scatter.19.cloned.1.call-update) | async-done | bytes 196624 | tf_op jit(solution)/shard_map/reduce_scatter | solution.py:74
  312.9 7.1 %all-reduce.3 = (f32[512]{0:T(512)S(1)}, f32[512]{0:T(512)S(1)}) all-reduce(f32[512]{0:T(512)S(1)} %get-tuple-element.19, f32[512]{0:T(512)S(1)} %get-tuple-element.18), channel_id=1, replica_groups=mesh['dp'=4,'row'=4,'col'=2] {'row'}, use_global_device_ids=true, to_apply=%region_20.21 | all-reduce | flops 1024 | bytes 8192 | tf_op jit(solution)/shard_map/psum | solution.py:102
  320.0 12.2 %reduce-scatter.15.cloned.1.call-done = f32[512,192]{0,1:T(8,128)} async-done(((f32[1024,192]{0,1:T(8,128)}), f32[512,192]{0,1:T(8,128)}) %reduce-scatter.15.cloned.1.call-update) | async-done | bytes 393232 | tf_op jit(solution)/shard_map/reduce_scatter | solution.py:56
  335.7 7.4 %all_gather.37 = bf16[1024,192]{0,1:T(8,128)(2,1)S(1)} all-gather(bf16[512,192]{0,1:T(8,128)(2,1)S(1)} %multiply_convert_fusion.2), channel_id=1, replica_groups=mesh['dp'=4,'row'=4,'col'=2] {'col'}, dimensions={0}, use_global_device_ids=true | all-gather | bytes 589824 | tf_op jit(solution)/shard_map/all_gather | solution.py:84
  345.3 23.3 %reduce-scatter.21.cloned.1.call-done = bf16[256,384]{1,0:T(8,128)(2,1)} async-done(((bf16[1024,384]{1,0:T(8,128)(2,1)}), bf16[256,384]{1,0:T(8,128)(2,1)}) %reduce-scatter.21.cloned.1.call-update) | async-done | bytes 196624 | tf_op jit(solution)/shard_map/reduce_scatter | solution.py:92
  376.6 3.6 convolution_convert_fusion.3
  386.4 13.1 %all-gather.10.cloned.1.call-done = bf16[1024,1152]{0,1:T(8,128)(2,1)} async-done(((bf16[256,1152]{0,1:T(8,128)(2,1)}), bf16[1024,1152]{0,1:T(8,128)(2,1)}) %all-gather.10.cloned.1.call-update) | async-done | bytes 2359312 | tf_op jit(solution)/shard_map/all_gather | solution.py:66
  399.6 3.4 convolution_convert_fusion.6
  408.1 8.1 %reduce-scatter.23.cloned.1.call-done = bf16[512,192]{0,1:T(8,128)(2,1)} async-done(((bf16[1024,192]{0,1:T(8,128)(2,1)}), bf16[512,192]{0,1:T(8,128)(2,1)}) %reduce-scatter.23.cloned.1.call-update) | async-done | bytes 196624 | tf_op jit(solution)/shard_map/reduce_scatter | solution.py:74
  424.1 4.3 all-gather.1
  435.7 19.8 %all-reduce.6 = (bf16[6,192]{1,0:T(8,128)(2,1)S(1)}, bf16[384]{0:T(512)(128)(2,1)S(1)}, bf16[384]{0:T(512)(128)(2,1)S(1)}, bf16[192]{0:T(256)(128)(2,1)S(1)}, bf...) all-reduce(bf16[6,192]{1,0:T(8,128)(2,1)S(1)} %convert_element_type, ...), channel_id=1, replica_groups=mesh['dp'=4,'row'=4,'col'=2] {'dp'}, use_global_device_ids=true, to_apply=%region_37.38 | all-reduce | flops 3840 | bytes 15360 | tf_op jit(solution)/shard_map/psum | solution.py:322
  460.1 6.1 %all-reduce.2 = (f32[512]{0:T(512)S(1)}, f32[512]{0:T(512)S(1)}) all-reduce(f32[512]{0:T(512)S(1)} %get-tuple-element.17, f32[512]{0:T(512)S(1)} %get-tuple-element.16), channel_id=1, replica_groups=mesh['dp'=4,'row'=4,'col'=2] {'row'}, use_global_device_ids=true, to_apply=%region_27.28 | all-reduce | flops 1024 | bytes 8192 | tf_op jit(solution)/shard_map/psum | solution.py:102
  466.3 6.7 %all-reduce.1 = bf16[4,384]{1,0:T(4,128)(2,1)S(1)} all-reduce(bf16[4,384]{1,0:T(4,128)(2,1)S(1)} %convolution_convert_fusion.11), channel_id=11, replica_groups=mesh['dp'=4,'row'=4,'col'=2] {'row'}, use_global_device_ids=true, to_apply=%region_34.35.clone | all-reduce | flops 1536 | bytes 6144
  475.2 62.7 %all-reduce.10.cloned.1.call-done = (bf16[6,192,384]{2,1,0:T(8,128)(2,1)}, bf16[192,384]{1,0:T(8,128)(2,1)}, bf16[192,384]{1,0:T(8,128)(2,1)}, bf16[192,384]{1,0...) async-done(((bf16[6,192,384]{2,1,0:T(8,128)(2,1)}, bf16[192,384]{1,0:T(8,128)(2,1)}, bf16[192,384]{1,0:T(8,128)(2,1)}, ...) | async-done | bytes 2654224 | tf_op jit(solution)/shard_map/psum | solution.py:321
  (257 shorter events, 87.5 us)
Async XLA Ops:
  7.2 9.5 %copy-start = (bf16[6,192,384]{2,1,0:T(8,128)(2,1)S(1)}, bf16[6,192,384]{2,1,0:T(8,128)(2,1)}, u32[]{:S(2)}) copy-start(bf16[6,192,384]{2,1,0:T(8,128)(2,1)} %param.18) | copy-start | bytes 2654212
  7.2 90.4 %reduce-scatter.9.cloned.1.call-start = ((), (), s32[]{:S(2)}) async-start(), calls=%async_computation.8 | async-start | bytes 5898240 | tf_op jit(solution)/shard_map/reduce_scatter | solution.py:38
  17.6 18.9 %copy-start.3 = (bf16[192,512]{1,0:T(8,128)(2,1)S(1)}, bf16[192,512]{1,0:T(8,128)(2,1)}, u32[]{:S(2)}) copy-start(bf16[192,512]{1,0:T(8,128)(2,1)} %param.16) | copy-start | bytes 589828
  30.2 14.5 %copy-start.5 = (f32[24,8,2,256]{3,1,2,0:T(8,128)}, f32[24,8,2,256]{3,1,2,0:T(8,128)S(1)}, u32[]{:S(2)}) copy-start(f32[24,8,2,256]{3,1,2,0:T(8,128)S(1)} %copy.133) | copy-start | bytes 1179652
  30.6 14.1 %copy-start.39 = (bf16[192,384]{1,0:T(8,128)(2,1)S(1)}, bf16[192,384]{1,0:T(8,128)(2,1)}, u32[]{:S(2)}) copy-start(bf16[192,384]{1,0:T(8,128)(2,1)} %param.20) | copy-start | bytes 442372
  30.6 14.1 %copy-start.40 = (bf16[192,384]{1,0:T(8,128)(2,1)S(1)}, bf16[192,384]{1,0:T(8,128)(2,1)}, u32[]{:S(2)}) copy-start(bf16[192,384]{1,0:T(8,128)(2,1)} %param.21) | copy-start | bytes 442372
  30.6 14.1 %copy-start.41 = (bf16[192,384]{1,0:T(8,128)(2,1)S(1)}, bf16[192,384]{1,0:T(8,128)(2,1)}, u32[]{:S(2)}) copy-start(bf16[192,384]{1,0:T(8,128)(2,1)} %param.22) | copy-start | bytes 442372
  49.3 82.0 %reduce-scatter.11.cloned.1.call-start = ((), (), s32[]{:S(2)}) async-start(), calls=%async_computation.9 | async-start | bytes 1179648 | tf_op jit(solution)/shard_map/reduce_scatter | solution.py:56
  101.1 9.7 %copy-start.32 = (bf16[192,384]{1,0:T(8,128)(2,1)S(1)}, bf16[192,384]{1,0:T(8,128)(2,1)}, u32[]{:S(2)}) copy-start(bf16[192,384]{1,0:T(8,128)(2,1)} %param.25) | copy-start | bytes 442372
  112.1 59.5 %reduce-scatter.17.cloned.1.call-start = ((), (), s32[]{:S(2)}) async-start(), calls=%async_computation.13 | async-start | bytes 3932160 | tf_op jit(solution)/shard_map/reduce_scatter | solution.py:92
  122.4 257.8 %copy-start.2 = (bf16[1024,192]{0,1:T(8,128)(2,1)}, bf16[1024,192]{0,1:T(8,128)(2,1)S(1)}, u32[]{:S(2)}) copy-start(bf16[1024,192]{0,1:T(8,128)(2,1)S(1)} %all_gather.35) | copy-start | bytes 1179652
  126.3 106.2 %reduce-scatter.13.cloned.1.call-start = ((), (), s32[]{:S(2)}) async-start(), calls=%async_computation.10 | async-start | bytes 7864320 | tf_op jit(solution)/shard_map/reduce_scatter | solution.py:38
  127.0 6.2 %copy-start.11 = (f32[24,8,2,256]{3,1,2,0:T(8,128)}, f32[24,8,2,256]{3,1,2,0:T(8,128)S(1)}, u32[]{:S(2)}) copy-start(f32[24,8,2,256]{3,1,2,0:T(8,128)S(1)} %copy.132) | copy-start | bytes 1179652
  138.9 10.2 %copy-start.34 = (bf16[192,1536]{1,0:T(8,128)(2,1)S(1)}, bf16[192,1536]{1,0:T(8,128)(2,1)}, u32[]{:S(2)}) copy-start(bf16[192,1536]{1,0:T(8,128)(2,1)} %param.27) | copy-start | bytes 1769476
  152.8 112.5 %all-gather.8.cloned.1.call-start = ((), (), s32[]{:S(2)}) async-start(), calls=%async_computation.14 | async-start | bytes 3932160 | tf_op jit(solution)/shard_map/all_gather | solution.py:66
  236.6 59.2 %all-gather.6.cloned.1.call-start = ((), (), s32[]{:S(2)}) async-start(), calls=%async_computation.11 | async-start | bytes 3932160 | tf_op jit(solution)/shard_map/all_gather | solution.py:48
  237.2 74.6 %reduce-scatter.19.cloned.1.call-start = ((), (), s32[]{:S(2)}) async-start(), calls=%async_computation.15 | async-start | bytes 589824 | tf_op jit(solution)/shard_map/reduce_scatter | solution.py:74
  269.2 30.7 %copy-start.53 = (bf16[192]{0:T(256)(128)(2,1)S(1)}, bf16[192]{0:T(256)(128)(2,1)}, u32[]{:S(2)}) copy-start(bf16[192]{0:T(256)(128)(2,1)} %param.30) | copy-start | bytes 1156
  269.2 62.9 %reduce-scatter.15.cloned.1.call-start = ((), (), s32[]{:S(2)}) async-start(), calls=%async_computation.12 | async-start | bytes 1179648 | tf_op jit(solution)/shard_map/reduce_scatter | solution.py:56
  299.9 32.3 %copy-start.49 = (f32[192]{0:T(256)S(1)}, f32[192]{0:T(256)}, u32[]{:S(2)}) copy-start(f32[192]{0:T(256)} %convert_element_type.204) | copy-start | bytes 2308
  299.9 68.7 %reduce-scatter.21.cloned.1.call-start = ((), (), s32[]{:S(2)}) async-start(), calls=%async_computation.16 | async-start | bytes 983040 | tf_op jit(solution)/shard_map/reduce_scatter | solution.py:92
  334.9 9.0 %copy-start.33 = (bf16[192,384]{1,0:T(8,128)(2,1)S(1)}, bf16[192,384]{1,0:T(8,128)(2,1)}, u32[]{:S(2)}) copy-start(bf16[192,384]{1,0:T(8,128)(2,1)} %param.25) | copy-start | bytes 442372
  335.7 9.6 %copy-start.43 = (f32[6,256]{1,0:T(8,128)S(1)}, f32[6,256]{1,0:T(8,128)}, u32[]{:S(2)}) copy-start(f32[6,256]{1,0:T(8,128)} %copy-done.42) | copy-start | bytes 18436
  345.3 54.3 %all-gather.10.cloned.1.call-start = ((), (), s32[]{:S(2)}) async-start(), calls=%async_computation.17 | async-start | bytes 2949120 | tf_op jit(solution)/shard_map/all_gather | solution.py:66
  375.1 41.2 %reduce-scatter.23.cloned.1.call-start = ((), (), s32[]{:S(2)}) async-start(), calls=%async_computation.18 | async-start | bytes 589824 | tf_op jit(solution)/shard_map/reduce_scatter | solution.py:74
  403.0 134.9 %all-reduce.10.cloned.1.call-start = ((), (), s32[]{:S(2)}) async-start(), calls=%async_computation.19 | async-start | bytes 5308416 | tf_op jit(solution)/shard_map/psum | solution.py:321
  407.3 21.1 %copy-start.45 = (bf16[4,1,384]{2,1,0:T(2,128)(2,1)S(1)}, bf16[4,1,384]{2,1,0:T(2,128)(2,1)}, u32[]{:S(2)}) copy-start(bf16[4,1,384]{2,1,0:T(2,128)(2,1)} %copy-done.44) | copy-start | bytes 9220
  435.1 37.9 %copy-start.46 = (bf16[1,384]{1,0:T(2,128)(2,1)S(1)}, bf16[1,384]{1,0:T(2,128)(2,1)}, u32[]{:S(2)}) copy-start(bf16[1,384]{1,0:T(2,128)(2,1)} %param.17) | copy-start | bytes 2308
  435.1 37.9 %copy-start.47 = (f32[1,384]{1,0:T(1,128)S(1)}, f32[1,384]{1,0:T(1,128)}, u32[]{:S(2)}) copy-start(f32[1,384]{1,0:T(1,128)} %get-tuple-element.53) | copy-start | bytes 4612
  435.5 38.8 %copy-start.6 = (f32[24,8,2,256]{3,1,2,0:T(8,128)S(1)}, f32[24,8,2,256]{3,1,2,0:T(8,128)}, u32[]{:S(2)}) copy-start(f32[24,8,2,256]{3,1,2,0:T(8,128)} %copy-done.5) | copy-start | bytes 1179652
  435.5 38.8 %copy-start.15 = (f32[512,192]{0,1:T(8,128)S(1)}, f32[512,192]{0,1:T(8,128)}, u32[]{:S(2)}) copy-start(f32[512,192]{0,1:T(8,128)} %copy-done.14) | copy-start | bytes 1179652
  435.5 38.8 %copy-start.18 = (bf16[512,192]{0,1:T(8,128)(2,1)S(1)}, bf16[512,192]{0,1:T(8,128)(2,1)}, u32[]{:S(2)}) copy-start(bf16[512,192]{0,1:T(8,128)(2,1)} %reduce-scatter.23.cloned.1.call-done) | copy-start | bytes 589828
  (35 other events, 60.1 us)
Sparse Core Ops, SparseCore 0:
  49.4 48.1 reduce-scatter.8
  112.2 18.4 reduce-scatter.10
  133.2 38.3 reduce-scatter.16
  174.1 58.3 reduce-scatter.12
  236.7 28.5 all-gather.7
  267.3 28.5 all-gather.5
  298.7 13.1 reduce-scatter.18
  314.7 17.4 reduce-scatter.14
  345.4 23.2 reduce-scatter.20
  375.2 24.3 all-gather.9
  403.1 13.1 reduce-scatter.22
  430.0 107.8 all-reduce.9
where the time goes:
time: 554 us; the launch traced here: 553 us
  waiting for transfers between devices  313 us (56%)
  blocking collectives  110 us (20%)
  other arithmetic  42.6 us (8%)
  matrix products  39.3 us (7%)
  local copies, waits for them, and re-layouts  31 us (6%)
  between operations  15.5 us (3%)
    reduce_scatter x2, waiting for transfers between devices, forward_rows(): lax.psum_scatter(row_term(jnp.int32(0), share_rows * lax.axis_size('row')...  109 us
    psum x1, waiting for transfers between devices, body(): lax.psum(grad_w_mod.astype(jnp.bfloat16), 'dp').astype(jnp.float32)  62.7 us
    reduce_scatter x2, waiting for transfers between devices, backward_cols(): lax.psum_scatter(row_term(jnp.int32(0), lax.axis_size('row') * share_rows...  41.4 us
    all_gather x2, waiting for transfers between devices, backward_rows(): gathered = lax.all_gather(grad_part, 'row', axis=0, tiled=True)  41.2 us
    all_gather x1, waiting for transfers between devices, forward_cols(): gathered = lax.all_gather(local_part, 'row', axis=0, tiled=True)  26.5 us
    psum x4, blocking collectives, row_totals(): lax.psum((jnp.sum(first_term, axis=-1), jnp.sum(second_term, axis=-1)), '...  24.6 us
    all_gather x3, blocking collectives, backward_cols(): gathered = lax.all_gather(grad_part, 'col', axis=0, tiled=True)  20.8 us
    reduce_scatter x2, waiting for transfers between devices, backward_rows(): lax.psum_scatter(row_term(jnp.int32(0), lax.axis_size('col') * share_rows...  19.9 us
  transfers between devices with their start and end apart: 12, of which 11 were waited for; matrix products, arithmetic and copies ran while one was open for 10% of the time, Pallas kernels for 0%

commit v1 on v0

v1 whole, which is shorter than its diff:
```python
from functools import partial

import jax
import jax.numpy as jnp
from jax import lax
from jax.sharding import PartitionSpec as P

D = 768
HEAD_DIM = 64
LEN = 256
ORDER = (0, 2, 1, 3)
F32 = jnp.float32
BF16 = jnp.bfloat16


def contract(left, right, left_dim, right_dim):
    return lax.dot_general(
        left, right, (((left_dim,), (right_dim,)), ((), ())), preferred_element_type=F32
    )


def contract_heads(left, right, left_dim, right_dim):
    return lax.dot_general(
        left, right, (((left_dim,), (right_dim,)), ((0,), (0,))), preferred_element_type=F32
    )


def swap_row(value, offset):
    size = lax.axis_size("row")
    return lax.ppermute(value, "row", [(i, i ^ offset) for i in range(size)])


def swap_col(value):
    return lax.ppermute(value, "col", [(0, 1), (1, 0)])


def after(value, earlier):
    return lax.optimization_barrier((value, earlier))[0]


def gather_row(shard, far=None):
    if far is None:
        far = swap_row(shard, 2)
    return jnp.concatenate([shard, far, swap_row(shard, 1), swap_row(far, 1)], axis=0)


def pair_sum(partial_sum):
    mine = partial_sum.astype(BF16)
    return mine.astype(F32) + swap_col(mine).astype(F32)


def scatter_row(full):
    half = full.shape[0] // 2
    quarter = half // 2
    near = full[:half].astype(F32) + swap_row(full[half:], 1).astype(F32)
    near = near.astype(BF16)
    own = near[:quarter].astype(F32) + swap_row(near[quarter:], 2).astype(F32)
    return own.astype(BF16)


def sum_dp(value):
    size = lax.axis_size("dp")
    place = lax.axis_index("dp") % 4
    inner = jnp.logical_or(place == 1, place == 2)
    inward = [(i, i + 1) if i % 4 == 0 else (i, i - 1) for i in range(size) if i % 4 in (0, 3)]
    middle = [(i, i ^ 3) for i in range(size) if i % 4 in (1, 2)]
    outward = [(b, a) for a, b in inward]
    first = (value.astype(F32) + lax.ppermute(value, "dp", inward).astype(F32)).astype(BF16)
    total = first.astype(F32) + lax.ppermute(first, "dp", middle).astype(F32)
    total = total.astype(BF16)
    step = 4
    while step < size:
        other = lax.ppermute(total, "dp", [(i, i ^ step) for i in range(size)])
        total = (total.astype(F32) + other.astype(F32)).astype(BF16)
        step *= 2
    back = lax.ppermute(total, "dp", outward)
    return jnp.where(inner, total, back).astype(F32)


def latent_of(local, row, col):
    per_col = local.shape[1] // LEN
    both = jnp.concatenate([local, swap_col(local)], axis=1)

    def block(latent):
        place = jnp.where(latent // per_col == col, 0, per_col) + latent % per_col
        return lax.dynamic_slice_in_dim(both, place * LEN, LEN, axis=1)

    return jnp.concatenate(
        [block(row)] + [swap_row(block(row ^ k), k) for k in ORDER[1:]], axis=0
    )


def spread_out(full, row, col):
    rows, cols = lax.axis_size("row"), lax.axis_size("col")
    per_col = rows // cols
    width = full.shape[0] // rows
    got = {0: full[:width]}
    for place, k in enumerate(ORDER):
        if k:
            pairs = [(r * cols + r // per_col, (r ^ k) * cols + r // per_col) for r in range(rows)]
            got[k] = lax.ppermute(
                full[place * width : (place + 1) * width], ("row", "col"), pairs
            )
    here = row // per_col == col
    first = jnp.where(here, got[0], got[2])
    second = jnp.where(here, got[1], got[3])
    even = row % 2 == 0
    return jnp.concatenate(
        [jnp.where(even, first, second), jnp.where(even, second, first)], axis=1
    )


def normalize(values):
    centre = jnp.mean(values, axis=0, keepdims=True)
    moved = values - centre
    inverse = lax.rsqrt(jnp.mean(moved * moved, axis=0, keepdims=True) + 1e-06)
    return moved * inverse, inverse


def normalize_back(grad, normed, inverse):
    return inverse * (
        grad
        - jnp.mean(grad, axis=0, keepdims=True)
        - normed * jnp.mean(grad * normed, axis=0, keepdims=True)
    )


def body(
    tokens,
    condition,
    w_mod,
    b_mod,
    w_query,
    w_key,
    w_value,
    b_query,
    b_value,
    w_out,
    b_out,
    w_up,
    b_up,
    w_down,
    b_down,
    cotangent,
):
    row = lax.axis_index("row")
    col = lax.axis_index("col")
    rows = lax.axis_size("row")
    width_row = tokens.shape[0]
    width_col = w_query.shape[1]
    heads = width_col // HEAD_DIM

    w_joined_own = jnp.concatenate([w_query, w_key, w_value], axis=1)
    far_joined = swap_row(w_joined_own, 2)
    far_out = swap_row(after(w_out, far_joined), 2)
    far_up = swap_row(after(w_up, far_out), 2)
    far_down = swap_row(after(w_down, far_up), 2)
    w_joined = gather_row(w_joined_own, far_joined)
    w_out_all = gather_row(w_out, far_out)
    w_up_all = gather_row(w_up, far_up)
    w_down_all = gather_row(w_down, far_down)

    condition_float = condition.astype(F32)
    silu_cond = jax.nn.silu(condition_float).astype(BF16)
    cond_rows = jnp.concatenate(
        [silu_cond] + [swap_row(silu_cond, k) for k in ORDER[1:]], axis=0
    )
    mod_flat = w_mod.reshape(-1, w_mod.shape[2])
    terms = contract(cond_rows, mod_flat, 1, 1)
    terms = terms + swap_col(terms)
    terms = terms.reshape(rows, 6, width_row) + b_mod.astype(F32)[None]
    extra = jnp.stack([b_out, b_down]).astype(F32)
    packed = jnp.concatenate([terms, jnp.broadcast_to(extra[None], (rows, 2, width_row))], axis=1)
    vectors = jnp.concatenate(
        [packed[0]] + [swap_row(packed[i], k) for i, k in enumerate(ORDER) if k], axis=1
    )
    columns = vectors.T
    shift_attn, scale_attn, gate_attn, shift_mlp, scale_mlp, gate_mlp, bias_out, bias_down = (
        columns[:, i : i + 1] for i in range(8)
    )

    x = latent_of(tokens, row, col).astype(F32)
    normed_attn, inverse_attn = normalize(x)
    hidden_attn = (normed_attn * (1.0 + scale_attn) + shift_attn).astype(BF16)
    joined = contract(w_joined, hidden_attn, 0, 0)

    def split_heads(matrix):
        return matrix.reshape(heads, HEAD_DIM, LEN)

    queries = split_heads((joined[:width_col] + b_query.astype(F32)[:, None]).astype(BF16))
    keys = split_heads(joined[width_col : 2 * width_col].astype(BF16))
    values = split_heads((joined[2 * width_col :] + b_value.astype(F32)[:, None]).astype(BF16))
    scale_factor = HEAD_DIM ** (-0.5)
    scores = contract_heads(queries, keys, 1, 1) * scale_factor
    exponent = jnp.exp(scores - jnp.max(scores, axis=-1, keepdims=True))
    full_probs = exponent / jnp.sum(exponent, axis=-1, keepdims=True)
    probabilities = full_probs.astype(BF16)
    attended = contract_heads(values, probabilities, 2, 2).reshape(width_col, LEN).astype(BF16)
    projected = pair_sum(contract(w_out_all, attended, 1, 0)) + bias_out
    residual = x + gate_attn * projected

    normed_mlp, inverse_mlp = normalize(residual)
    hidden_mlp = (normed_mlp * (1.0 + scale_mlp) + shift_mlp).astype(BF16)
    upward = contract(w_up_all, hidden_mlp, 0, 0) + b_up.astype(F32)[:, None]
    activated, gelu_back = jax.vjp(partial(jax.nn.gelu, approximate=True), upward)
    activated = activated.astype(BF16)
    downward = pair_sum(contract(w_down_all, activated, 1, 0)) + bias_down
    output = spread_out((residual + gate_mlp * downward).astype(BF16), row, col)

    cot = latent_of(cotangent, row, col).astype(F32)
    grad_gate_mlp = jnp.sum(cot * downward, axis=1)
    grad_down = (cot * gate_mlp).astype(BF16)
    grad_activated = contract(w_down_all, grad_down, 0, 0)
    grad_w_down = sum_dp(scatter_row(contract(grad_down, activated, 1, 1).astype(BF16)))
    grad_b_down = jnp.sum(grad_down.astype(F32), axis=1)
    grad_upward = gelu_back(grad_activated)[0].astype(BF16)
    grad_hidden = pair_sum(contract(w_up_all, grad_upward, 1, 0))
    grad_w_up = sum_dp(scatter_row(contract(hidden_mlp, grad_upward, 1, 1).astype(BF16)))
    grad_b_up = jnp.sum(grad_upward.astype(F32), axis=1)
    grad_scale_mlp = jnp.sum(grad_hidden * normed_mlp, axis=1)
    grad_shift_mlp = jnp.sum(grad_hidden, axis=1)
    grad_residual = cot + normalize_back(grad_hidden * (1.0 + scale_mlp), normed_mlp, inverse_mlp)

    grad_gate_attn = jnp.sum(grad_residual * projected, axis=1)
    grad_projected = (grad_residual * gate_attn).astype(BF16)
    grad_w_out = sum_dp(scatter_row(contract(grad_projected, attended, 1, 1).astype(BF16)))
    grad_b_out = jnp.sum(grad_projected.astype(F32), axis=1)
    grad_heads = split_heads(contract(w_out_all, grad_projected, 0, 0).astype(BF16))
    grad_probs = contract_heads(grad_heads, values, 1, 1)
    grad_values = contract_heads(grad_heads, probabilities, 2, 1)
    inner = jnp.sum(full_probs * grad_probs, axis=-1, keepdims=True)
    grad_scores = (full_probs * (grad_probs - inner)).astype(BF16)
    grad_queries = contract_heads(keys, grad_scores, 2, 2) * scale_factor
    grad_keys = contract_heads(queries, grad_scores, 2, 1) * scale_factor
    grad_joined = jnp.concatenate(
        [part.reshape(width_col, LEN).astype(BF16) for part in (grad_queries, grad_keys, grad_values)],
        axis=0,
    )
    grad_hidden = pair_sum(contract(w_joined, grad_joined, 1, 0))
    grad_w_joined = sum_dp(scatter_row(contract(hidden_attn, grad_joined, 1, 1).astype(BF16)))
    grad_b_joined = jnp.sum(grad_joined.astype(F32), axis=1)
    grad_scale_attn = jnp.sum(grad_hidden * normed_attn, axis=1)
    grad_shift_attn = jnp.sum(grad_hidden, axis=1)
    grad_x = grad_residual + normalize_back(
        grad_hidden * (1.0 + scale_attn), normed_attn, inverse_attn
    )
    grad_tokens = spread_out(grad_x.astype(BF16), row, col).astype(F32)

    own_vectors = jnp.stack(
        [
            grad_shift_attn,
            grad_scale_attn,
            grad_gate_attn,
            grad_shift_mlp,
            grad_scale_mlp,
            grad_gate_mlp,
            grad_b_down,
            grad_b_out,
        ]
    ).astype(BF16)
    pieces = [own_vectors[:, i * width_row : (i + 1) * width_row] for i in range(rows)]
    by_latent = jnp.stack([pieces[0]] + [swap_row(pieces[i], k) for i, k in enumerate(ORDER) if k])
    grad_mod = by_latent[:, :6].reshape(rows, -1)
    grad_silu = contract(grad_mod, mod_flat, 1, 0)
    grad_silu = grad_silu[0:1] + sum(
        swap_row(grad_silu[i : i + 1], k) for i, k in enumerate(ORDER) if k
    )
    grad_condition = jax.vjp(jax.nn.silu, condition_float)[1](grad_silu)[0]
    message = jnp.concatenate([by_latent.reshape(rows, -1), cond_rows], axis=1)
    everyone = lax.all_gather(message, "dp", axis=0, tiled=True)
    all_mod = everyone[:, : 6 * width_row]
    all_cond = everyone[:, 8 * width_row :]
    grad_w_mod = contract(all_mod, all_cond, 0, 0).reshape(w_mod.shape)
    sums = jnp.sum(everyone[:, : 8 * width_row].astype(F32), axis=0)
    grad_b_mod = sums[: 6 * width_row].reshape(b_mod.shape)
    grad_b_down = sums[6 * width_row : 7 * width_row]
    grad_b_out = sums[7 * width_row :]
    bias_sums = lax.psum(
        jnp.concatenate([grad_b_up, grad_b_joined[:width_col], grad_b_joined[2 * width_col :]]),
        ("dp", "row"),
    )
    hidden_width = grad_b_up.shape[0]
    return (
        output,
        grad_tokens,
        grad_condition,
        grad_w_mod,
        grad_b_mod,
        grad_w_joined[:, :width_col],
        grad_w_joined[:, width_col : 2 * width_col],
        grad_w_joined[:, 2 * width_col :],
        bias_sums[hidden_width : hidden_width + width_col],
        bias_sums[hidden_width + width_col :],
        grad_w_out,
        grad_b_out,
        grad_w_up,
        bias_sums[:hidden_width],
        grad_w_down,
        grad_b_down,
    )


def solution(mesh):
    placed = (
        P("row", ("dp", "col")),
        P(("dp", "row"), "col"),
        P(None, "row", "col"),
        P(None, "row"),
        P("row", "col"),
        P("row", "col"),
        P("row", "col"),
        P("col"),
        P("col"),
        P("row", "col"),
        P("row"),
        P("row", "col"),
        P("col"),
        P("row", "col"),
        P("row"),
        P("row", ("dp", "col")),
    )
    return jax.shard_map(
        body,
        mesh=mesh,
        in_specs=placed,
        out_specs=(
            P("row", ("dp", "col")),
            P("row", ("dp", "col")),
            P(("dp", "row"), "col"),
            P(None, "row", "col"),
            P(None, "row"),
            P("row", "col"),
            P("row", "col"),
            P("row", "col"),
            P("col"),
            P("col"),
            P("row", "col"),
            P("row"),
            P("row", "col"),
            P("col"),
            P("row", "col"),
            P("row"),
        ),
        check_vma=False,
    )
```

time: 554 us -> 350 us (0.63)
  waiting for transfers between devices: 313 us -> 117 us
  starting transfers between devices: 0.5 us -> 69.2 us
  blocking collectives: 110 us -> 73.3 us
  matrix products: 39.3 us -> 21 us
  other arithmetic: 42.6 us -> 28.5 us
  between operations: 15.5 us -> 2.23 us
  local copies, waits for them, and re-layouts: 31 us -> 36.6 us
    reduce_scatter x8 -> x0, waiting for transfers between devices: 182 us -> none  [the longest x2 109 us: forward_rows(): lax.psum_scatter(row_term(jnp.int32(0), share_rows * lax.axis_size('row')...]
    ppermute x0 -> x63, waiting for transfers between devices: none -> 117 us  [the longest x38 44.4 us: swap_row(): return lax.ppermute(value, 'row', [(i, i ^ offset) for i in range(size)])]
    ppermute x0 -> x63, starting transfers between devices: none -> 69.2 us  [the longest x38 24.5 us: swap_row(): return lax.ppermute(value, 'row', [(i, i ^ offset) for i in range(size)])]
    all_gather x3 -> x0, waiting for transfers between devices: 67.7 us -> none  [the longest x2 41.2 us: backward_rows(): gathered = lax.all_gather(grad_part, 'row', axis=0, tiled=True)]
    psum x1 -> x0, waiting for transfers between devices: 62.7 us -> none  [body(): lax.psum(grad_w_mod.astype(jnp.bfloat16), 'dp').astype(jnp.float32)]
    all_gather x7 -> x1, blocking collectives: 50.4 us -> 13.9 us  [body(): everyone = lax.all_gather(message, 'dp', axis=0, tiled=True)]
    dot_general x21 -> x20, matrix products: 39.3 us -> 18.7 us  [the longest x15 15.7 us: contract(): lax.dot_general(left, right, (((left_dim,), (right_dim,)), ((), ())), pre...]
    unnamed x2 -> x0, blocking collectives: 15.6 us -> none
  transfers between devices with their start and end apart: 12 -> 63, of which waited for: 11 -> 22; matrix products, arithmetic and copies ran while one was open for 10% -> 23% of each run, Pallas kernels for 0% -> 0%
where the time goes in v1:
time: 350 us; the launch traced here: 348 us
  waiting for transfers between devices  117 us (33%)
  blocking collectives  73.3 us (21%)
  starting transfers between devices  69.2 us (20%)
  local copies, waits for them, and re-layouts  36.6 us (10%)
  other arithmetic  28.5 us (8%)
  matrix products  21 us (6%)
    psum x1, blocking collectives, body(): lax.psum(jnp.concatenate([grad_b_up, grad_b_joined[:width_col], grad_b_jo...  59.4 us
    ppermute x38, waiting for transfers between devices, swap_row(): return lax.ppermute(value, 'row', [(i, i ^ offset) for i in range(size)])  44.4 us
    ppermute x4, waiting for transfers between devices, sum_dp(): back = lax.ppermute(total, 'dp', outward)  31.8 us
    ppermute x38, starting transfers between devices, swap_row(): return lax.ppermute(value, 'row', [(i, i ^ offset) for i in range(size)])  24.5 us
    ppermute x7, waiting for transfers between devices, swap_col(): return lax.ppermute(value, 'col', [(0, 1), (1, 0)])  20.6 us
    ppermute x4, waiting for transfers between devices, sum_dp(): lax.ppermute(value, 'dp', inward).astype(F32)  18 us
    dot_general x15, matrix products, contract(): lax.dot_general(left, right, (((left_dim,), (right_dim,)), ((), ())), pre...  15.7 us
    unnamed x178, local copies, waits for them, and re-layouts  15.5 us
  transfers between devices with their start and end apart: 63, of which 22 were waited for; matrix products, arithmetic and copies ran while one was open for 23% of the time, Pallas kernels for 0%

profile of v1, /device:TPU:0, one launch (start us, length us, event | category | flops | bytes accessed | tf_op | source)
XLA Modules:
  0.0 347.7 jit_solution(9308859822196866191)
XLA Ops:
  1.5 2.5 collective-permute-start.6
  6.6 2.0 constant_dynamic-update-slice_fusion.12
  13.2 3.4 collective-permute-done.7
  24.1 3.2 collective-permute-done.28
  29.6 5.7 %collective-permute-done.3 = bf16[192,256]{1,0:T(8,128)(2,1)S(1)} collective-permute-done((bf16[192,256]{1,0:T(8,128)(2,1)S(1)}, bf16[192,256]{1,0:T(8,128)(2,1)S(1)}, u32[]{:S(2)}, u32[]{:S(2)}) %collective-permute-start.3) | collective-permute-done | bytes 98336 | tf_op jit(solution)/shard_map/ppermute | solution.py:30
  39.2 3.6 %collective-permute-done.12 = bf16[192,384]{1,0:T(8,128)(2,1)S(1)} collective-permute-done((bf16[192,384]{1,0:T(8,128)(2,1)S(1)}, bf16[192,384]{1,0:T(8,128)(2,1)S(1)}, u32[]{:S(2)}, u32[]{:S(2)}) %collective-permute-start.12) | collective-permute-done | bytes 147488 | tf_op jit(solution)/shard_map/ppermute | solution.py:30
  49.0 2.3 fusion.93
  53.3 8.8 %collective-permute-done.18 = bf16[192,1536]{1,0:T(8,128)(2,1)} collective-permute-done((bf16[192,1536]{1,0:T(8,128)(2,1)}, bf16[192,1536]{1,0:T(8,128)(2,1)}, u32[]{:S(2)}, u32[]{:S(2)}) %collective-permute-start.18) | collective-permute-done | bytes 589856 | tf_op jit(solution)/shard_map/ppermute | solution.py:30
  67.5 5.4 %collective-permute-done.17 = bf16[768,256]{1,0:T(8,128)(2,1)S(1)} collective-permute-done((bf16[768,256]{1,0:T(8,128)(2,1)S(1)}, bf16[768,256]{1,0:T(8,128)(2,1)S(1)}, u32[]{:S(2)}, u32[]{:S(2)}) %collective-permute-start.17) | collective-permute-done | bytes 393248 | tf_op jit(solution)/shard_map/ppermute | solution.py:34
  73.5 6.2 %collective-permute-done.19 = bf16[192,1536]{1,0:T(8,128)(2,1)S(1)} collective-permute-done((bf16[192,1536]{1,0:T(8,128)(2,1)S(1)}, bf16[192,1536]{1,0:T(8,128)(2,1)S(1)}, u32[]{:S(2)}, u32[]{:S(2)}) %collective-permute-start.19) | collective-permute-done | bytes 589856 | tf_op jit(solution)/shard_map/ppermute | solution.py:30
  85.1 2.7 convert_reduce_fusion
  96.4 8.0 %collective-permute-done.32 = bf16[768,256]{1,0:T(8,128)(2,1)S(1)} collective-permute-done((bf16[768,256]{1,0:T(8,128)(2,1)S(1)}, bf16[768,256]{1,0:T(8,128)(2,1)S(1)}, u32[]{:S(2)}, u32[]{:S(2)}) %collective-permute-start.32) | collective-permute-done | bytes 393248 | tf_op jit(solution)/shard_map/ppermute | solution.py:34
  106.4 2.6 fusion.83
  115.8 3.0 collective-permute-start.25
  126.5 59.4 %psum.7 = f32[2304]{0:T(1024)S(1)} all-reduce(f32[2304]{0:T(1024)} %pad_maximum_fusion.7), channel_id=1, replica_groups=mesh['dp'=4,'row'=4,'col'=2] {'dp','row'}, use_global_device_ids=true, to_apply=%region_22.23 | all-reduce | flops 2304 | bytes 18432 | tf_op jit(solution)/shard_map/psum | solution.py:278
  187.1 2.0 add_convert_fusion
  195.6 2.4 multiply_reduce_fusion.2
  199.0 2.0 collective-permute-start.37
  206.3 13.9 %all-gather = bf16[4,4,1920]{2,1,0:T(4,128)(2,1)} all-gather(bf16[1,4,1920]{2,1,0:T(4,128)(2,1)S(1)} %maximum_bitcast_fusion.1), channel_id=1, replica_groups=mesh['dp'=4,'row'=4,'col'=2] {'dp'}, dimensions={0}, use_global_device_ids=true | all-gather | bytes 76800 | tf_op jit(solution)/shard_map/all_gather | solution.py:270
  221.7 2.5 fusion.40
  233.6 2.4 collective-permute-start.35
  236.0 2.0 collective-permute-start.36
  238.7 4.2 %collective-permute-start.34 = (bf16[192,256]{1,0:T(8,128)(2,1)}, bf16[192,256]{1,0:T(8,128)(2,1)S(1)}, u32[]{:S(2)}, u32[]{:S(2)}) collective-permute-start(bf16[192,256]{1,0:T(8,128)(2,1)} %get-tuple-element.61), channel_id=1, source_target_pairs={{0,4},{2,6},{5,1},{7,3},{8,12},{10,14},{13,9},{15,11},{16,20},{18,... | collective-permute-start | bytes 294920 | tf_op jit(solution)/shard_map/ppermute | solution.py:101
  256.1 3.3 collective-permute-done.59
  259.6 6.6 %collective-permute-start.60 = (bf16[192,1536]{1,0:T(8,128)(2,1)S(1)}, bf16[192,1536]{1,0:T(8,128)(2,1)S(1)}, u32[]{:S(2)}, u32[]{:S(2)}) collective-permute-start(bf16[192,1536]{1,0:T(8,128)(2,1)S(1)} %add_convert_fusion.5), channel_id=1, source_target_pairs={{0,8},{24,16},{1,9},{25,17},{2,10},{26,18},{3,11},{27,19},{4,12},{... | collective-permute-start | bytes 1769480 | tf_op jit(solution)/shard_map/ppermute | solution.py:68
  267.0 14.1 %collective-permute-done.44 = bf16[192,1152]{1,0:T(8,128)(2,1)S(1)} collective-permute-done((bf16[192,1152]{1,0:T(8,128)(2,1)S(1)}, bf16[192,1152]{1,0:T(8,128)(2,1)S(1)}, u32[]{:S(2)}, u32[]{:S(2)}) %collective-permute-start.44) | collective-permute-done | bytes 442400 | tf_op jit(solution)/shard_map/ppermute | solution.py:30
  281.3 6.0 %collective-permute-start.45 = (bf16[192,1152]{1,0:T(8,128)(2,1)S(1)}, bf16[192,1152]{1,0:T(8,128)(2,1)S(1)}, u32[]{:S(2)}, u32[]{:S(2)}) collective-permute-start(bf16[192,1152]{1,0:T(8,128)(2,1)S(1)} %add_convert_fusion.11), channel_id=1, source_target_pairs={{0,8},{24,16},{1,9},{25,17},{2,10},{26,18},{3,11},{27,19},{4,12},{... | collective-permute-start | bytes 1327112 | tf_op jit(solution)/shard_map/ppermute | solution.py:68
  289.7 8.2 %collective-permute-done.45 = bf16[192,1152]{1,0:T(8,128)(2,1)S(1)} collective-permute-done((bf16[192,1152]{1,0:T(8,128)(2,1)S(1)}, bf16[192,1152]{1,0:T(8,128)(2,1)S(1)}, u32[]{:S(2)}, u32[]{:S(2)}) %collective-permute-start.45) | collective-permute-done | bytes 442400 | tf_op jit(solution)/shard_map/ppermute | solution.py:68
  298.7 8.8 %collective-permute-done.55 = bf16[192,1536]{1,0:T(8,128)(2,1)S(1)} collective-permute-done((bf16[192,1536]{1,0:T(8,128)(2,1)S(1)}, bf16[192,1536]{1,0:T(8,128)(2,1)S(1)}, u32[]{:S(2)}, u32[]{:S(2)}) %collective-permute-start.55) | collective-permute-done | bytes 589856 | tf_op jit(solution)/shard_map/ppermute | solution.py:68
  312.7 15.9 %collective-permute-done.62 = bf16[192,1536]{1,0:T(8,128)(2,1)S(1)} collective-permute-done((bf16[192,1536]{1,0:T(8,128)(2,1)S(1)}, bf16[192,1536]{1,0:T(8,128)(2,1)S(1)}, u32[]{:S(2)}, u32[]{:S(2)}) %collective-permute-start.62) | collective-permute-done | bytes 589856 | tf_op jit(solution)/shard_map/ppermute | solution.py:76
  329.7 8.4 %collective-permute-done.47 = bf16[192,1152]{1,0:T(8,128)(2,1)S(1)} collective-permute-done((bf16[192,1152]{1,0:T(8,128)(2,1)S(1)}, bf16[192,1152]{1,0:T(8,128)(2,1)S(1)}, u32[]{:S(2)}, u32[]{:S(2)}) %collective-permute-start.47) | collective-permute-done | bytes 442400 | tf_op jit(solution)/shard_map/ppermute | solution.py:76
  339.1 7.5 %collective-permute-done.57 = bf16[192,1536]{1,0:T(8,128)(2,1)S(1)} collective-permute-done((bf16[192,1536]{1,0:T(8,128)(2,1)S(1)}, bf16[192,1536]{1,0:T(8,128)(2,1)S(1)}, u32[]{:S(2)}, u32[]{:S(2)}) %collective-permute-start.57) | collective-permute-done | bytes 589856 | tf_op jit(solution)/shard_map/ppermute | solution.py:76
  (400 shorter events, 116.4 us)
Async XLA Ops:
  4.7 76.5 %collective-permute-start.20 = (bf16[192,1536]{1,0:T(8,128)(2,1)}, bf16[192,1536]{1,0:T(8,128)(2,1)}, u32[]{:S(2)}, u32[]{:S(2)}) collective-permute-start(bf16[192,1536]{1,0:T(8,128)(2,1)} %param.29), channel_id=1, source_target_pairs={{0,2},{2,0},{4,6},{6,4},{1,3},{3,1},{5,7},{7,5},{8,10},{10,8},{12,... | collective-permute-start | bytes 1769480 | tf_op jit(solution)/shard_map/ppermute | solution.py:30
  4.8 18.7 %collective-permute-start = (bf16[192,512]{1,0:T(8,128)(2,1)}, bf16[192,512]{1,0:T(8,128)(2,1)S(1)}, u32[]{:S(2)}, u32[]{:S(2)}) collective-permute-start(bf16[192,512]{1,0:T(8,128)(2,1)} %param.16), channel_id=1, source_target_pairs={{0,1},{1,0},{2,3},{3,2},{4,5},{5,4},{6,7},{7,6},{8,9},{9,8},{10,11... | collective-permute-start | bytes 589832 | tf_op jit(solution)/shard_map/ppermute | solution.py:34
  21.0 16.5 %collective-permute-start.11 = (bf16[192,1152]{1,0:T(8,128)(2,1)}, bf16[192,1152]{1,0:T(8,128)(2,1)S(1)}, u32[]{:S(2)}, u32[]{:S(2)}) collective-permute-start(bf16[192,1152]{1,0:T(8,128)(2,1)} %copy-done.38), channel_id=1, source_target_pairs={{0,4},{2,6},{4,0},{6,2},{1,5},{3,7},{5,1},{7,3},{8,12},{10,14},{12... | collective-permute-start | bytes 1327112 | tf_op jit(solution)/shard_map/ppermute | solution.py:30
  23.7 11.6 %collective-permute-start.3 = (bf16[192,256]{1,0:T(8,128)(2,1)S(1)}, bf16[192,256]{1,0:T(8,128)(2,1)S(1)}, u32[]{:S(2)}, u32[]{:S(2)}) collective-permute-start(bf16[192,256]{1,0:T(8,128)(2,1)S(1)} %get-tuple-element.72), channel_id=1, source_target_pairs={{0,6},{2,4},{4,2},{6,0},{1,7},{3,5},{5,3},{7,1},{8,14},{10,12},{12... | collective-permute-start | bytes 294920 | tf_op jit(solution)/shard_map/ppermute | solution.py:30
  23.7 12.2 %collective-permute-start.2 = (bf16[192,256]{1,0:T(8,128)(2,1)S(1)}, bf16[192,256]{1,0:T(8,128)(2,1)S(1)}, u32[]{:S(2)}, u32[]{:S(2)}) collective-permute-start(bf16[192,256]{1,0:T(8,128)(2,1)S(1)} %get-tuple-element.73), channel_id=1, source_target_pairs={{0,2},{2,0},{4,6},{6,4},{1,3},{3,1},{5,7},{7,5},{8,10},{10,8},{12,... | collective-permute-start | bytes 294920 | tf_op jit(solution)/shard_map/ppermute | solution.py:30
  42.8 22.0 %collective-permute-start.22 = (bf16[192,1536]{1,0:T(8,128)(2,1)}, bf16[192,1536]{1,0:T(8,128)(2,1)}, u32[]{:S(2)}, u32[]{:S(2)}) collective-permute-start(bf16[192,1536]{1,0:T(8,128)(2,1)} %param.27), channel_id=1, source_target_pairs={{0,2},{2,0},{4,6},{6,4},{1,3},{3,1},{5,7},{7,5},{8,10},{10,8},{12,... | collective-permute-start | bytes 1769480 | tf_op jit(solution)/shard_map/ppermute | solution.py:30
  44.1 40.9 %collective-permute-start.31 = (bf16[192,256]{1,0:T(8,128)(2,1)}, bf16[192,256]{1,0:T(8,128)(2,1)}, u32[]{:S(2)}, u32[]{:S(2)}) collective-permute-start(bf16[192,256]{1,0:T(8,128)(2,1)} %get-tuple-element.65), channel_id=1, source_target_pairs={{0,6},{2,4},{4,2},{6,0},{1,7},{3,5},{5,3},{7,1},{8,14},{10,12},{12... | collective-permute-start | bytes 294920 | tf_op jit(solution)/shard_map/ppermute | solution.py:30
  45.5 39.6 %collective-permute-start.30 = (bf16[192,256]{1,0:T(8,128)(2,1)}, bf16[192,256]{1,0:T(8,128)(2,1)}, u32[]{:S(2)}, u32[]{:S(2)}) collective-permute-start(bf16[192,256]{1,0:T(8,128)(2,1)} %get-tuple-element.66), channel_id=1, source_target_pairs={{0,2},{2,0},{4,6},{6,4},{1,3},{3,1},{5,7},{7,5},{8,10},{10,8},{12,... | collective-permute-start | bytes 294920 | tf_op jit(solution)/shard_map/ppermute | solution.py:30
  45.9 16.3 %collective-permute-start.18 = (bf16[192,1536]{1,0:T(8,128)(2,1)}, bf16[192,1536]{1,0:T(8,128)(2,1)}, u32[]{:S(2)}, u32[]{:S(2)}) collective-permute-start(bf16[192,1536]{1,0:T(8,128)(2,1)} %param.27), channel_id=1, source_target_pairs={{0,4},{2,6},{4,0},{6,2},{1,5},{3,7},{5,1},{7,3},{8,12},{10,14},{12... | collective-permute-start | bytes 1769480 | tf_op jit(solution)/shard_map/ppermute | solution.py:30
  62.2 10.8 %collective-permute-start.17 = (bf16[768,256]{1,0:T(8,128)(2,1)S(1)}, bf16[768,256]{1,0:T(8,128)(2,1)S(1)}, u32[]{:S(2)}, u32[]{:S(2)}) collective-permute-start(bf16[768,256]{1,0:T(8,128)(2,1)S(1)} %convolution_convert_fusion.7), channel_id=1, source_target_pairs={{0,1},{1,0},{2,3},{3,2},{4,5},{5,4},{6,7},{7,6},{8,9},{9,8},{10,11... | collective-permute-start | bytes 1179656 | tf_op jit(solution)/shard_map/ppermute | solution.py:34
  64.8 14.8 %collective-permute-start.19 = (bf16[192,1536]{1,0:T(8,128)(2,1)S(1)}, bf16[192,1536]{1,0:T(8,128)(2,1)S(1)}, u32[]{:S(2)}, u32[]{:S(2)}) collective-permute-start(bf16[192,1536]{1,0:T(8,128)(2,1)S(1)} %copy-done.27), channel_id=1, source_target_pairs={{0,4},{2,6},{4,0},{6,2},{1,5},{3,7},{5,1},{7,3},{8,12},{10,14},{12... | collective-permute-start | bytes 1769480 | tf_op jit(solution)/shard_map/ppermute | solution.py:30
  84.4 12.0 %collective-permute-start.24 = (bf16[768,256]{1,0:T(8,128)(2,1)S(1)}, bf16[768,256]{1,0:T(8,128)(2,1)S(1)}, u32[]{:S(2)}, u32[]{:S(2)}) collective-permute-start(bf16[768,256]{1,0:T(8,128)(2,1)S(1)} %convolution_convert_fusion.6), channel_id=1, source_target_pairs={{0,1},{1,0},{2,3},{3,2},{4,5},{5,4},{6,7},{7,6},{8,9},{9,8},{10,11... | collective-permute-start | bytes 1179656 | tf_op jit(solution)/shard_map/ppermute | solution.py:34
  88.6 15.9 %collective-permute-start.32 = (bf16[768,256]{1,0:T(8,128)(2,1)S(1)}, bf16[768,256]{1,0:T(8,128)(2,1)S(1)}, u32[]{:S(2)}, u32[]{:S(2)}) collective-permute-start(bf16[768,256]{1,0:T(8,128)(2,1)S(1)} %convolution_convert_fusion.5), channel_id=1, source_target_pairs={{0,1},{1,0},{2,3},{3,2},{4,5},{5,4},{6,7},{7,6},{8,9},{9,8},{10,11... | collective-permute-start | bytes 1179656 | tf_op jit(solution)/shard_map/ppermute | solution.py:34
  93.3 93.8 %collective-permute-start.58 = (bf16[384,1536]{1,0:T(8,128)(2,1)}, bf16[384,1536]{1,0:T(8,128)(2,1)}, u32[]{:S(2)}, u32[]{:S(2)}) collective-permute-start(bf16[384,1536]{1,0:T(8,128)(2,1)} %slice.316), channel_id=1, source_target_pairs={{0,2},{2,0},{4,6},{6,4},{1,3},{3,1},{5,7},{7,5},{8,10},{10,8},{12,... | collective-permute-start | bytes 3538952 | tf_op jit(solution)/shard_map/ppermute | solution.py:30
  95.5 156.7 %collective-permute-start.53 = (bf16[384,1536]{1,0:T(8,128)(2,1)}, bf16[384,1536]{1,0:T(8,128)(2,1)}, u32[]{:S(2)}, u32[]{:S(2)}) collective-permute-start(bf16[384,1536]{1,0:T(8,128)(2,1)} %slice.311), channel_id=1, source_target_pairs={{0,2},{2,0},{4,6},{6,4},{1,3},{3,1},{5,7},{7,5},{8,10},{10,8},{12,... | collective-permute-start | bytes 3538952 | tf_op jit(solution)/shard_map/ppermute | solution.py:30
  114.5 78.2 %collective-permute-start.33 = (bf16[768,256]{1,0:T(8,128)(2,1)}, bf16[768,256]{1,0:T(8,128)(2,1)}, u32[]{:S(2)}, u32[]{:S(2)}) collective-permute-start(bf16[768,256]{1,0:T(8,128)(2,1)} %convolution_convert_fusion.4), channel_id=1, source_target_pairs={{0,1},{1,0},{2,3},{3,2},{4,5},{5,4},{6,7},{7,6},{8,9},{9,8},{10,11... | collective-permute-start | bytes 1179656 | tf_op jit(solution)/shard_map/ppermute | solution.py:34
  115.8 117.8 %collective-permute-start.25 = (bf16[192,256]{1,0:T(8,128)(2,1)}, bf16[192,256]{1,0:T(8,128)(2,1)}, u32[]{:S(2)}, u32[]{:S(2)}) collective-permute-start(bf16[192,256]{1,0:T(8,128)(2,1)} %get-tuple-element.68), channel_id=1, source_target_pairs={{0,4},{2,6},{5,1},{7,3},{8,12},{10,14},{13,9},{15,11},{16,20},{18,... | collective-permute-start | bytes 294920 | tf_op jit(solution)/shard_map/ppermute | solution.py:101
  125.6 64.4 %collective-permute-start.48 = (bf16[384,384]{1,0:T(8,128)(2,1)}, bf16[384,384]{1,0:T(8,128)(2,1)}, u32[]{:S(2)}, u32[]{:S(2)}) collective-permute-start(bf16[384,384]{1,0:T(8,128)(2,1)} %slice.306), channel_id=1, source_target_pairs={{0,2},{2,0},{4,6},{6,4},{1,3},{3,1},{5,7},{7,5},{8,10},{10,8},{12,... | collective-permute-start | bytes 884744 | tf_op jit(solution)/shard_map/ppermute | solution.py:30
  230.9 12.1 %collective-permute-start.27 = (bf16[192,256]{1,0:T(8,128)(2,1)}, bf16[192,256]{1,0:T(8,128)(2,1)S(1)}, u32[]{:S(2)}, u32[]{:S(2)}) collective-permute-start(bf16[192,256]{1,0:T(8,128)(2,1)} %get-tuple-element.69), channel_id=1, source_target_pairs={{0,6},{2,4},{5,3},{7,1},{8,14},{10,12},{13,11},{15,9},{16,22},{18,... | collective-permute-start | bytes 294920 | tf_op jit(solution)/shard_map/ppermute | solution.py:101
  243.0 12.5 %collective-permute-start.43 = (bf16[384,1152]{1,0:T(8,128)(2,1)}, bf16[384,1152]{1,0:T(8,128)(2,1)S(1)}, u32[]{:S(2)}, u32[]{:S(2)}) collective-permute-start(bf16[384,1152]{1,0:T(8,128)(2,1)} %slice.295), channel_id=1, source_target_pairs={{0,2},{2,0},{4,6},{6,4},{1,3},{3,1},{5,7},{7,5},{8,10},{10,8},{12,... | collective-permute-start | bytes 2654216 | tf_op jit(solution)/shard_map/ppermute | solution.py:30
  243.1 16.4 %collective-permute-start.59 = (bf16[192,1536]{1,0:T(8,128)(2,1)}, bf16[192,1536]{1,0:T(8,128)(2,1)S(1)}, u32[]{:S(2)}, u32[]{:S(2)}) collective-permute-start(bf16[192,1536]{1,0:T(8,128)(2,1)} %slice.318), channel_id=1, source_target_pairs={{0,4},{2,6},{4,0},{6,2},{1,5},{3,7},{5,1},{7,3},{8,12},{10,14},{12... | collective-permute-start | bytes 1769480 | tf_op jit(solution)/shard_map/ppermute | solution.py:30
  250.7 15.6 %collective-permute-start.52 = (bf16[192,384]{1,0:T(8,128)(2,1)S(1)}, bf16[192,384]{1,0:T(8,128)(2,1)S(1)}, u32[]{:S(2)}, u32[]{:S(2)}) collective-permute-start(bf16[192,384]{1,0:T(8,128)(2,1)S(1)} %add_convert_fusion.15), channel_id=1, source_target_pairs={{8,0},{16,24},{9,1},{17,25},{10,2},{18,26},{11,3},{19,27},{12,4},{... | collective-permute-start | bytes 442376 | tf_op jit(solution)/shard_map/ppermute | solution.py:76
  253.7 33.6 %collective-permute-start.54 = (bf16[192,1536]{1,0:T(8,128)(2,1)S(1)}, bf16[192,1536]{1,0:T(8,128)(2,1)S(1)}, u32[]{:S(2)}, u32[]{:S(2)}) collective-permute-start(bf16[192,1536]{1,0:T(8,128)(2,1)S(1)} %slice.313), channel_id=1, source_target_pairs={{0,4},{2,6},{4,0},{6,2},{1,5},{3,7},{5,1},{7,3},{8,12},{10,14},{12... | collective-permute-start | bytes 1769480 | tf_op jit(solution)/shard_map/ppermute | solution.py:30
  255.8 25.4 %collective-permute-start.44 = (bf16[192,1152]{1,0:T(8,128)(2,1)S(1)}, bf16[192,1152]{1,0:T(8,128)(2,1)S(1)}, u32[]{:S(2)}, u32[]{:S(2)}) collective-permute-start(bf16[192,1152]{1,0:T(8,128)(2,1)S(1)} %slice.297), channel_id=1, source_target_pairs={{0,4},{2,6},{4,0},{6,2},{1,5},{3,7},{5,1},{7,3},{8,12},{10,14},{12... | collective-permute-start | bytes 1327112 | tf_op jit(solution)/shard_map/ppermute | solution.py:30
  259.6 29.2 %collective-permute-start.60 = (bf16[192,1536]{1,0:T(8,128)(2,1)S(1)}, bf16[192,1536]{1,0:T(8,128)(2,1)S(1)}, u32[]{:S(2)}, u32[]{:S(2)}) collective-permute-start(bf16[192,1536]{1,0:T(8,128)(2,1)S(1)} %add_convert_fusion.5), channel_id=1, source_target_pairs={{0,8},{24,16},{1,9},{25,17},{2,10},{26,18},{3,11},{27,19},{4,12},{... | collective-permute-start | bytes 1769480 | tf_op jit(solution)/shard_map/ppermute | solution.py:68
  281.3 16.6 %collective-permute-start.45 = (bf16[192,1152]{1,0:T(8,128)(2,1)S(1)}, bf16[192,1152]{1,0:T(8,128)(2,1)S(1)}, u32[]{:S(2)}, u32[]{:S(2)}) collective-permute-start(bf16[192,1152]{1,0:T(8,128)(2,1)S(1)} %add_convert_fusion.11), channel_id=1, source_target_pairs={{0,8},{24,16},{1,9},{25,17},{2,10},{26,18},{3,11},{27,19},{4,12},{... | collective-permute-start | bytes 1327112 | tf_op jit(solution)/shard_map/ppermute | solution.py:68
  287.5 20.0 %collective-permute-start.55 = (bf16[192,1536]{1,0:T(8,128)(2,1)S(1)}, bf16[192,1536]{1,0:T(8,128)(2,1)S(1)}, u32[]{:S(2)}, u32[]{:S(2)}) collective-permute-start(bf16[192,1536]{1,0:T(8,128)(2,1)S(1)} %add_convert_fusion.8), channel_id=1, source_target_pairs={{0,8},{24,16},{1,9},{25,17},{2,10},{26,18},{3,11},{27,19},{4,12},{... | collective-permute-start | bytes 1769480 | tf_op jit(solution)/shard_map/ppermute | solution.py:68
  289.0 19.4 %collective-permute-start.61 = (bf16[192,1536]{1,0:T(8,128)(2,1)S(1)}, bf16[192,1536]{1,0:T(8,128)(2,1)S(1)}, u32[]{:S(2)}, u32[]{:S(2)}) collective-permute-start(bf16[192,1536]{1,0:T(8,128)(2,1)S(1)} %add_convert_fusion.4), channel_id=1, source_target_pairs={{8,16},{16,8},{9,17},{17,9},{10,18},{18,10},{11,19},{19,11},{12,20... | collective-permute-start | bytes 1769480 | tf_op jit(solution)/shard_map/ppermute | solution.py:69
  298.0 11.8 %collective-permute-start.46 = (bf16[192,1152]{1,0:T(8,128)(2,1)S(1)}, bf16[192,1152]{1,0:T(8,128)(2,1)S(1)}, u32[]{:S(2)}, u32[]{:S(2)}) collective-permute-start(bf16[192,1152]{1,0:T(8,128)(2,1)S(1)} %add_convert_fusion.10), channel_id=1, source_target_pairs={{8,16},{16,8},{9,17},{17,9},{10,18},{18,10},{11,19},{19,11},{12,20... | collective-permute-start | bytes 1327112 | tf_op jit(solution)/shard_map/ppermute | solution.py:69
  308.5 20.1 %collective-permute-start.62 = (bf16[192,1536]{1,0:T(8,128)(2,1)S(1)}, bf16[192,1536]{1,0:T(8,128)(2,1)S(1)}, u32[]{:S(2)}, u32[]{:S(2)}) collective-permute-start(bf16[192,1536]{1,0:T(8,128)(2,1)S(1)} %add_convert_fusion.3), channel_id=1, source_target_pairs={{8,0},{16,24},{9,1},{17,25},{10,2},{18,26},{11,3},{19,27},{12,4},{... | collective-permute-start | bytes 1769480 | tf_op jit(solution)/shard_map/ppermute | solution.py:76
  310.0 28.1 %collective-permute-start.47 = (bf16[192,1152]{1,0:T(8,128)(2,1)S(1)}, bf16[192,1152]{1,0:T(8,128)(2,1)S(1)}, u32[]{:S(2)}, u32[]{:S(2)}) collective-permute-start(bf16[192,1152]{1,0:T(8,128)(2,1)S(1)} %add_convert_fusion.9), channel_id=1, source_target_pairs={{8,0},{16,24},{9,1},{17,25},{10,2},{18,26},{11,3},{19,27},{12,4},{... | collective-permute-start | bytes 1327112 | tf_op jit(solution)/shard_map/ppermute | solution.py:76
  311.4 35.2 %collective-permute-start.57 = (bf16[192,1536]{1,0:T(8,128)(2,1)S(1)}, bf16[192,1536]{1,0:T(8,128)(2,1)S(1)}, u32[]{:S(2)}, u32[]{:S(2)}) collective-permute-start(bf16[192,1536]{1,0:T(8,128)(2,1)S(1)} %add_convert_fusion.6), channel_id=1, source_target_pairs={{8,0},{16,24},{9,1},{17,25},{10,2},{18,26},{11,3},{19,27},{12,4},{... | collective-permute-start | bytes 1769480 | tf_op jit(solution)/shard_map/ppermute | solution.py:76
  (113 other events, 852.6 us)

commit v2 on v1

--- a/solution.py
+++ b/solution.py
@@ -49,32 +49,66 @@
     return mine.astype(F32) + swap_col(mine).astype(F32)
 
 
-def scatter_row(full):
-    half = full.shape[0] // 2
+def near_sum(left, right):
+    half = left.shape[0] // 2
     quarter = half // 2
-    near = full[:half].astype(F32) + swap_row(full[half:], 1).astype(F32)
-    near = near.astype(BF16)
-    own = near[:quarter].astype(F32) + swap_row(near[quarter:], 2).astype(F32)
-    return own.astype(BF16)
-
-
-def sum_dp(value):
+    other = swap_row(contract(left[half:], right, 1, 1).astype(BF16), 1)
+    own = contract(left[:quarter], right, 1, 1) + other[:quarter].astype(F32)
+    far = contract(left[quarter:half], right, 1, 1) + other[quarter:].astype(F32)
+    return own, far.astype(BF16)
+
+
+def far_sum(near):
+    return (near[0] + swap_row(near[1], 2).astype(F32)).astype(BF16)
+
+
+def dp_pairs():
     size = lax.axis_size("dp")
-    place = lax.axis_index("dp") % 4
-    inner = jnp.logical_or(place == 1, place == 2)
     inward = [(i, i + 1) if i % 4 == 0 else (i, i - 1) for i in range(size) if i % 4 in (0, 3)]
     middle = [(i, i ^ 3) for i in range(size) if i % 4 in (1, 2)]
-    outward = [(b, a) for a, b in inward]
-    first = (value.astype(F32) + lax.ppermute(value, "dp", inward).astype(F32)).astype(BF16)
-    total = first.astype(F32) + lax.ppermute(first, "dp", middle).astype(F32)
+    return inward, middle, [(b, a) for a, b in inward]
+
+
+def dp_first(value):
+    return (value.astype(F32) + lax.ppermute(value, "dp", dp_pairs()[0]).astype(F32)).astype(BF16)
+
+
+def dp_second(first):
+    size = lax.axis_size("dp")
+    total = first.astype(F32) + lax.ppermute(first, "dp", dp_pairs()[1]).astype(F32)
     total = total.astype(BF16)
     step = 4
     while step < size:
         other = lax.ppermute(total, "dp", [(i, i ^ step) for i in range(size)])
         total = (total.astype(F32) + other.astype(F32)).astype(BF16)
         step *= 2
-    back = lax.ppermute(total, "dp", outward)
+    return total
+
+
+def dp_third(total):
+    place = lax.axis_index("dp") % 4
+    inner = jnp.logical_or(place == 1, place == 2)
+    back = lax.ppermute(total, "dp", dp_pairs()[2])
     return jnp.where(inner, total, back).astype(F32)
+
+
+def gather_dp(value):
+    size = lax.axis_size("dp")
+    place = lax.axis_index("dp")
+    step = 1
+    while step < size:
+        other = lax.ppermute(value, "dp", [(i, i ^ step) for i in range(size)])
+        upper = (place // step) % 2 == 1
+        value = jnp.concatenate(
+            [jnp.where(upper, other, value), jnp.where(upper, value, other)], axis=0
+        )
+        step *= 2
+    return value
+
+
+def beside(columns):
+    lane = lax.broadcasted_iota(jnp.int32, (1, len(columns)), 1)
+    return sum(jnp.where(lane == i, column, 0.0) for i, column in enumerate(columns))
 
 
 def latent_of(local, row, col):
@@ -152,13 +186,6 @@
 
     w_joined_own = jnp.concatenate([w_query, w_key, w_value], axis=1)
     far_joined = swap_row(w_joined_own, 2)
-    far_out = swap_row(after(w_out, far_joined), 2)
-    far_up = swap_row(after(w_up, far_out), 2)
-    far_down = swap_row(after(w_down, far_up), 2)
-    w_joined = gather_row(w_joined_own, far_joined)
-    w_out_all = gather_row(w_out, far_out)
-    w_up_all = gather_row(w_up, far_up)
-    w_down_all = gather_row(w_down, far_down)
 
     condition_float = condition.astype(F32)
     silu_cond = jax.nn.silu(condition_float).astype(BF16)
@@ -175,11 +202,21 @@
         [packed[0]] + [swap_row(packed[i], k) for i, k in enumerate(ORDER) if k], axis=1
     )
     columns = vectors.T
+    local_tokens = latent_of(tokens, row, col)
+    held = (vectors, local_tokens, far_joined)
+    far_out = swap_row(after(w_out, held), 2)
+    far_up = swap_row(after(w_up, far_out), 2)
+    far_down = swap_row(after(w_down, far_up), 2)
+    cot = latent_of(after(cotangent, far_up), row, col).astype(F32)
+    w_joined = gather_row(w_joined_own, far_joined)
+    w_out_all = gather_row(w_out, far_out)
+    w_up_all = gather_row(w_up, far_up)
+    w_down_all = gather_row(w_down, far_down)
     shift_attn, scale_attn, gate_attn, shift_mlp, scale_mlp, gate_mlp, bias_out, bias_down = (
         columns[:, i : i + 1] for i in range(8)
     )
 
-    x = latent_of(tokens, row, col).astype(F32)
+    x = local_tokens.astype(F32)
     normed_attn, inverse_attn = normalize(x)
     hidden_attn = (normed_attn * (1.0 + scale_attn) + shift_attn).astype(BF16)
     joined = contract(w_joined, hidden_attn, 0, 0)
@@ -204,30 +241,36 @@
     upward = contract(w_up_all, hidden_mlp, 0, 0) + b_up.astype(F32)[:, None]
     activated, gelu_back = jax.vjp(partial(jax.nn.gelu, approximate=True), upward)
     activated = activated.astype(BF16)
-    downward = pair_sum(contract(w_down_all, activated, 1, 0)) + bias_down
-    output = spread_out((residual + gate_mlp * downward).astype(BF16), row, col)
-
-    cot = latent_of(cotangent, row, col).astype(F32)
-    grad_gate_mlp = jnp.sum(cot * downward, axis=1)
+
     grad_down = (cot * gate_mlp).astype(BF16)
     grad_activated = contract(w_down_all, grad_down, 0, 0)
-    grad_w_down = sum_dp(scatter_row(contract(grad_down, activated, 1, 1).astype(BF16)))
-    grad_b_down = jnp.sum(grad_down.astype(F32), axis=1)
+    grad_b_down = jnp.sum(grad_down.astype(F32), axis=1, keepdims=True)
     grad_upward = gelu_back(grad_activated)[0].astype(BF16)
+    near_down = near_sum(grad_down, activated)
     grad_hidden = pair_sum(contract(w_up_all, grad_upward, 1, 0))
-    grad_w_up = sum_dp(scatter_row(contract(hidden_mlp, grad_upward, 1, 1).astype(BF16)))
-    grad_b_up = jnp.sum(grad_upward.astype(F32), axis=1)
-    grad_scale_mlp = jnp.sum(grad_hidden * normed_mlp, axis=1)
-    grad_shift_mlp = jnp.sum(grad_hidden, axis=1)
+    near_up = near_sum(hidden_mlp, grad_upward)
+    grad_b_up = jnp.sum(grad_upward.astype(F32), axis=1, keepdims=True)
+    grad_hidden, near_down, near_up = lax.optimization_barrier((grad_hidden, near_down, near_up))
+    sum_down = far_sum(near_down)
+    grad_scale_mlp = jnp.sum(grad_hidden * normed_mlp, axis=1, keepdims=True)
+    grad_shift_mlp = jnp.sum(grad_hidden, axis=1, keepdims=True)
     grad_residual = cot + normalize_back(grad_hidden * (1.0 + scale_mlp), normed_mlp, inverse_mlp)
 
-    grad_gate_attn = jnp.sum(grad_residual * projected, axis=1)
+    down_partial = after(contract(w_down_all, activated, 1, 0), grad_hidden)
+    downward = pair_sum(down_partial) + bias_down
+    output = spread_out((residual + gate_mlp * downward).astype(BF16), row, col)
+    grad_gate_mlp = jnp.sum(cot * downward, axis=1, keepdims=True)
+
+    grad_gate_attn = jnp.sum(grad_residual * projected, axis=1, keepdims=True)
     grad_projected = (grad_residual * gate_attn).astype(BF16)
-    grad_w_out = sum_dp(scatter_row(contract(grad_projected, attended, 1, 1).astype(BF16)))
-    grad_b_out = jnp.sum(grad_projected.astype(F32), axis=1)
+    near_out = near_sum(grad_projected, attended)
+    grad_b_out = jnp.sum(grad_projected.astype(F32), axis=1, keepdims=True)
     grad_heads = split_heads(contract(w_out_all, grad_projected, 0, 0).astype(BF16))
     grad_probs = contract_heads(grad_heads, values, 1, 1)
     grad_values = contract_heads(grad_heads, probabilities, 2, 1)
+    grad_probs, sum_down = lax.optimization_barrier((grad_probs, sum_down))
+    first_down = dp_first(sum_down)
+    sum_up = far_sum(near_up)
     inner = jnp.sum(full_probs * grad_probs, axis=-1, keepdims=True)
     grad_scores = (full_probs * (grad_probs - inner)).astype(BF16)
     grad_queries = contract_heads(keys, grad_scores, 2, 2) * scale_factor
@@ -237,16 +280,23 @@
         axis=0,
     )
     grad_hidden = pair_sum(contract(w_joined, grad_joined, 1, 0))
-    grad_w_joined = sum_dp(scatter_row(contract(hidden_attn, grad_joined, 1, 1).astype(BF16)))
-    grad_b_joined = jnp.sum(grad_joined.astype(F32), axis=1)
-    grad_scale_attn = jnp.sum(grad_hidden * normed_attn, axis=1)
-    grad_shift_attn = jnp.sum(grad_hidden, axis=1)
+    near_joined = near_sum(hidden_attn, grad_joined)
+    grad_b_joined = jnp.sum(grad_joined.astype(F32), axis=1, keepdims=True)
+    sum_out = far_sum(near_out)
+    grad_hidden, near_joined, first_down, sum_up, sum_out, output = lax.optimization_barrier(
+        (grad_hidden, near_joined, first_down, sum_up, sum_out, output)
+    )
+    total_down = dp_second(first_down)
+    first_up = dp_first(sum_up)
+    sum_joined = far_sum(near_joined)
+    grad_scale_attn = jnp.sum(grad_hidden * normed_attn, axis=1, keepdims=True)
+    grad_shift_attn = jnp.sum(grad_hidden, axis=1, keepdims=True)
     grad_x = grad_residual + normalize_back(
         grad_hidden * (1.0 + scale_attn), normed_attn, inverse_attn
     )
-    grad_tokens = spread_out(grad_x.astype(BF16), row, col).astype(F32)
-
-    own_vectors = jnp.stack(
+    grad_tokens = spread_out(grad_x.astype(BF16), row, col)
+
+    own_vectors = beside(
         [
             grad_shift_attn,
             grad_scale_attn,
@@ -257,8 +307,14 @@
             grad_b_down,
             grad_b_out,
         ]
-    ).astype(BF16)
-    pieces = [own_vectors[:, i * width_row : (i + 1) * width_row] for i in range(rows)]
+    ).astype(BF16).T
+    bias_grads = jnp.concatenate(
+        [grad_b_up, grad_b_joined[:width_col], grad_b_joined[2 * width_col :]]
+    ).reshape(-1, width_row).astype(BF16)
+    pieces = [
+        jnp.concatenate([own_vectors[:, i * width_row : (i + 1) * width_row], bias_grads])
+        for i in range(rows)
+    ]
     by_latent = jnp.stack([pieces[0]] + [swap_row(pieces[i], k) for i, k in enumerate(ORDER) if k])
     grad_mod = by_latent[:, :6].reshape(rows, -1)
     grad_silu = contract(grad_mod, mod_flat, 1, 0)
@@ -266,23 +322,40 @@
         swap_row(grad_silu[i : i + 1], k) for i, k in enumerate(ORDER) if k
     )
     grad_condition = jax.vjp(jax.nn.silu, condition_float)[1](grad_silu)[0]
-    message = jnp.concatenate([by_latent.reshape(rows, -1), cond_rows], axis=1)
-    everyone = lax.all_gather(message, "dp", axis=0, tiled=True)
+    bias_terms = by_latent[:, 8:].astype(F32)
+    bias_terms = (bias_terms[0] + bias_terms[1]) + (bias_terms[2] + bias_terms[3])
+    message = jnp.concatenate(
+        [
+            by_latent[:, :8].reshape(rows, -1),
+            cond_rows,
+            bias_terms.astype(BF16).reshape(rows, -1),
+        ],
+        axis=1,
+    )
+    everyone = gather_dp(message)
     all_mod = everyone[:, : 6 * width_row]
-    all_cond = everyone[:, 8 * width_row :]
+    all_cond = everyone[:, 8 * width_row : 8 * width_row + width_col]
     grad_w_mod = contract(all_mod, all_cond, 0, 0).reshape(w_mod.shape)
     sums = jnp.sum(everyone[:, : 8 * width_row].astype(F32), axis=0)
     grad_b_mod = sums[: 6 * width_row].reshape(b_mod.shape)
     grad_b_down = sums[6 * width_row : 7 * width_row]
     grad_b_out = sums[7 * width_row :]
-    bias_sums = lax.psum(
-        jnp.concatenate([grad_b_up, grad_b_joined[:width_col], grad_b_joined[2 * width_col :]]),
-        ("dp", "row"),
-    )
+    bias_parts = everyone[:, 8 * width_row + width_col :].astype(F32)
+    bias_sums = jnp.sum(bias_parts.reshape(-1, rows, bias_parts.shape[1]), axis=0).reshape(-1)
     hidden_width = grad_b_up.shape[0]
+
+    first_out = dp_first(sum_out)
+    first_joined = dp_first(sum_joined)
+    total_up = dp_second(first_up)
+    total_out = dp_second(first_out)
+    total_joined = dp_second(first_joined)
+    grad_w_down = dp_third(total_down)
+    grad_w_up = dp_third(total_up)
+    grad_w_out = dp_third(total_out)
+    grad_w_joined = dp_third(total_joined)
     return (
         output,
-        grad_tokens,
+        grad_tokens.astype(F32),
         grad_condition,
         grad_w_mod,
         grad_b_mod,

time: 350 us -> 277 us (0.79)
  blocking collectives: 73.3 us -> 0 us
  matrix products: 21 us -> 40.7 us
  local copies, waits for them, and re-layouts: 36.6 us -> 22.3 us
  waiting for transfers between devices: 117 us -> 107 us
  starting transfers between devices: 69.2 us -> 75.9 us
    psum x1 -> x0, blocking collectives: 59.4 us -> none  [body(): lax.psum(jnp.concatenate([grad_b_up, grad_b_joined[:width_col], grad_b_jo...]
    dot_general x15 -> x23, matrix products: 15.7 us -> 35.8 us  [contract(): lax.dot_general(left, right, (((left_dim,), (right_dim,)), ((), ())), pre...]
    all_gather x1 -> x0, blocking collectives: 13.9 us -> none  [body(): everyone = lax.all_gather(message, 'dp', axis=0, tiled=True)]
    ppermute x12 -> x14, waiting for transfers between devices: 49.8 us -> 39.5 us  [the longest x4 29.6 us: dp_third(): back = lax.ppermute(total, 'dp', dp_pairs()[2])]
    ppermute x6, waiting for transfers between devices: 1.94 us -> 9.81 us  [spread_out(): lax.ppermute(full[place * width:(place + 1) * width], ('row', 'col'), pairs)]
    ppermute x12 -> x14, starting transfers between devices: 23.4 us -> 29.4 us  [the longest x4 17.2 us: dp_first(): lax.ppermute(value, 'dp', dp_pairs()[0]).astype(F32)]
    slice x8 -> x2, local copies, waits for them, and re-layouts: 5.77 us -> 0.01 us  [the longest x1 0.01 us: body(): grad_b_joined[2 * width_col:]]
    ppermute x7, starting transfers between devices: 6.51 us -> 12 us  [swap_col(): return lax.ppermute(value, 'col', [(0, 1), (1, 0)])]
  transfers between devices with their start and end apart: 63 -> 65, of which waited for: 22 -> 29; matrix products, arithmetic and copies ran while one was open for 23% -> 27% of each run, Pallas kernels for 0% -> 0%
where the time goes in v2:
time: 277 us; the launch traced here: 276 us
  waiting for transfers between devices  107 us (39%)
  starting transfers between devices  75.9 us (27%)
  matrix products  40.7 us (15%)
  other arithmetic  27.6 us (10%)
  local copies, waits for them, and re-layouts  22.3 us (8%)
    ppermute x38, waiting for transfers between devices, swap_row(): return lax.ppermute(value, 'row', [(i, i ^ offset) for i in range(size)])  40.3 us
    dot_general x23, matrix products, contract(): lax.dot_general(left, right, (((left_dim,), (right_dim,)), ((), ())), pre...  35.8 us
    ppermute x4, waiting for transfers between devices, dp_third(): back = lax.ppermute(total, 'dp', dp_pairs()[2])  29.6 us
    ppermute x38, starting transfers between devices, swap_row(): return lax.ppermute(value, 'row', [(i, i ^ offset) for i in range(size)])  23.8 us
    ppermute x4, starting transfers between devices, dp_first(): lax.ppermute(value, 'dp', dp_pairs()[0]).astype(F32)  17.2 us
    ppermute x7, waiting for transfers between devices, swap_col(): return lax.ppermute(value, 'col', [(0, 1), (1, 0)])  17.1 us
    unnamed x215, local copies, waits for them, and re-layouts  13.7 us
    ppermute x7, starting transfers between devices, swap_col(): return lax.ppermute(value, 'col', [(0, 1), (1, 0)])  12 us
  transfers between devices with their start and end apart: 65, of which 29 were waited for; matrix products, arithmetic and copies ran while one was open for 27% of the time, Pallas kernels for 0%

profile of v2, /device:TPU:0, one launch (start us, length us, event | category | flops | bytes accessed | tf_op | source)
XLA Modules:
  0.0 275.8 jit_solution(5333853999939236440)
XLA Ops:
  3.6 3.0 %collective-permute-start = (bf16[192,1152]{1,0:T(8,128)(2,1)S(1)}, bf16[192,1152]{1,0:T(8,128)(2,1)S(1)}, u32[]{:S(2)}, u32[]{:S(2)}) collective-permute-start(bf16[192,1152]{1,0:T(8,128)(2,1)S(1)} %constant_dynamic-update-slice_fusion), channel_id=1, source_target_pairs={{0,4},{2,6},{4,0},{6,2},{1,5},{3,7},{5,1},{7,3},{8,12},{10,14},{12... | collective-permute-start | bytes 1327112 | tf_op jit(solution)/shard_map/ppermute | solution.py:30
  19.0 2.0 collective-permute-done.10
  27.4 3.8 %collective-permute-done.3 = bf16[192,512]{1,0:T(8,128)(2,1)S(1)} collective-permute-done((bf16[192,512]{1,0:T(8,128)(2,1)S(1)}, bf16[192,512]{1,0:T(8,128)(2,1)S(1)}, u32[]{:S(2)}, u32[]{:S(2)}) %collective-permute-start.3) | collective-permute-done | bytes 196640 | tf_op jit(solution)/shard_map/ppermute | solution.py:34
  33.5 2.5 collective-permute-done.6
  39.9 4.5 %collective-permute-done.14 = bf16[192,384]{1,0:T(8,128)(2,1)S(1)} collective-permute-done((bf16[192,384]{1,0:T(8,128)(2,1)S(1)}, bf16[192,384]{1,0:T(8,128)(2,1)S(1)}, u32[]{:S(2)}, u32[]{:S(2)}) %collective-permute-start.14) | collective-permute-done | bytes 147488 | tf_op jit(solution)/shard_map/ppermute | solution.py:30
  46.8 2.1 fusion.33
  54.5 6.9 %collective-permute-done.17 = bf16[192,1536]{1,0:T(8,128)(2,1)} collective-permute-done((bf16[192,1536]{1,0:T(8,128)(2,1)}, bf16[192,1536]{1,0:T(8,128)(2,1)}, u32[]{:S(2)}, u32[]{:S(2)}) %collective-permute-start.17) | collective-permute-done | bytes 589856 | tf_op jit(solution)/shard_map/ppermute | solution.py:30
  70.5 2.3 collective-permute-done.21
  77.0 11.0 %collective-permute-done.25 = bf16[192,1536]{1,0:T(8,128)(2,1)S(1)} collective-permute-done((bf16[192,1536]{1,0:T(8,128)(2,1)}, bf16[192,1536]{1,0:T(8,128)(2,1)S(1)}, u32[]{:S(2)}, u32[]{:S(2)}) %collective-permute-start.25) | collective-permute-done | bytes 589856 | tf_op jit(solution)/shard_map/ppermute | solution.py:30
  91.2 2.3 fusion.112
  98.2 2.5 fusion.125
  100.7 5.7 %collective-permute-done.28 = bf16[768,256]{1,0:T(8,128)(2,1)} collective-permute-done((bf16[768,256]{1,0:T(8,128)(2,1)}, bf16[768,256]{1,0:T(8,128)(2,1)}, u32[]{:S(2)}, u32[]{:S(2)}) %collective-permute-start.28) | collective-permute-done | bytes 393248 | tf_op jit(solution)/shard_map/ppermute | solution.py:34
  110.8 2.4 convert_add_fusion.2
  113.2 2.3 add_convert_fusion.6
  122.1 3.6 %collective-permute-done.38 = bf16[768,256]{1,0:T(8,128)(2,1)S(1)} collective-permute-done((bf16[768,256]{1,0:T(8,128)(2,1)S(1)}, bf16[768,256]{1,0:T(8,128)(2,1)S(1)}, u32[]{:S(2)}, u32[]{:S(2)}) %collective-permute-start.38) | collective-permute-done | bytes 393248 | tf_op jit(solution)/shard_map/ppermute | solution.py:34
  139.8 8.7 %collective-permute-done.41 = bf16[192,256]{1,0:T(8,128)(2,1)S(1)} collective-permute-done((bf16[192,256]{1,0:T(8,128)(2,1)S(1)}, bf16[192,256]{1,0:T(8,128)(2,1)S(1)}, u32[]{:S(2)}, u32[]{:S(2)}) %collective-permute-start.41) | collective-permute-done | bytes 98336 | tf_op jit(solution)/shard_map/ppermute | solution.py:135
  157.3 2.5 convolution_convert_fusion.3
  161.6 2.3 convolution_convert_fusion
  163.9 4.5 %collective-permute-start.34 = (bf16[192,1536]{1,0:T(8,128)(2,1)S(1)}, bf16[192,1536]{1,0:T(8,128)(2,1)}, u32[]{:S(2)}, u32[]{:S(2)}) collective-permute-start(bf16[192,1536]{1,0:T(8,128)(2,1)S(1)} %copy-done.9), channel_id=1, source_target_pairs={{0,8},{24,16},{1,9},{25,17},{2,10},{26,18},{3,11},{27,19},{4,12},{... | collective-permute-start | bytes 1769480 | tf_op jit(solution)/shard_map/ppermute | solution.py:73
  172.1 5.2 %collective-permute-done.37 = bf16[192,384]{1,0:T(8,128)(2,1)S(1)} collective-permute-done((bf16[192,384]{1,0:T(8,128)(2,1)S(1)}, bf16[192,384]{1,0:T(8,128)(2,1)S(1)}, u32[]{:S(2)}, u32[]{:S(2)}) %collective-permute-start.37) | collective-permute-done | bytes 147488 | tf_op jit(solution)/shard_map/ppermute | solution.py:30
  182.0 2.3 convert_add_fusion.4
  184.5 2.2 add_convert_fusion.11
  195.4 2.6 collective-permute-start.51
  201.1 2.1 collective-permute-start.42
  205.8 3.1 %collective-permute-done.52 = bf16[8,2496]{1,0:T(8,128)(2,1)S(1)} collective-permute-done((bf16[8,2496]{1,0:T(8,128)(2,1)S(1)}, bf16[8,2496]{1,0:T(8,128)(2,1)S(1)}, u32[]{:S(2)}, u32[]{:S(2)}) %collective-permute-start.52) | collective-permute-done | bytes 39968 | tf_op jit(solution)/shard_map/ppermute | solution.py:100
  208.9 2.2 collective-permute-start.57
  216.2 9.0 %collective-permute-start.60 = (bf16[192,1536]{1,0:T(8,128)(2,1)S(1)}, bf16[192,1536]{1,0:T(8,128)(2,1)S(1)}, u32[]{:S(2)}, u32[]{:S(2)}) collective-permute-start(bf16[192,1536]{1,0:T(8,128)(2,1)S(1)} %add_convert_fusion.3), channel_id=1, source_target_pairs={{0,8},{24,16},{1,9},{25,17},{2,10},{26,18},{3,11},{27,19},{4,12},{... | collective-permute-start | bytes 1769480 | tf_op jit(solution)/shard_map/ppermute | solution.py:73
  228.1 4.9 %collective-permute-done.59 = bf16[192,384]{1,0:T(8,128)(2,1)S(1)} collective-permute-done((bf16[192,384]{1,0:T(8,128)(2,1)S(1)}, bf16[192,384]{1,0:T(8,128)(2,1)S(1)}, u32[]{:S(2)}, u32[]{:S(2)}) %collective-permute-start.59) | collective-permute-done | bytes 147488 | tf_op jit(solution)/shard_map/ppermute | solution.py:91
  239.6 4.6 %collective-permute-done.54 = bf16[192,1152]{1,0:T(8,128)(2,1)S(1)} collective-permute-done((bf16[192,1152]{1,0:T(8,128)(2,1)S(1)}, bf16[192,1152]{1,0:T(8,128)(2,1)S(1)}, u32[]{:S(2)}, u32[]{:S(2)}) %collective-permute-start.54) | collective-permute-done | bytes 442400 | tf_op jit(solution)/shard_map/ppermute | solution.py:73
  246.4 9.2 %collective-permute-done.64 = bf16[192,1536]{1,0:T(8,128)(2,1)S(1)} collective-permute-done((bf16[192,1536]{1,0:T(8,128)(2,1)S(1)}, bf16[192,1536]{1,0:T(8,128)(2,1)S(1)}, u32[]{:S(2)}, u32[]{:S(2)}) %collective-permute-start.64) | collective-permute-done | bytes 589856 | tf_op jit(solution)/shard_map/ppermute | solution.py:91
  258.1 11.9 %collective-permute-done.62 = bf16[192,1536]{1,0:T(8,128)(2,1)S(1)} collective-permute-done((bf16[192,1536]{1,0:T(8,128)(2,1)S(1)}, bf16[192,1536]{1,0:T(8,128)(2,1)S(1)}, u32[]{:S(2)}, u32[]{:S(2)}) %collective-permute-start.62) | collective-permute-done | bytes 589856 | tf_op jit(solution)/shard_map/ppermute | solution.py:91
  271.1 3.7 %collective-permute-done.56 = bf16[192,1152]{1,0:T(8,128)(2,1)S(1)} collective-permute-done((bf16[192,1152]{1,0:T(8,128)(2,1)S(1)}, bf16[192,1152]{1,0:T(8,128)(2,1)S(1)}, u32[]{:S(2)}, u32[]{:S(2)}) %collective-permute-start.56) | collective-permute-done | bytes 442400 | tf_op jit(solution)/shard_map/ppermute | solution.py:91
  (453 shorter events, 135.3 us)
Async XLA Ops:
  3.6 34.9 %collective-permute-start = (bf16[192,1152]{1,0:T(8,128)(2,1)S(1)}, bf16[192,1152]{1,0:T(8,128)(2,1)S(1)}, u32[]{:S(2)}, u32[]{:S(2)}) collective-permute-start(bf16[192,1152]{1,0:T(8,128)(2,1)S(1)} %constant_dynamic-update-slice_fusion), channel_id=1, source_target_pairs={{0,4},{2,6},{4,0},{6,2},{1,5},{3,7},{5,1},{7,3},{8,12},{10,14},{12... | collective-permute-start | bytes 1327112 | tf_op jit(solution)/shard_map/ppermute | solution.py:30
  6.7 40.1 %collective-permute-start.1 = (bf16[192,1152]{1,0:T(8,128)(2,1)S(1)}, bf16[192,1152]{1,0:T(8,128)(2,1)}, u32[]{:S(2)}, u32[]{:S(2)}) collective-permute-start(bf16[192,1152]{1,0:T(8,128)(2,1)S(1)} %constant_dynamic-update-slice_fusion), channel_id=1, source_target_pairs={{0,2},{2,0},{4,6},{6,4},{1,3},{3,1},{5,7},{7,5},{8,10},{10,8},{12,... | collective-permute-start | bytes 1327112 | tf_op jit(solution)/shard_map/ppermute | solution.py:30
  8.0 8.9 %collective-permute-start.7 = (bf16[1,384]{1,0:T(2,128)(2,1)S(1)}, bf16[1,384]{1,0:T(2,128)(2,1)S(1)}, u32[]{:S(2)}, u32[]{:S(2)}) collective-permute-start(bf16[1,384]{1,0:T(2,128)(2,1)S(1)} %multiply_convert_fusion.3), channel_id=1, source_target_pairs={{0,4},{2,6},{4,0},{6,2},{1,5},{3,7},{5,1},{7,3},{8,12},{10,14},{12... | collective-permute-start | bytes 2312 | tf_op jit(solution)/shard_map/ppermute | solution.py:30
  36.1 53.9 %collective-permute-start.26 = (bf16[192,1536]{1,0:T(8,128)(2,1)}, bf16[192,1536]{1,0:T(8,128)(2,1)}, u32[]{:S(2)}, u32[]{:S(2)}) collective-permute-start(bf16[192,1536]{1,0:T(8,128)(2,1)} %param.29), channel_id=1, source_target_pairs={{0,2},{2,0},{4,6},{6,4},{1,3},{3,1},{5,7},{7,5},{8,10},{10,8},{12,... | collective-permute-start | bytes 1769480 | tf_op jit(solution)/shard_map/ppermute | solution.py:30
  44.4 19.8 %collective-permute-start.23 = (bf16[192,1536]{1,0:T(8,128)(2,1)}, bf16[192,1536]{1,0:T(8,128)(2,1)}, u32[]{:S(2)}, u32[]{:S(2)}) collective-permute-start(bf16[192,1536]{1,0:T(8,128)(2,1)} %param.27), channel_id=1, source_target_pairs={{0,2},{2,0},{4,6},{6,4},{1,3},{3,1},{5,7},{7,5},{8,10},{10,8},{12,... | collective-permute-start | bytes 1769480 | tf_op jit(solution)/shard_map/ppermute | solution.py:30
  45.7 15.7 %collective-permute-start.17 = (bf16[192,1536]{1,0:T(8,128)(2,1)}, bf16[192,1536]{1,0:T(8,128)(2,1)}, u32[]{:S(2)}, u32[]{:S(2)}) collective-permute-start(bf16[192,1536]{1,0:T(8,128)(2,1)} %param.27), channel_id=1, source_target_pairs={{0,4},{2,6},{4,0},{6,2},{1,5},{3,7},{5,1},{7,3},{8,12},{10,14},{12... | collective-permute-start | bytes 1769480 | tf_op jit(solution)/shard_map/ppermute | solution.py:30
  52.7 12.7 %collective-permute-start.22 = (bf16[768,256]{1,0:T(8,128)(2,1)S(1)}, bf16[768,256]{1,0:T(8,128)(2,1)S(1)}, u32[]{:S(2)}, u32[]{:S(2)}) collective-permute-start(bf16[768,256]{1,0:T(8,128)(2,1)S(1)} %convolution_convert_fusion.5), channel_id=1, source_target_pairs={{0,1},{1,0},{2,3},{3,2},{4,5},{5,4},{6,7},{7,6},{8,9},{9,8},{10,11... | collective-permute-start | bytes 1179656 | tf_op jit(solution)/shard_map/ppermute | solution.py:34
  63.1 12.6 %collective-permute-start.24 = (bf16[192,1536]{1,0:T(8,128)(2,1)}, bf16[192,1536]{1,0:T(8,128)(2,1)S(1)}, u32[]{:S(2)}, u32[]{:S(2)}) collective-permute-start(bf16[192,1536]{1,0:T(8,128)(2,1)} %collective-permute-done.17), channel_id=1, source_target_pairs={{0,2},{2,0},{4,6},{6,4},{1,3},{3,1},{5,7},{7,5},{8,10},{10,8},{12,... | collective-permute-start | bytes 1769480 | tf_op jit(solution)/shard_map/ppermute | solution.py:30
  72.7 15.2 %collective-permute-start.25 = (bf16[192,1536]{1,0:T(8,128)(2,1)}, bf16[192,1536]{1,0:T(8,128)(2,1)S(1)}, u32[]{:S(2)}, u32[]{:S(2)}) collective-permute-start(bf16[192,1536]{1,0:T(8,128)(2,1)} %param.29), channel_id=1, source_target_pairs={{0,4},{2,6},{4,0},{6,2},{1,5},{3,7},{5,1},{7,3},{8,12},{10,14},{12... | collective-permute-start | bytes 1769480 | tf_op jit(solution)/shard_map/ppermute | solution.py:30
  89.5 18.2 %collective-permute-start.29 = (bf16[384,1536]{1,0:T(8,128)(2,1)}, bf16[384,1536]{1,0:T(8,128)(2,1)}, u32[]{:S(2)}, u32[]{:S(2)}) collective-permute-start(bf16[384,1536]{1,0:T(8,128)(2,1)} %convolution_convert_fusion.2), channel_id=1, source_target_pairs={{0,2},{2,0},{4,6},{6,4},{1,3},{3,1},{5,7},{7,5},{8,10},{10,8},{12,... | collective-permute-start | bytes 3538952 | tf_op jit(solution)/shard_map/ppermute | solution.py:30
  95.1 11.3 %collective-permute-start.28 = (bf16[768,256]{1,0:T(8,128)(2,1)}, bf16[768,256]{1,0:T(8,128)(2,1)}, u32[]{:S(2)}, u32[]{:S(2)}) collective-permute-start(bf16[768,256]{1,0:T(8,128)(2,1)} %convolution_convert_fusion.4), channel_id=1, source_target_pairs={{0,1},{1,0},{2,3},{3,2},{4,5},{5,4},{6,7},{7,6},{8,9},{9,8},{10,11... | collective-permute-start | bytes 1179656 | tf_op jit(solution)/shard_map/ppermute | solution.py:34
  98.2 12.5 %collective-permute-start.30 = (bf16[384,1536]{1,0:T(8,128)(2,1)}, bf16[384,1536]{1,0:T(8,128)(2,1)}, u32[]{:S(2)}, u32[]{:S(2)}) collective-permute-start(bf16[384,1536]{1,0:T(8,128)(2,1)} %convolution_convert_fusion.1), channel_id=1, source_target_pairs={{0,2},{2,0},{4,6},{6,4},{1,3},{3,1},{5,7},{7,5},{8,10},{10,8},{12,... | collective-permute-start | bytes 3538952 | tf_op jit(solution)/shard_map/ppermute | solution.py:30
  115.6 10.2 %collective-permute-start.38 = (bf16[768,256]{1,0:T(8,128)(2,1)S(1)}, bf16[768,256]{1,0:T(8,128)(2,1)S(1)}, u32[]{:S(2)}, u32[]{:S(2)}) collective-permute-start(bf16[768,256]{1,0:T(8,128)(2,1)S(1)} %fusion.125), channel_id=1, source_target_pairs={{0,1},{1,0},{2,3},{3,2},{4,5},{5,4},{6,7},{7,6},{8,9},{9,8},{10,11... | collective-permute-start | bytes 1179656 | tf_op jit(solution)/shard_map/ppermute | solution.py:34
  120.1 30.2 %collective-permute-start.31 = (bf16[192,1536]{1,0:T(8,128)(2,1)S(1)}, bf16[192,1536]{1,0:T(8,128)(2,1)S(1)}, u32[]{:S(2)}, u32[]{:S(2)}) collective-permute-start(bf16[192,1536]{1,0:T(8,128)(2,1)S(1)} %add_convert_fusion.7), channel_id=1, source_target_pairs={{0,4},{2,6},{4,0},{6,2},{1,5},{3,7},{5,1},{7,3},{8,12},{10,14},{12... | collective-permute-start | bytes 1769480 | tf_op jit(solution)/shard_map/ppermute | solution.py:30
  121.1 47.5 %collective-permute-start.35 = (bf16[192,1536]{1,0:T(8,128)(2,1)}, bf16[192,1536]{1,0:T(8,128)(2,1)}, u32[]{:S(2)}, u32[]{:S(2)}) collective-permute-start(bf16[192,1536]{1,0:T(8,128)(2,1)} %add_convert_fusion.6), channel_id=1, source_target_pairs={{0,4},{2,6},{4,0},{6,2},{1,5},{3,7},{5,1},{7,3},{8,12},{10,14},{12... | collective-permute-start | bytes 1769480 | tf_op jit(solution)/shard_map/ppermute | solution.py:30
  135.7 12.8 %collective-permute-start.41 = (bf16[192,256]{1,0:T(8,128)(2,1)S(1)}, bf16[192,256]{1,0:T(8,128)(2,1)S(1)}, u32[]{:S(2)}, u32[]{:S(2)}) collective-permute-start(bf16[192,256]{1,0:T(8,128)(2,1)S(1)} %get-tuple-element.101), channel_id=1, source_target_pairs={{0,6},{2,4},{5,3},{7,1},{8,14},{10,12},{13,11},{15,9},{16,22},{18,... | collective-permute-start | bytes 294920 | tf_op jit(solution)/shard_map/ppermute | solution.py:135
  137.0 12.6 %collective-permute-start.39 = (bf16[192,256]{1,0:T(8,128)(2,1)S(1)}, bf16[192,256]{1,0:T(8,128)(2,1)S(1)}, u32[]{:S(2)}, u32[]{:S(2)}) collective-permute-start(bf16[192,256]{1,0:T(8,128)(2,1)S(1)} %get-tuple-element.100), channel_id=1, source_target_pairs={{0,4},{2,6},{5,1},{7,3},{8,12},{10,14},{13,9},{15,11},{16,20},{18,... | collective-permute-start | bytes 294920 | tf_op jit(solution)/shard_map/ppermute | solution.py:135
  139.6 30.3 %collective-permute-start.36 = (bf16[384,384]{1,0:T(8,128)(2,1)}, bf16[384,384]{1,0:T(8,128)(2,1)S(1)}, u32[]{:S(2)}, u32[]{:S(2)}) collective-permute-start(bf16[384,384]{1,0:T(8,128)(2,1)} %convolution_convert_fusion.6), channel_id=1, source_target_pairs={{0,2},{2,0},{4,6},{6,4},{1,3},{3,1},{5,7},{7,5},{8,10},{10,8},{12,... | collective-permute-start | bytes 884744 | tf_op jit(solution)/shard_map/ppermute | solution.py:30
  159.8 18.4 %collective-permute-start.32 = (bf16[768,256]{1,0:T(8,128)(2,1)}, bf16[768,256]{1,0:T(8,128)(2,1)}, u32[]{:S(2)}, u32[]{:S(2)}) collective-permute-start(bf16[768,256]{1,0:T(8,128)(2,1)} %convolution_convert_fusion.3), channel_id=1, source_target_pairs={{0,1},{1,0},{2,3},{3,2},{4,5},{5,4},{6,7},{7,6},{8,9},{9,8},{10,11... | collective-permute-start | bytes 1179656 | tf_op jit(solution)/shard_map/ppermute | solution.py:34
  163.9 18.1 %collective-permute-start.33 = (bf16[384,1152]{1,0:T(8,128)(2,1)}, bf16[384,1152]{1,0:T(8,128)(2,1)}, u32[]{:S(2)}, u32[]{:S(2)}) collective-permute-start(bf16[384,1152]{1,0:T(8,128)(2,1)} %convolution_convert_fusion), channel_id=1, source_target_pairs={{0,2},{2,0},{4,6},{6,4},{1,3},{3,1},{5,7},{7,5},{8,10},{10,8},{12,... | collective-permute-start | bytes 2654216 | tf_op jit(solution)/shard_map/ppermute | solution.py:30
  163.9 16.9 %collective-permute-start.34 = (bf16[192,1536]{1,0:T(8,128)(2,1)S(1)}, bf16[192,1536]{1,0:T(8,128)(2,1)}, u32[]{:S(2)}, u32[]{:S(2)}) collective-permute-start(bf16[192,1536]{1,0:T(8,128)(2,1)S(1)} %copy-done.9), channel_id=1, source_target_pairs={{0,8},{24,16},{1,9},{25,17},{2,10},{26,18},{3,11},{27,19},{4,12},{... | collective-permute-start | bytes 1769480 | tf_op jit(solution)/shard_map/ppermute | solution.py:73
  190.7 34.5 %collective-permute-start.43 = (bf16[192,256]{1,0:T(8,128)(2,1)}, bf16[192,256]{1,0:T(8,128)(2,1)S(1)}, u32[]{:S(2)}, u32[]{:S(2)}) collective-permute-start(bf16[192,256]{1,0:T(8,128)(2,1)} %get-tuple-element.99), channel_id=1, source_target_pairs={{0,2},{2,0},{5,7},{7,5},{8,10},{10,8},{13,15},{15,13},{16,18},{18,... | collective-permute-start | bytes 294920 | tf_op jit(solution)/shard_map/ppermute | solution.py:135
  192.6 33.3 %collective-permute-start.44 = (bf16[192,256]{1,0:T(8,128)(2,1)}, bf16[192,256]{1,0:T(8,128)(2,1)}, u32[]{:S(2)}, u32[]{:S(2)}) collective-permute-start(bf16[192,256]{1,0:T(8,128)(2,1)} %get-tuple-element.98), channel_id=1, source_target_pairs={{0,6},{2,4},{5,3},{7,1},{8,14},{10,12},{13,11},{15,9},{16,22},{18,... | collective-permute-start | bytes 294920 | tf_op jit(solution)/shard_map/ppermute | solution.py:135
  201.1 26.2 %collective-permute-start.42 = (bf16[192,256]{1,0:T(8,128)(2,1)}, bf16[192,256]{1,0:T(8,128)(2,1)S(1)}, u32[]{:S(2)}, u32[]{:S(2)}) collective-permute-start(bf16[192,256]{1,0:T(8,128)(2,1)} %get-tuple-element.97), channel_id=1, source_target_pairs={{0,4},{2,6},{5,1},{7,3},{8,12},{10,14},{13,9},{15,11},{16,20},{18,... | collective-permute-start | bytes 294920 | tf_op jit(solution)/shard_map/ppermute | solution.py:135
  203.2 30.6 %collective-permute-start.53 = (bf16[192,1152]{1,0:T(8,128)(2,1)}, bf16[192,1152]{1,0:T(8,128)(2,1)}, u32[]{:S(2)}, u32[]{:S(2)}) collective-permute-start(bf16[192,1152]{1,0:T(8,128)(2,1)} %add_convert_fusion.11), channel_id=1, source_target_pairs={{0,4},{2,6},{4,0},{6,2},{1,5},{3,7},{5,1},{7,3},{8,12},{10,14},{12... | collective-permute-start | bytes 1327112 | tf_op jit(solution)/shard_map/ppermute | solution.py:30
  216.2 21.1 %collective-permute-start.60 = (bf16[192,1536]{1,0:T(8,128)(2,1)S(1)}, bf16[192,1536]{1,0:T(8,128)(2,1)S(1)}, u32[]{:S(2)}, u32[]{:S(2)}) collective-permute-start(bf16[192,1536]{1,0:T(8,128)(2,1)S(1)} %add_convert_fusion.3), channel_id=1, source_target_pairs={{0,8},{24,16},{1,9},{25,17},{2,10},{26,18},{3,11},{27,19},{4,12},{... | collective-permute-start | bytes 1769480 | tf_op jit(solution)/shard_map/ppermute | solution.py:73
  225.3 12.8 %collective-permute-start.63 = (bf16[192,1536]{1,0:T(8,128)(2,1)S(1)}, bf16[192,1536]{1,0:T(8,128)(2,1)S(1)}, u32[]{:S(2)}, u32[]{:S(2)}) collective-permute-start(bf16[192,1536]{1,0:T(8,128)(2,1)S(1)} %add_convert_fusion.4), channel_id=1, source_target_pairs={{8,16},{16,8},{9,17},{17,9},{10,18},{18,10},{11,19},{19,11},{12,20... | collective-permute-start | bytes 1769480 | tf_op jit(solution)/shard_map/ppermute | solution.py:78
  234.9 9.3 %collective-permute-start.54 = (bf16[192,1152]{1,0:T(8,128)(2,1)S(1)}, bf16[192,1152]{1,0:T(8,128)(2,1)S(1)}, u32[]{:S(2)}, u32[]{:S(2)}) collective-permute-start(bf16[192,1152]{1,0:T(8,128)(2,1)S(1)} %add_convert_fusion.10), channel_id=1, source_target_pairs={{0,8},{24,16},{1,9},{25,17},{2,10},{26,18},{3,11},{27,19},{4,12},{... | collective-permute-start | bytes 1327112 | tf_op jit(solution)/shard_map/ppermute | solution.py:73
  238.3 17.4 %collective-permute-start.64 = (bf16[192,1536]{1,0:T(8,128)(2,1)S(1)}, bf16[192,1536]{1,0:T(8,128)(2,1)S(1)}, u32[]{:S(2)}, u32[]{:S(2)}) collective-permute-start(bf16[192,1536]{1,0:T(8,128)(2,1)S(1)} %add_convert_fusion), channel_id=1, source_target_pairs={{8,0},{16,24},{9,1},{17,25},{10,2},{18,26},{11,3},{19,27},{12,4},{... | collective-permute-start | bytes 1769480 | tf_op jit(solution)/shard_map/ppermute | solution.py:91
  244.3 12.4 %collective-permute-start.55 = (bf16[192,1152]{1,0:T(8,128)(2,1)S(1)}, bf16[192,1152]{1,0:T(8,128)(2,1)S(1)}, u32[]{:S(2)}, u32[]{:S(2)}) collective-permute-start(bf16[192,1152]{1,0:T(8,128)(2,1)S(1)} %add_convert_fusion.9), channel_id=1, source_target_pairs={{8,16},{16,8},{9,17},{17,9},{10,18},{18,10},{11,19},{19,11},{12,20... | collective-permute-start | bytes 1327112 | tf_op jit(solution)/shard_map/ppermute | solution.py:78
  245.1 24.9 %collective-permute-start.62 = (bf16[192,1536]{1,0:T(8,128)(2,1)S(1)}, bf16[192,1536]{1,0:T(8,128)(2,1)S(1)}, u32[]{:S(2)}, u32[]{:S(2)}) collective-permute-start(bf16[192,1536]{1,0:T(8,128)(2,1)S(1)} %add_convert_fusion.1), channel_id=1, source_target_pairs={{8,0},{16,24},{9,1},{17,25},{10,2},{18,26},{11,3},{19,27},{12,4},{... | collective-permute-start | bytes 1769480 | tf_op jit(solution)/shard_map/ppermute | solution.py:91
  256.8 17.9 %collective-permute-start.56 = (bf16[192,1152]{1,0:T(8,128)(2,1)S(1)}, bf16[192,1152]{1,0:T(8,128)(2,1)S(1)}, u32[]{:S(2)}, u32[]{:S(2)}) collective-permute-start(bf16[192,1152]{1,0:T(8,128)(2,1)S(1)} %add_convert_fusion.8), channel_id=1, source_target_pairs={{8,0},{16,24},{9,1},{17,25},{10,2},{18,26},{11,3},{19,27},{12,4},{... | collective-permute-start | bytes 1327112 | tf_op jit(solution)/shard_map/ppermute | solution.py:91
  (134 other events, 898.2 us)

commit v3 on v2

--- a/solution.py
+++ b/solution.py
@@ -184,14 +184,13 @@
     width_col = w_query.shape[1]
     heads = width_col // HEAD_DIM
 
-    w_joined_own = jnp.concatenate([w_query, w_key, w_value], axis=1)
-    far_joined = swap_row(w_joined_own, 2)
-
     condition_float = condition.astype(F32)
     silu_cond = jax.nn.silu(condition_float).astype(BF16)
     cond_rows = jnp.concatenate(
         [silu_cond] + [swap_row(silu_cond, k) for k in ORDER[1:]], axis=0
     )
+    w_joined_own = jnp.concatenate([after(w_query, cond_rows), w_key, w_value], axis=1)
+    far_joined = swap_row(w_joined_own, 2)
     mod_flat = w_mod.reshape(-1, w_mod.shape[2])
     terms = contract(cond_rows, mod_flat, 1, 1)
     terms = terms + swap_col(terms)
@@ -203,7 +202,7 @@
     )
     columns = vectors.T
     local_tokens = latent_of(tokens, row, col)
-    held = (vectors, local_tokens, far_joined)
+    held = (local_tokens, far_joined)
     far_out = swap_row(after(w_out, held), 2)
     far_up = swap_row(after(w_up, far_out), 2)
     far_down = swap_row(after(w_down, far_up), 2)
@@ -269,7 +268,8 @@
     grad_probs = contract_heads(grad_heads, values, 1, 1)
     grad_values = contract_heads(grad_heads, probabilities, 2, 1)
     grad_probs, sum_down = lax.optimization_barrier((grad_probs, sum_down))
-    first_down = dp_first(sum_down)
+    total_down = lax.psum(sum_down, "dp")
+    grad_w_down = total_down.astype(F32)
     sum_up = far_sum(near_up)
     inner = jnp.sum(full_probs * grad_probs, axis=-1, keepdims=True)
     grad_scores = (full_probs * (grad_probs - inner)).astype(BF16)
@@ -279,15 +279,12 @@
         [part.reshape(width_col, LEN).astype(BF16) for part in (grad_queries, grad_keys, grad_values)],
         axis=0,
     )
+    sum_out = far_sum(near_out)
+    grad_joined, sum_up, sum_out = lax.optimization_barrier((grad_joined, sum_up, sum_out))
+    grad_w_up, grad_w_out = (t.astype(F32) for t in lax.psum((after(sum_up, total_down), sum_out), "dp"))
     grad_hidden = pair_sum(contract(w_joined, grad_joined, 1, 0))
     near_joined = near_sum(hidden_attn, grad_joined)
     grad_b_joined = jnp.sum(grad_joined.astype(F32), axis=1, keepdims=True)
-    sum_out = far_sum(near_out)
-    grad_hidden, near_joined, first_down, sum_up, sum_out, output = lax.optimization_barrier(
-        (grad_hidden, near_joined, first_down, sum_up, sum_out, output)
-    )
-    total_down = dp_second(first_down)
-    first_up = dp_first(sum_up)
     sum_joined = far_sum(near_joined)
     grad_scale_attn = jnp.sum(grad_hidden * normed_attn, axis=1, keepdims=True)
     grad_shift_attn = jnp.sum(grad_hidden, axis=1, keepdims=True)
@@ -344,15 +341,7 @@
     bias_sums = jnp.sum(bias_parts.reshape(-1, rows, bias_parts.shape[1]), axis=0).reshape(-1)
     hidden_width = grad_b_up.shape[0]
 
-    first_out = dp_first(sum_out)
-    first_joined = dp_first(sum_joined)
-    total_up = dp_second(first_up)
-    total_out = dp_second(first_out)
-    total_joined = dp_second(first_joined)
-    grad_w_down = dp_third(total_down)
-    grad_w_up = dp_third(total_up)
-    grad_w_out = dp_third(total_out)
-    grad_w_joined = dp_third(total_joined)
+    grad_w_joined = dp_third(dp_second(dp_first(sum_joined)))
     return (
         output,
         grad_tokens.astype(F32),

time: 277 us -> 288 us (1.040)
  waiting for transfers between devices: 107 us -> 130 us
  starting transfers between devices: 75.9 us -> 53.7 us
  between operations: 2.49 us -> 15.9 us
  matrix products: 40.7 us -> 34.4 us
  other arithmetic: 27.6 us -> 32.3 us
    psum x0 -> x2, waiting for transfers between devices: none -> 20.1 us  [the longest x1 20.1 us: body(): total_down = lax.psum(sum_down, 'dp')]
    ppermute x38, waiting for transfers between devices: 40.3 us -> 55.6 us  [swap_row(): return lax.ppermute(value, 'row', [(i, i ^ offset) for i in range(size)])]
    ppermute x4 -> x1, starting transfers between devices: 17.2 us -> 2.86 us  [dp_first(): lax.ppermute(value, 'dp', dp_pairs()[0]).astype(F32)]
    ppermute x4 -> x1, waiting for transfers between devices: 29.6 us -> 17 us  [dp_third(): back = lax.ppermute(total, 'dp', dp_pairs()[2])]
    convert_element_type x0 -> x3, other arithmetic: none -> 6.13 us  [the longest x2 3.85 us: body(): t.astype(F32)]
    dot_general x23, matrix products: 35.8 us -> 30.2 us  [contract(): lax.dot_general(left, right, (((left_dim,), (right_dim,)), ((), ())), pre...]
    ppermute x4 -> x1, waiting for transfers between devices: 6.79 us -> 11.9 us  [dp_first(): lax.ppermute(value, 'dp', dp_pairs()[0]).astype(F32)]
    ppermute x7, starting transfers between devices: 12 us -> 7.82 us  [swap_col(): return lax.ppermute(value, 'col', [(0, 1), (1, 0)])]
  transfers between devices with their start and end apart: 65 -> 58, of which waited for: 29 -> 24; matrix products, arithmetic and copies ran while one was open for 27% -> 27% of each run, Pallas kernels for 0% -> 0%
where the time goes in v3:
time: 288 us; the launch traced here: 287 us
  waiting for transfers between devices  130 us (45%)
  starting transfers between devices  53.7 us (19%)
  matrix products  34.4 us (12%)
  other arithmetic  32.3 us (11%)
  local copies, waits for them, and re-layouts  20.5 us (7%)
  between operations  15.9 us (6%)
    ppermute x38, waiting for transfers between devices, swap_row(): return lax.ppermute(value, 'row', [(i, i ^ offset) for i in range(size)])  55.6 us
    dot_general x23, matrix products, contract(): lax.dot_general(left, right, (((left_dim,), (right_dim,)), ((), ())), pre...  30.2 us
    ppermute x38, starting transfers between devices, swap_row(): return lax.ppermute(value, 'row', [(i, i ^ offset) for i in range(size)])  26.5 us
    psum x1, waiting for transfers between devices, body(): total_down = lax.psum(sum_down, 'dp')  20.1 us
    ppermute x7, waiting for transfers between devices, swap_col(): return lax.ppermute(value, 'col', [(0, 1), (1, 0)])  17.7 us
    ppermute x1, waiting for transfers between devices, dp_third(): back = lax.ppermute(total, 'dp', dp_pairs()[2])  17 us
    unnamed x201, local copies, waits for them, and re-layouts  12.9 us
    ppermute x1, waiting for transfers between devices, dp_first(): lax.ppermute(value, 'dp', dp_pairs()[0]).astype(F32)  11.9 us
  transfers between devices with their start and end apart: 58, of which 24 were waited for; matrix products, arithmetic and copies ran while one was open for 27% of the time, Pallas kernels for 0%

profile of v3, /device:TPU:0, one launch (start us, length us, event | category | flops | bytes accessed | tf_op | source)
XLA Modules:
  0.0 287.3 jit_solution(4822275479391119767)
XLA Ops:
  8.1 2.5 collective-permute-start.6
  13.3 2.0 constant_dynamic-update-slice_fusion.12
  20.8 3.7 %collective-permute-done.7 = f32[4,1152]{1,0:T(4,128)S(1)} collective-permute-done((f32[4,1152]{1,0:T(4,128)S(1)}, f32[4,1152]{1,0:T(4,128)S(1)}, u32[]{:S(2)}, u32[]{:S(2)}) %collective-permute-start.7) | collective-permute-done | bytes 18464 | tf_op jit(solution)/shard_map/ppermute | solution.py:34
  27.9 2.1 collective-permute-done.8
  36.8 9.4 %collective-permute-done.11 = bf16[192,1152]{1,0:T(8,128)(2,1)S(1)} collective-permute-done((bf16[192,1152]{1,0:T(8,128)(2,1)S(1)}, bf16[192,1152]{1,0:T(8,128)(2,1)S(1)}, u32[]{:S(2)}, u32[]{:S(2)}) %collective-permute-start.11) | collective-permute-done | bytes 442400 | tf_op jit(solution)/shard_map/ppermute | solution.py:30
  48.2 3.1 %collective-permute-done.12 = bf16[192,384]{1,0:T(8,128)(2,1)S(1)} collective-permute-done((bf16[192,384]{1,0:T(8,128)(2,1)S(1)}, bf16[192,384]{1,0:T(8,128)(2,1)S(1)}, u32[]{:S(2)}, u32[]{:S(2)}) %collective-permute-start.12) | collective-permute-done | bytes 147488 | tf_op jit(solution)/shard_map/ppermute | solution.py:30
  59.1 9.3 %collective-permute-done.18 = bf16[192,1536]{1,0:T(8,128)(2,1)} collective-permute-done((bf16[192,1536]{1,0:T(8,128)(2,1)}, bf16[192,1536]{1,0:T(8,128)(2,1)}, u32[]{:S(2)}, u32[]{:S(2)}) %collective-permute-start.18) | collective-permute-done | bytes 589856 | tf_op jit(solution)/shard_map/ppermute | solution.py:30
  71.8 2.7 collective-permute-done.24
  77.1 2.4 collective-permute-done.27
  84.0 11.1 %collective-permute-done.19 = bf16[192,1536]{1,0:T(8,128)(2,1)S(1)} collective-permute-done((bf16[192,1536]{1,0:T(8,128)(2,1)S(1)}, bf16[192,1536]{1,0:T(8,128)(2,1)S(1)}, u32[]{:S(2)}, u32[]{:S(2)}) %collective-permute-start.19) | collective-permute-done | bytes 589856 | tf_op jit(solution)/shard_map/ppermute | solution.py:30
  98.4 2.3 fusion.103
  104.4 2.5 fusion.116
  106.9 6.7 %collective-permute-done.28 = bf16[768,256]{1,0:T(8,128)(2,1)} collective-permute-done((bf16[768,256]{1,0:T(8,128)(2,1)}, bf16[768,256]{1,0:T(8,128)(2,1)}, u32[]{:S(2)}, u32[]{:S(2)}) %collective-permute-start.28) | collective-permute-done | bytes 393248 | tf_op jit(solution)/shard_map/ppermute | solution.py:34
  117.9 2.4 convert_add_fusion.2
  120.4 2.3 add_convert_fusion.2
  128.2 4.7 %collective-permute-done.31 = bf16[768,256]{1,0:T(8,128)(2,1)S(1)} collective-permute-done((bf16[768,256]{1,0:T(8,128)(2,1)S(1)}, bf16[768,256]{1,0:T(8,128)(2,1)S(1)}, u32[]{:S(2)}, u32[]{:S(2)}) %collective-permute-start.31) | collective-permute-done | bytes 393248 | tf_op jit(solution)/shard_map/ppermute | solution.py:34
  146.9 7.0 %collective-permute-done.34 = bf16[192,256]{1,0:T(8,128)(2,1)S(1)} collective-permute-done((bf16[192,256]{1,0:T(8,128)(2,1)S(1)}, bf16[192,256]{1,0:T(8,128)(2,1)S(1)}, u32[]{:S(2)}, u32[]{:S(2)}) %collective-permute-start.34) | collective-permute-done | bytes 98336 | tf_op jit(solution)/shard_map/ppermute | solution.py:135
  161.7 2.0 add_convert_fusion
  165.5 2.5 collective-permute-start.38
  168.1 3.1 %collective-permute-done.38 = bf16[192,384]{1,0:T(8,128)(2,1)S(1)} collective-permute-done((bf16[192,384]{1,0:T(8,128)(2,1)S(1)}, bf16[192,384]{1,0:T(8,128)(2,1)S(1)}, u32[]{:S(2)}, u32[]{:S(2)}) %collective-permute-start.38) | collective-permute-done | bytes 147488 | tf_op jit(solution)/shard_map/ppermute | solution.py:30
  172.8 2.1 convolution_convert_fusion.3
  176.4 3.1 %collective-permute-start.39 = (bf16[768,256]{1,0:T(8,128)(2,1)S(1)}, bf16[768,256]{1,0:T(8,128)(2,1)}, u32[]{:S(2)}, u32[]{:S(2)}) collective-permute-start(bf16[768,256]{1,0:T(8,128)(2,1)S(1)} %convolution_convert_fusion.3), channel_id=1, source_target_pairs={{0,1},{1,0},{2,3},{3,2},{4,5},{5,4},{6,7},{7,6},{8,9},{9,8},{10,11... | collective-permute-start | bytes 1179656 | tf_op jit(solution)/shard_map/ppermute | solution.py:34
  180.3 20.1 %all-reduce.4.cloned.1.call-done = bf16[192,1536]{1,0:T(8,128)(2,1)} async-done(((bf16[192,1536]{1,0:T(8,128)(2,1)}), bf16[192,1536]{1,0:T(8,128)(2,1)}) %all-reduce.4.cloned.1.call-update) | async-done | bytes 589840 | tf_op jit(solution)/shard_map/psum | solution.py:271
  200.5 2.3 convert_element_type.356
  211.5 2.1 collective-permute-start.46
  214.5 2.9 %collective-permute-start.42 = (bf16[192,256]{1,0:T(8,128)(2,1)}, bf16[192,256]{1,0:T(8,128)(2,1)}, u32[]{:S(2)}, u32[]{:S(2)}) collective-permute-start(bf16[192,256]{1,0:T(8,128)(2,1)} %get-tuple-element.96), channel_id=1, source_target_pairs={{0,6},{2,4},{5,3},{7,1},{8,14},{10,12},{13,11},{15,9},{16,22},{18,... | collective-permute-start | bytes 294920 | tf_op jit(solution)/shard_map/ppermute | solution.py:135
  217.5 2.3 collective-permute-start.40
  225.5 9.7 %collective-permute-done.52 = bf16[192,1152]{1,0:T(8,128)(2,1)S(1)} collective-permute-done((bf16[192,1152]{1,0:T(8,128)(2,1)S(1)}, bf16[192,1152]{1,0:T(8,128)(2,1)S(1)}, u32[]{:S(2)}, u32[]{:S(2)}) %collective-permute-start.52) | collective-permute-done | bytes 442400 | tf_op jit(solution)/shard_map/ppermute | solution.py:30
  236.4 2.9 collective-permute-start.53
  240.7 11.9 %collective-permute-done.53 = bf16[192,1152]{1,0:T(8,128)(2,1)S(1)} collective-permute-done((bf16[192,1152]{1,0:T(8,128)(2,1)S(1)}, bf16[192,1152]{1,0:T(8,128)(2,1)S(1)}, u32[]{:S(2)}, u32[]{:S(2)}) %collective-permute-start.53) | collective-permute-done | bytes 442400 | tf_op jit(solution)/shard_map/ppermute | solution.py:73
  260.2 2.2 convert_element_type.355
  262.4 17.0 %collective-permute-done.55 = bf16[192,1152]{1,0:T(8,128)(2,1)S(1)} collective-permute-done((bf16[192,1152]{1,0:T(8,128)(2,1)S(1)}, bf16[192,1152]{1,0:T(8,128)(2,1)S(1)}, u32[]{:S(2)}, u32[]{:S(2)}) %collective-permute-start.55) | collective-permute-done | bytes 442400 | tf_op jit(solution)/shard_map/ppermute | solution.py:91
  (422 shorter events, 109.1 us)
Async XLA Ops:
  7.2 193.1 %all-reduce.4.cloned.1.call-start = ((), (), s32[]{:S(2)}) async-start(), calls=%async_computation | async-start | bytes 1179648 | tf_op jit(solution)/shard_map/psum | solution.py:271
  8.1 11.0 %collective-permute-start.6 = (bf16[1,384]{1,0:T(2,128)(2,1)S(1)}, bf16[1,384]{1,0:T(2,128)(2,1)S(1)}, u32[]{:S(2)}, u32[]{:S(2)}) collective-permute-start(bf16[1,384]{1,0:T(2,128)(2,1)S(1)} %multiply_convert_fusion.3), channel_id=1, source_target_pairs={{0,6},{2,4},{4,2},{6,0},{1,7},{3,5},{5,3},{7,1},{8,14},{10,12},{12... | collective-permute-start | bytes 2312 | tf_op jit(solution)/shard_map/ppermute | solution.py:30
  10.5 8.6 %collective-permute-start.5 = (bf16[1,384]{1,0:T(2,128)(2,1)S(1)}, bf16[1,384]{1,0:T(2,128)(2,1)S(1)}, u32[]{:S(2)}, u32[]{:S(2)}) collective-permute-start(bf16[1,384]{1,0:T(2,128)(2,1)S(1)} %multiply_convert_fusion.3), channel_id=1, source_target_pairs={{0,2},{2,0},{4,6},{6,4},{1,3},{3,1},{5,7},{7,5},{8,10},{10,8},{12,... | collective-permute-start | bytes 2312 | tf_op jit(solution)/shard_map/ppermute | solution.py:30
  11.3 18.7 %collective-permute-start = (bf16[192,512]{1,0:T(8,128)(2,1)}, bf16[192,512]{1,0:T(8,128)(2,1)S(1)}, u32[]{:S(2)}, u32[]{:S(2)}) collective-permute-start(bf16[192,512]{1,0:T(8,128)(2,1)} %param.16), channel_id=1, source_target_pairs={{0,1},{1,0},{2,3},{3,2},{4,5},{5,4},{6,7},{7,6},{8,9},{9,8},{10,11... | collective-permute-start | bytes 589832 | tf_op jit(solution)/shard_map/ppermute | solution.py:34
  13.2 83.9 %collective-permute-start.20 = (bf16[192,1536]{1,0:T(8,128)(2,1)}, bf16[192,1536]{1,0:T(8,128)(2,1)}, u32[]{:S(2)}, u32[]{:S(2)}) collective-permute-start(bf16[192,1536]{1,0:T(8,128)(2,1)} %param.29), channel_id=1, source_target_pairs={{0,2},{2,0},{4,6},{6,4},{1,3},{3,1},{5,7},{7,5},{8,10},{10,8},{12,... | collective-permute-start | bytes 1769480 | tf_op jit(solution)/shard_map/ppermute | solution.py:30
  27.7 23.6 %collective-permute-start.13 = (bf16[192,384]{1,0:T(8,128)(2,1)S(1)}, bf16[192,384]{1,0:T(8,128)(2,1)S(1)}, u32[]{:S(2)}, u32[]{:S(2)}) collective-permute-start(bf16[192,384]{1,0:T(8,128)(2,1)S(1)} %copy-done.43), channel_id=1, source_target_pairs={{0,2},{2,0},{4,6},{6,4},{1,3},{3,1},{5,7},{7,5},{8,10},{10,8},{12,... | collective-permute-start | bytes 442376 | tf_op jit(solution)/shard_map/ppermute | solution.py:30
  34.3 11.8 %collective-permute-start.11 = (bf16[192,1152]{1,0:T(8,128)(2,1)S(1)}, bf16[192,1152]{1,0:T(8,128)(2,1)S(1)}, u32[]{:S(2)}, u32[]{:S(2)}) collective-permute-start(bf16[192,1152]{1,0:T(8,128)(2,1)S(1)} %constant_dynamic-update-slice_fusion.2), channel_id=1, source_target_pairs={{0,4},{2,6},{4,0},{6,2},{1,5},{3,7},{5,1},{7,3},{8,12},{10,14},{12... | collective-permute-start | bytes 1327112 | tf_op jit(solution)/shard_map/ppermute | solution.py:30
  35.7 18.7 %collective-permute-start.15 = (bf16[192,1152]{1,0:T(8,128)(2,1)S(1)}, bf16[192,1152]{1,0:T(8,128)(2,1)S(1)}, u32[]{:S(2)}, u32[]{:S(2)}) collective-permute-start(bf16[192,1152]{1,0:T(8,128)(2,1)S(1)} %constant_dynamic-update-slice_fusion.2), channel_id=1, source_target_pairs={{0,2},{2,0},{4,6},{6,4},{1,3},{3,1},{5,7},{7,5},{8,10},{10,8},{12,... | collective-permute-start | bytes 1327112 | tf_op jit(solution)/shard_map/ppermute | solution.py:30
  51.3 18.8 %collective-permute-start.22 = (bf16[192,1536]{1,0:T(8,128)(2,1)}, bf16[192,1536]{1,0:T(8,128)(2,1)}, u32[]{:S(2)}, u32[]{:S(2)}) collective-permute-start(bf16[192,1536]{1,0:T(8,128)(2,1)} %param.27), channel_id=1, source_target_pairs={{0,2},{2,0},{4,6},{6,4},{1,3},{3,1},{5,7},{7,5},{8,10},{10,8},{12,... | collective-permute-start | bytes 1769480 | tf_op jit(solution)/shard_map/ppermute | solution.py:30
  52.7 15.7 %collective-permute-start.18 = (bf16[192,1536]{1,0:T(8,128)(2,1)}, bf16[192,1536]{1,0:T(8,128)(2,1)}, u32[]{:S(2)}, u32[]{:S(2)}) collective-permute-start(bf16[192,1536]{1,0:T(8,128)(2,1)} %param.27), channel_id=1, source_target_pairs={{0,4},{2,6},{4,0},{6,2},{1,5},{3,7},{5,1},{7,3},{8,12},{10,14},{12... | collective-permute-start | bytes 1769480 | tf_op jit(solution)/shard_map/ppermute | solution.py:30
  58.4 12.9 %collective-permute-start.17 = (bf16[768,256]{1,0:T(8,128)(2,1)S(1)}, bf16[768,256]{1,0:T(8,128)(2,1)S(1)}, u32[]{:S(2)}, u32[]{:S(2)}) collective-permute-start(bf16[768,256]{1,0:T(8,128)(2,1)S(1)} %convolution_convert_fusion.5), channel_id=1, source_target_pairs={{0,1},{1,0},{2,3},{3,2},{4,5},{5,4},{6,7},{7,6},{8,9},{9,8},{10,11... | collective-permute-start | bytes 1179656 | tf_op jit(solution)/shard_map/ppermute | solution.py:34
  69.0 13.7 %collective-permute-start.23 = (bf16[192,1536]{1,0:T(8,128)(2,1)}, bf16[192,1536]{1,0:T(8,128)(2,1)S(1)}, u32[]{:S(2)}, u32[]{:S(2)}) collective-permute-start(bf16[192,1536]{1,0:T(8,128)(2,1)} %collective-permute-done.18), channel_id=1, source_target_pairs={{0,2},{2,0},{4,6},{6,4},{1,3},{3,1},{5,7},{7,5},{8,10},{10,8},{12,... | collective-permute-start | bytes 1769480 | tf_op jit(solution)/shard_map/ppermute | solution.py:30
  79.4 15.7 %collective-permute-start.19 = (bf16[192,1536]{1,0:T(8,128)(2,1)S(1)}, bf16[192,1536]{1,0:T(8,128)(2,1)S(1)}, u32[]{:S(2)}, u32[]{:S(2)}) collective-permute-start(bf16[192,1536]{1,0:T(8,128)(2,1)S(1)} %copy-done.34), channel_id=1, source_target_pairs={{0,4},{2,6},{4,0},{6,2},{1,5},{3,7},{5,1},{7,3},{8,12},{10,14},{12... | collective-permute-start | bytes 1769480 | tf_op jit(solution)/shard_map/ppermute | solution.py:30
  96.6 18.2 %collective-permute-start.29 = (bf16[384,1536]{1,0:T(8,128)(2,1)}, bf16[384,1536]{1,0:T(8,128)(2,1)}, u32[]{:S(2)}, u32[]{:S(2)}) collective-permute-start(bf16[384,1536]{1,0:T(8,128)(2,1)} %convolution_convert_fusion.2), channel_id=1, source_target_pairs={{0,2},{2,0},{4,6},{6,4},{1,3},{3,1},{5,7},{7,5},{8,10},{10,8},{12,... | collective-permute-start | bytes 3538952 | tf_op jit(solution)/shard_map/ppermute | solution.py:30
  102.2 11.3 %collective-permute-start.28 = (bf16[768,256]{1,0:T(8,128)(2,1)}, bf16[768,256]{1,0:T(8,128)(2,1)}, u32[]{:S(2)}, u32[]{:S(2)}) collective-permute-start(bf16[768,256]{1,0:T(8,128)(2,1)} %convolution_convert_fusion.4), channel_id=1, source_target_pairs={{0,1},{1,0},{2,3},{3,2},{4,5},{5,4},{6,7},{7,6},{8,9},{9,8},{10,11... | collective-permute-start | bytes 1179656 | tf_op jit(solution)/shard_map/ppermute | solution.py:34
  104.4 13.5 %collective-permute-start.30 = (bf16[384,1536]{1,0:T(8,128)(2,1)}, bf16[384,1536]{1,0:T(8,128)(2,1)}, u32[]{:S(2)}, u32[]{:S(2)}) collective-permute-start(bf16[384,1536]{1,0:T(8,128)(2,1)} %convolution_convert_fusion.1), channel_id=1, source_target_pairs={{0,2},{2,0},{4,6},{6,4},{1,3},{3,1},{5,7},{7,5},{8,10},{10,8},{12,... | collective-permute-start | bytes 3538952 | tf_op jit(solution)/shard_map/ppermute | solution.py:30
  122.7 10.2 %collective-permute-start.31 = (bf16[768,256]{1,0:T(8,128)(2,1)S(1)}, bf16[768,256]{1,0:T(8,128)(2,1)S(1)}, u32[]{:S(2)}, u32[]{:S(2)}) collective-permute-start(bf16[768,256]{1,0:T(8,128)(2,1)S(1)} %fusion.116), channel_id=1, source_target_pairs={{0,1},{1,0},{2,3},{3,2},{4,5},{5,4},{6,7},{7,6},{8,9},{9,8},{10,11... | collective-permute-start | bytes 1179656 | tf_op jit(solution)/shard_map/ppermute | solution.py:34
  126.1 29.5 %collective-permute-start.35 = (bf16[192,1536]{1,0:T(8,128)(2,1)S(1)}, bf16[192,1536]{1,0:T(8,128)(2,1)S(1)}, u32[]{:S(2)}, u32[]{:S(2)}) collective-permute-start(bf16[192,1536]{1,0:T(8,128)(2,1)S(1)} %add_convert_fusion.3), channel_id=1, source_target_pairs={{0,4},{2,6},{4,0},{6,2},{1,5},{3,7},{5,1},{7,3},{8,12},{10,14},{12... | collective-permute-start | bytes 1769480 | tf_op jit(solution)/shard_map/ppermute | solution.py:30
  126.4 34.4 %collective-permute-start.36 = (bf16[192,1536]{1,0:T(8,128)(2,1)}, bf16[192,1536]{1,0:T(8,128)(2,1)}, u32[]{:S(2)}, u32[]{:S(2)}) collective-permute-start(bf16[192,1536]{1,0:T(8,128)(2,1)} %add_convert_fusion.2), channel_id=1, source_target_pairs={{0,4},{2,6},{4,0},{6,2},{1,5},{3,7},{5,1},{7,3},{8,12},{10,14},{12... | collective-permute-start | bytes 1769480 | tf_op jit(solution)/shard_map/ppermute | solution.py:30
  142.8 11.0 %collective-permute-start.34 = (bf16[192,256]{1,0:T(8,128)(2,1)S(1)}, bf16[192,256]{1,0:T(8,128)(2,1)S(1)}, u32[]{:S(2)}, u32[]{:S(2)}) collective-permute-start(bf16[192,256]{1,0:T(8,128)(2,1)S(1)} %get-tuple-element.99), channel_id=1, source_target_pairs={{0,6},{2,4},{5,3},{7,1},{8,14},{10,12},{13,11},{15,9},{16,22},{18,... | collective-permute-start | bytes 294920 | tf_op jit(solution)/shard_map/ppermute | solution.py:135
  144.1 10.8 %collective-permute-start.32 = (bf16[192,256]{1,0:T(8,128)(2,1)S(1)}, bf16[192,256]{1,0:T(8,128)(2,1)S(1)}, u32[]{:S(2)}, u32[]{:S(2)}) collective-permute-start(bf16[192,256]{1,0:T(8,128)(2,1)S(1)} %get-tuple-element.98), channel_id=1, source_target_pairs={{0,4},{2,6},{5,1},{7,3},{8,12},{10,14},{13,9},{15,11},{16,20},{18,... | collective-permute-start | bytes 294920 | tf_op jit(solution)/shard_map/ppermute | solution.py:135
  146.4 18.0 %collective-permute-start.37 = (bf16[384,384]{1,0:T(8,128)(2,1)}, bf16[384,384]{1,0:T(8,128)(2,1)}, u32[]{:S(2)}, u32[]{:S(2)}) collective-permute-start(bf16[384,384]{1,0:T(8,128)(2,1)} %convolution_convert_fusion.6), channel_id=1, source_target_pairs={{0,2},{2,0},{4,6},{6,4},{1,3},{3,1},{5,7},{7,5},{8,10},{10,8},{12,... | collective-permute-start | bytes 884744 | tf_op jit(solution)/shard_map/ppermute | solution.py:30
  158.5 100.1 %all-reduce.6.cloned.1.call-start = ((), (), s32[]{:S(2)}) async-start(), calls=%async_computation.1 | async-start | bytes 1474560 | tf_op jit(solution)/shard_map/psum | solution.py:284
  176.4 26.4 %collective-permute-start.39 = (bf16[768,256]{1,0:T(8,128)(2,1)S(1)}, bf16[768,256]{1,0:T(8,128)(2,1)}, u32[]{:S(2)}, u32[]{:S(2)}) collective-permute-start(bf16[768,256]{1,0:T(8,128)(2,1)S(1)} %convolution_convert_fusion.3), channel_id=1, source_target_pairs={{0,1},{1,0},{2,3},{3,2},{4,5},{5,4},{6,7},{7,6},{8,9},{9,8},{10,11... | collective-permute-start | bytes 1179656 | tf_op jit(solution)/shard_map/ppermute | solution.py:34
  179.9 42.3 %collective-permute-start.51 = (bf16[384,1152]{1,0:T(8,128)(2,1)}, bf16[384,1152]{1,0:T(8,128)(2,1)}, u32[]{:S(2)}, u32[]{:S(2)}) collective-permute-start(bf16[384,1152]{1,0:T(8,128)(2,1)} %convolution_convert_fusion), channel_id=1, source_target_pairs={{0,2},{2,0},{4,6},{6,4},{1,3},{3,1},{5,7},{7,5},{8,10},{10,8},{12,... | collective-permute-start | bytes 2654216 | tf_op jit(solution)/shard_map/ppermute | solution.py:30
  209.1 48.6 %collective-permute-start.41 = (bf16[192,256]{1,0:T(8,128)(2,1)}, bf16[192,256]{1,0:T(8,128)(2,1)S(1)}, u32[]{:S(2)}, u32[]{:S(2)}) collective-permute-start(bf16[192,256]{1,0:T(8,128)(2,1)} %get-tuple-element.97), channel_id=1, source_target_pairs={{0,2},{2,0},{5,7},{7,5},{8,10},{10,8},{13,15},{15,13},{16,18},{18,... | collective-permute-start | bytes 294920 | tf_op jit(solution)/shard_map/ppermute | solution.py:135
  214.5 43.2 %collective-permute-start.42 = (bf16[192,256]{1,0:T(8,128)(2,1)}, bf16[192,256]{1,0:T(8,128)(2,1)}, u32[]{:S(2)}, u32[]{:S(2)}) collective-permute-start(bf16[192,256]{1,0:T(8,128)(2,1)} %get-tuple-element.96), channel_id=1, source_target_pairs={{0,6},{2,4},{5,3},{7,1},{8,14},{10,12},{13,11},{15,9},{16,22},{18,... | collective-permute-start | bytes 294920 | tf_op jit(solution)/shard_map/ppermute | solution.py:135
  217.5 40.3 %collective-permute-start.40 = (bf16[192,256]{1,0:T(8,128)(2,1)S(1)}, bf16[192,256]{1,0:T(8,128)(2,1)}, u32[]{:S(2)}, u32[]{:S(2)}) collective-permute-start(bf16[192,256]{1,0:T(8,128)(2,1)S(1)} %get-tuple-element.95), channel_id=1, source_target_pairs={{0,4},{2,6},{5,1},{7,3},{8,12},{10,14},{13,9},{15,11},{16,20},{18,... | collective-permute-start | bytes 294920 | tf_op jit(solution)/shard_map/ppermute | solution.py:135
  223.6 11.6 %collective-permute-start.52 = (bf16[192,1152]{1,0:T(8,128)(2,1)S(1)}, bf16[192,1152]{1,0:T(8,128)(2,1)S(1)}, u32[]{:S(2)}, u32[]{:S(2)}) collective-permute-start(bf16[192,1152]{1,0:T(8,128)(2,1)S(1)} %add_convert_fusion.7), channel_id=1, source_target_pairs={{0,4},{2,6},{4,0},{6,2},{1,5},{3,7},{5,1},{7,3},{8,12},{10,14},{12... | collective-permute-start | bytes 1327112 | tf_op jit(solution)/shard_map/ppermute | solution.py:30
  223.8 15.4 %collective-permute-start.50 = (bf16[8,2496]{1,0:T(8,128)(2,1)S(1)}, bf16[8,2496]{1,0:T(8,128)(2,1)S(1)}, u32[]{:S(2)}, u32[]{:S(2)}) collective-permute-start(bf16[8,2496]{1,0:T(8,128)(2,1)S(1)} %pad_maximum_fusion.7), channel_id=1, source_target_pairs={{0,16},{8,24},{16,0},{24,8},{1,17},{9,25},{17,1},{25,9},{2,18},{10... | collective-permute-start | bytes 119816 | tf_op jit(solution)/shard_map/ppermute | solution.py:100
  236.4 16.3 %collective-permute-start.53 = (bf16[192,1152]{1,0:T(8,128)(2,1)S(1)}, bf16[192,1152]{1,0:T(8,128)(2,1)S(1)}, u32[]{:S(2)}, u32[]{:S(2)}) collective-permute-start(bf16[192,1152]{1,0:T(8,128)(2,1)S(1)} %add_convert_fusion.6), channel_id=1, source_target_pairs={{0,8},{24,16},{1,9},{25,17},{2,10},{26,18},{3,11},{27,19},{4,12},{... | collective-permute-start | bytes 1327112 | tf_op jit(solution)/shard_map/ppermute | solution.py:73
  254.8 24.6 %collective-permute-start.55 = (bf16[192,1152]{1,0:T(8,128)(2,1)S(1)}, bf16[192,1152]{1,0:T(8,128)(2,1)S(1)}, u32[]{:S(2)}, u32[]{:S(2)}) collective-permute-start(bf16[192,1152]{1,0:T(8,128)(2,1)S(1)} %add_convert_fusion.4), channel_id=1, source_target_pairs={{8,0},{16,24},{9,1},{17,25},{10,2},{18,26},{11,3},{19,27},{12,4},{... | collective-permute-start | bytes 1327112 | tf_op jit(solution)/shard_map/ppermute | solution.py:91
  (120 other events, 792.1 us)
Sparse Core Ops, SparseCore 0:
  158.6 41.7 all-reduce.3
  203.4 44.7 all-reduce.5

commit v4 on v3

--- a/solution.py
+++ b/solution.py
@@ -111,9 +111,12 @@
     return sum(jnp.where(lane == i, column, 0.0) for i, column in enumerate(columns))
 
 
-def latent_of(local, row, col):
-    per_col = local.shape[1] // LEN
-    both = jnp.concatenate([local, swap_col(local)], axis=1)
+def both_cols(local):
+    return jnp.concatenate([local, swap_col(local)], axis=1)
+
+
+def latent_of(both, row, col):
+    per_col = both.shape[1] // LEN // lax.axis_size("col")
 
     def block(latent):
         place = jnp.where(latent // per_col == col, 0, per_col) + latent % per_col
@@ -139,9 +142,7 @@
     first = jnp.where(here, got[0], got[2])
     second = jnp.where(here, got[1], got[3])
     even = row % 2 == 0
-    return jnp.concatenate(
-        [jnp.where(even, first, second), jnp.where(even, second, first)], axis=1
-    )
+    return jnp.where(even, first, second), jnp.where(even, second, first)
 
 
 def normalize(values):
@@ -194,6 +195,9 @@
     mod_flat = w_mod.reshape(-1, w_mod.shape[2])
     terms = contract(cond_rows, mod_flat, 1, 1)
     terms = terms + swap_col(terms)
+    terms, far_joined, both_tokens, both_cot = lax.optimization_barrier(
+        (terms, far_joined, both_cols(tokens), both_cols(cotangent))
+    )
     terms = terms.reshape(rows, 6, width_row) + b_mod.astype(F32)[None]
     extra = jnp.stack([b_out, b_down]).astype(F32)
     packed = jnp.concatenate([terms, jnp.broadcast_to(extra[None], (rows, 2, width_row))], axis=1)
@@ -201,16 +205,10 @@
         [packed[0]] + [swap_row(packed[i], k) for i, k in enumerate(ORDER) if k], axis=1
     )
     columns = vectors.T
-    local_tokens = latent_of(tokens, row, col)
-    held = (local_tokens, far_joined)
-    far_out = swap_row(after(w_out, held), 2)
-    far_up = swap_row(after(w_up, far_out), 2)
-    far_down = swap_row(after(w_down, far_up), 2)
-    cot = latent_of(after(cotangent, far_up), row, col).astype(F32)
+    local_tokens = latent_of(both_tokens, row, col)
+    far_out = swap_row(after(w_out, far_joined), 2)
+    far_up = swap_row(after(w_up, far_joined), 2)
     w_joined = gather_row(w_joined_own, far_joined)
-    w_out_all = gather_row(w_out, far_out)
-    w_up_all = gather_row(w_up, far_up)
-    w_down_all = gather_row(w_down, far_down)
     shift_attn, scale_attn, gate_attn, shift_mlp, scale_mlp, gate_mlp, bias_out, bias_down = (
         columns[:, i : i + 1] for i in range(8)
     )
@@ -232,7 +230,14 @@
     full_probs = exponent / jnp.sum(exponent, axis=-1, keepdims=True)
     probabilities = full_probs.astype(BF16)
     attended = contract_heads(values, probabilities, 2, 2).reshape(width_col, LEN).astype(BF16)
+    attended, far_out, far_up = lax.optimization_barrier((attended, far_out, far_up))
+    w_out_all = gather_row(w_out, far_out)
+    w_up_all = gather_row(w_up, far_up)
+    far_down = swap_row(after(w_down, far_up), 2)
+    cot = latent_of(after(both_cot, far_up), row, col).astype(F32)
     projected = pair_sum(contract(w_out_all, attended, 1, 0)) + bias_out
+    projected, far_down, cot = lax.optimization_barrier((projected, far_down, cot))
+    w_down_all = gather_row(w_down, far_down)
     residual = x + gate_attn * projected
 
     normed_mlp, inverse_mlp = normalize(residual)
@@ -257,7 +262,7 @@
 
     down_partial = after(contract(w_down_all, activated, 1, 0), grad_hidden)
     downward = pair_sum(down_partial) + bias_down
-    output = spread_out((residual + gate_mlp * downward).astype(BF16), row, col)
+    output = (residual + gate_mlp * downward).astype(BF16)
     grad_gate_mlp = jnp.sum(cot * downward, axis=1, keepdims=True)
 
     grad_gate_attn = jnp.sum(grad_residual * projected, axis=1, keepdims=True)
@@ -268,11 +273,13 @@
     grad_probs = contract_heads(grad_heads, values, 1, 1)
     grad_values = contract_heads(grad_heads, probabilities, 2, 1)
     grad_probs, sum_down = lax.optimization_barrier((grad_probs, sum_down))
-    total_down = lax.psum(sum_down, "dp")
-    grad_w_down = total_down.astype(F32)
+    first_down = dp_first(sum_down)
     sum_up = far_sum(near_up)
     inner = jnp.sum(full_probs * grad_probs, axis=-1, keepdims=True)
     grad_scores = (full_probs * (grad_probs - inner)).astype(BF16)
+    grad_scores, first_down, sum_up = lax.optimization_barrier((grad_scores, first_down, sum_up))
+    total_down = dp_second(first_down)
+    first_up = dp_first(sum_up)
     grad_queries = contract_heads(keys, grad_scores, 2, 2) * scale_factor
     grad_keys = contract_heads(queries, grad_scores, 2, 1) * scale_factor
     grad_joined = jnp.concatenate(
@@ -280,18 +287,24 @@
         axis=0,
     )
     sum_out = far_sum(near_out)
-    grad_joined, sum_up, sum_out = lax.optimization_barrier((grad_joined, sum_up, sum_out))
-    grad_w_up, grad_w_out = (t.astype(F32) for t in lax.psum((after(sum_up, total_down), sum_out), "dp"))
     grad_hidden = pair_sum(contract(w_joined, grad_joined, 1, 0))
     near_joined = near_sum(hidden_attn, grad_joined)
     grad_b_joined = jnp.sum(grad_joined.astype(F32), axis=1, keepdims=True)
+    grad_hidden, total_down, first_up, sum_out = lax.optimization_barrier(
+        (grad_hidden, total_down, first_up, sum_out)
+    )
     sum_joined = far_sum(near_joined)
+    grad_w_down = dp_third(total_down)
+    total_up = dp_second(first_up)
+    first_out = dp_first(sum_out)
     grad_scale_attn = jnp.sum(grad_hidden * normed_attn, axis=1, keepdims=True)
     grad_shift_attn = jnp.sum(grad_hidden, axis=1, keepdims=True)
     grad_x = grad_residual + normalize_back(
         grad_hidden * (1.0 + scale_attn), normed_attn, inverse_attn
     )
-    grad_tokens = spread_out(grad_x.astype(BF16), row, col)
+    spread = spread_out(jnp.concatenate([output, grad_x.astype(BF16)], axis=1), row, col)
+    output = jnp.concatenate([part[:, :LEN] for part in spread], axis=1)
+    grad_tokens = jnp.concatenate([part[:, LEN:] for part in spread], axis=1)
 
     own_vectors = beside(
         [
@@ -341,7 +354,12 @@
     bias_sums = jnp.sum(bias_parts.reshape(-1, rows, bias_parts.shape[1]), axis=0).reshape(-1)
     hidden_width = grad_b_up.shape[0]
 
-    grad_w_joined = dp_third(dp_second(dp_first(sum_joined)))
+    first_joined = dp_first(sum_joined)
+    total_out = dp_second(first_out)
+    grad_w_up = dp_third(total_up)
+    total_joined = dp_second(first_joined)
+    grad_w_out = dp_third(total_out)
+    grad_w_joined = dp_third(total_joined)
     return (
         output,
         grad_tokens.astype(F32),

time: 288 us -> 266 us (0.924)
  waiting for transfers between devices: 130 us -> 91.7 us
  starting transfers between devices: 53.7 us -> 77.5 us
  between operations: 15.9 us -> 2.52 us
  matrix products: 34.4 us -> 39.2 us
    ppermute x1 -> x4, starting transfers between devices: 2.86 us -> 23.2 us  [dp_first(): lax.ppermute(value, 'dp', dp_pairs()[0]).astype(F32)]
    psum x2 -> x0, waiting for transfers between devices: 20.1 us -> none  [the longest x1 20.1 us: body(): total_down = lax.psum(sum_down, 'dp')]
    ppermute x38, waiting for transfers between devices: 55.6 us -> 38.6 us  [swap_row(): return lax.ppermute(value, 'row', [(i, i ^ offset) for i in range(size)])]
    ppermute x1 -> x4, waiting for transfers between devices: 17 us -> 29 us  [dp_third(): back = lax.ppermute(total, 'dp', dp_pairs()[2])]
    ppermute x6 -> x3, waiting for transfers between devices: 8.02 us -> 0.01 us  [spread_out(): lax.ppermute(full[place * width:(place + 1) * width], ('row', 'col'), pairs)]
    convert_element_type x5 -> x2, other arithmetic: 7.92 us -> 0.33 us  [the longest x1 0.28 us: body(): grad_x.astype(BF16)]
    ppermute x7, waiting for transfers between devices: 17.7 us -> 11.8 us  [swap_col(): return lax.ppermute(value, 'col', [(0, 1), (1, 0)])]
    ppermute x6 -> x3, starting transfers between devices: 11.7 us -> 7.04 us  [spread_out(): lax.ppermute(full[place * width:(place + 1) * width], ('row', 'col'), pairs)]
  transfers between devices with their start and end apart: 58 -> 62, of which waited for: 24 -> 23; matrix products, arithmetic and copies ran while one was open for 27% -> 30% of each run, Pallas kernels for 0% -> 0%
where the time goes in v4:
time: 266 us; the launch traced here: 264 us
  waiting for transfers between devices  91.7 us (34%)
  starting transfers between devices  77.5 us (29%)
  matrix products  39.2 us (15%)
  other arithmetic  33.9 us (13%)
  local copies, waits for them, and re-layouts  19.3 us (7%)
    ppermute x38, waiting for transfers between devices, swap_row(): return lax.ppermute(value, 'row', [(i, i ^ offset) for i in range(size)])  38.6 us
    dot_general x23, matrix products, contract(): lax.dot_general(left, right, (((left_dim,), (right_dim,)), ((), ())), pre...  33.5 us
    ppermute x4, waiting for transfers between devices, dp_third(): back = lax.ppermute(total, 'dp', dp_pairs()[2])  29 us
    ppermute x38, starting transfers between devices, swap_row(): return lax.ppermute(value, 'row', [(i, i ^ offset) for i in range(size)])  25.2 us
    ppermute x4, starting transfers between devices, dp_first(): lax.ppermute(value, 'dp', dp_pairs()[0]).astype(F32)  23.2 us
    ppermute x7, waiting for transfers between devices, swap_col(): return lax.ppermute(value, 'col', [(0, 1), (1, 0)])  11.8 us
    ppermute x4, waiting for transfers between devices, dp_first(): lax.ppermute(value, 'dp', dp_pairs()[0]).astype(F32)  10.5 us
    unnamed x197, local copies, waits for them, and re-layouts  9.95 us
  transfers between devices with their start and end apart: 62, of which 23 were waited for; matrix products, arithmetic and copies ran while one was open for 30% of the time, Pallas kernels for 0%

profile of v4, /device:TPU:0, one launch (start us, length us, event | category | flops | bytes accessed | tf_op | source)
XLA Modules:
  0.0 264.1 jit_solution(3590266051052752632)
XLA Ops:
  1.5 2.5 collective-permute-start.2
  4.7 2.0 collective-permute-start.5
  9.4 1.9 constant_dynamic-update-slice_fusion.10
  11.4 2.0 constant_dynamic-update-slice_fusion.14
  14.3 2.0 collective-permute-start.4
  19.4 2.3 collective-permute-done.3
  21.9 5.0 %collective-permute-done.4 = bf16[192,1152]{1,0:T(8,128)(2,1)} collective-permute-done((bf16[192,1152]{1,0:T(8,128)(2,1)S(1)}, bf16[192,1152]{1,0:T(8,128)(2,1)}, u32[]{:S(2)}, u32[]{:S(2)}) %collective-permute-start.4) | collective-permute-done | bytes 442400 | tf_op jit(solution)/shard_map/ppermute | solution.py:30
  46.0 9.4 %collective-permute-done.16 = bf16[192,1536]{1,0:T(8,128)(2,1)S(1)} collective-permute-done((bf16[192,1536]{1,0:T(8,128)(2,1)}, bf16[192,1536]{1,0:T(8,128)(2,1)S(1)}, u32[]{:S(2)}, u32[]{:S(2)}) %collective-permute-start.16) | collective-permute-done | bytes 589856 | tf_op jit(solution)/shard_map/ppermute | solution.py:30
  64.8 9.4 %collective-permute-done.23 = bf16[192,256]{1,0:T(8,128)(2,1)S(1)} collective-permute-done((bf16[192,256]{1,0:T(8,128)(2,1)S(1)}, bf16[192,256]{1,0:T(8,128)(2,1)S(1)}, u32[]{:S(2)}, u32[]{:S(2)}) %collective-permute-start.23) | collective-permute-done | bytes 98336 | tf_op jit(solution)/shard_map/ppermute | solution.py:30
  82.1 2.3 fusion.105
  90.8 2.6 %fusion.118 = bf16[768,256]{1,0:T(8,128)(2,1)S(1)} fusion(bf16[768,1536]{1,0:T(8,128)(2,1)} %copy-done.43, bf16[1536,256]{0,1:T(8,128)(2,1)} %copy-done.3), kind=kOutput, calls=%fused_computation.276 | convolution fusion | flops 603979776 | bytes 3538944 | tf_op jit(solution)/shard_map/dot_general | solution.py:17
  93.4 3.9 %collective-permute-done.28 = bf16[768,256]{1,0:T(8,128)(2,1)} collective-permute-done((bf16[768,256]{1,0:T(8,128)(2,1)}, bf16[768,256]{1,0:T(8,128)(2,1)}, u32[]{:S(2)}, u32[]{:S(2)}) %collective-permute-start.28) | collective-permute-done | bytes 393248 | tf_op jit(solution)/shard_map/ppermute | solution.py:34
  101.5 2.4 convert_add_fusion.1
  103.9 2.2 add_convert_fusion.6
  110.7 5.6 %collective-permute-done.31 = bf16[768,256]{1,0:T(8,128)(2,1)S(1)} collective-permute-done((bf16[768,256]{1,0:T(8,128)(2,1)S(1)}, bf16[768,256]{1,0:T(8,128)(2,1)S(1)}, u32[]{:S(2)}, u32[]{:S(2)}) %collective-permute-start.31) | collective-permute-done | bytes 393248 | tf_op jit(solution)/shard_map/ppermute | solution.py:34
  116.3 2.0 multiply_reduce_fusion.1
  125.6 3.6 %collective-permute-start.33 = (bf16[192,1536]{1,0:T(8,128)(2,1)S(1)}, bf16[192,1536]{1,0:T(8,128)(2,1)S(1)}, u32[]{:S(2)}, u32[]{:S(2)}) collective-permute-start(bf16[192,1536]{1,0:T(8,128)(2,1)S(1)} %add_convert_fusion.5), channel_id=1, source_target_pairs={{0,8},{24,16},{1,9},{25,17},{2,10},{26,18},{3,11},{27,19},{4,12},{... | collective-permute-start | bytes 1769480 | tf_op jit(solution)/shard_map/ppermute | solution.py:73
  129.2 5.2 %collective-permute-done.34 = bf16[192,1536]{1,0:T(8,128)(2,1)} collective-permute-done((bf16[192,1536]{1,0:T(8,128)(2,1)}, bf16[192,1536]{1,0:T(8,128)(2,1)}, u32[]{:S(2)}, u32[]{:S(2)}) %collective-permute-start.34) | collective-permute-done | bytes 589856 | tf_op jit(solution)/shard_map/ppermute | solution.py:30
  134.5 2.3 add_convert_fusion.3
  139.7 2.5 multiply_convert_fusion
  147.9 2.4 convolution_convert_fusion.3
  152.4 5.5 %collective-permute-start.37 = (bf16[192,1536]{1,0:T(8,128)(2,1)}, bf16[192,1536]{1,0:T(8,128)(2,1)S(1)}, u32[]{:S(2)}, u32[]{:S(2)}) collective-permute-start(bf16[192,1536]{1,0:T(8,128)(2,1)} %add_convert_fusion.3), channel_id=1, source_target_pairs={{0,8},{24,16},{1,9},{25,17},{2,10},{26,18},{3,11},{27,19},{4,12},{... | collective-permute-start | bytes 1769480 | tf_op jit(solution)/shard_map/ppermute | solution.py:73
  161.9 5.5 %collective-permute-done.37 = bf16[192,1536]{1,0:T(8,128)(2,1)S(1)} collective-permute-done((bf16[192,1536]{1,0:T(8,128)(2,1)}, bf16[192,1536]{1,0:T(8,128)(2,1)S(1)}, u32[]{:S(2)}, u32[]{:S(2)}) %collective-permute-start.37) | collective-permute-done | bytes 589856 | tf_op jit(solution)/shard_map/ppermute | solution.py:73
  176.5 2.4 collective-permute-start.49
  182.0 3.2 %collective-permute-start.42 = (bf16[192,512]{1,0:T(8,128)(2,1)}, bf16[192,512]{1,0:T(8,128)(2,1)}, u32[]{:S(2)}, u32[]{:S(2)}) collective-permute-start(bf16[192,512]{1,0:T(8,128)(2,1)} %get-tuple-element.114), channel_id=1, source_target_pairs={{0,6},{2,4},{5,3},{7,1},{8,14},{10,12},{13,11},{15,9},{16,22},{18,... | collective-permute-start | bytes 589832 | tf_op jit(solution)/shard_map/ppermute | solution.py:138
  185.1 2.0 collective-permute-start.40
  192.0 4.6 %collective-permute-start.56 = (bf16[192,384]{1,0:T(8,128)(2,1)S(1)}, bf16[192,384]{1,0:T(8,128)(2,1)}, u32[]{:S(2)}, u32[]{:S(2)}) collective-permute-start(bf16[192,384]{1,0:T(8,128)(2,1)S(1)} %copy-done.36), channel_id=1, source_target_pairs={{0,8},{24,16},{1,9},{25,17},{2,10},{26,18},{3,11},{27,19},{4,12},{... | collective-permute-start | bytes 442376 | tf_op jit(solution)/shard_map/ppermute | solution.py:73
  211.8 12.9 %collective-permute-done.58 = bf16[192,384]{1,0:T(8,128)(2,1)S(1)} collective-permute-done((bf16[192,384]{1,0:T(8,128)(2,1)S(1)}, bf16[192,384]{1,0:T(8,128)(2,1)S(1)}, u32[]{:S(2)}, u32[]{:S(2)}) %collective-permute-start.58) | collective-permute-done | bytes 147488 | tf_op jit(solution)/shard_map/ppermute | solution.py:91
  226.7 9.5 %collective-permute-start.53 = (bf16[192,1152]{1,0:T(8,128)(2,1)S(1)}, bf16[192,1152]{1,0:T(8,128)(2,1)S(1)}, u32[]{:S(2)}, u32[]{:S(2)}) collective-permute-start(bf16[192,1152]{1,0:T(8,128)(2,1)S(1)} %add_convert_fusion.10), channel_id=1, source_target_pairs={{0,8},{24,16},{1,9},{25,17},{2,10},{26,18},{3,11},{27,19},{4,12},{... | collective-permute-start | bytes 1327112 | tf_op jit(solution)/shard_map/ppermute | solution.py:73
  237.6 5.0 %collective-permute-done.53 = bf16[192,1152]{1,0:T(8,128)(2,1)S(1)} collective-permute-done((bf16[192,1152]{1,0:T(8,128)(2,1)S(1)}, bf16[192,1152]{1,0:T(8,128)(2,1)S(1)}, u32[]{:S(2)}, u32[]{:S(2)}) %collective-permute-start.53) | collective-permute-done | bytes 442400 | tf_op jit(solution)/shard_map/ppermute | solution.py:73
  246.0 4.1 %collective-permute-done.60 = bf16[192,1536]{1,0:T(8,128)(2,1)S(1)} collective-permute-done((bf16[192,1536]{1,0:T(8,128)(2,1)S(1)}, bf16[192,1536]{1,0:T(8,128)(2,1)S(1)}, u32[]{:S(2)}, u32[]{:S(2)}) %collective-permute-start.60) | collective-permute-done | bytes 589856 | tf_op jit(solution)/shard_map/ppermute | solution.py:91
  251.2 11.9 %collective-permute-done.55 = bf16[192,1152]{1,0:T(8,128)(2,1)S(1)} collective-permute-done((bf16[192,1152]{1,0:T(8,128)(2,1)S(1)}, bf16[192,1152]{1,0:T(8,128)(2,1)S(1)}, u32[]{:S(2)}, u32[]{:S(2)}) %collective-permute-start.55) | collective-permute-done | bytes 442400 | tf_op jit(solution)/shard_map/ppermute | solution.py:91
  (430 shorter events, 121.2 us)
Async XLA Ops:
  1.5 12.4 %collective-permute-start.2 = (bf16[1,384]{1,0:T(2,128)(2,1)S(1)}, bf16[1,384]{1,0:T(2,128)(2,1)S(1)}, u32[]{:S(2)}, u32[]{:S(2)}) collective-permute-start(bf16[1,384]{1,0:T(2,128)(2,1)S(1)} %multiply_convert_fusion.4), channel_id=1, source_target_pairs={{0,6},{2,4},{4,2},{6,0},{1,7},{3,5},{5,3},{7,1},{8,14},{10,12},{12... | collective-permute-start | bytes 2312 | tf_op jit(solution)/shard_map/ppermute | solution.py:30
  4.7 17.1 %collective-permute-start.5 = (bf16[192,512]{1,0:T(8,128)(2,1)}, bf16[192,512]{1,0:T(8,128)(2,1)S(1)}, u32[]{:S(2)}, u32[]{:S(2)}) collective-permute-start(bf16[192,512]{1,0:T(8,128)(2,1)} %param.16), channel_id=1, source_target_pairs={{0,1},{1,0},{2,3},{3,2},{4,5},{5,4},{6,7},{7,6},{8,9},{9,8},{10,11... | collective-permute-start | bytes 589832 | tf_op jit(solution)/shard_map/ppermute | solution.py:34
  6.7 51.9 %collective-permute-start.17 = (bf16[192,384]{1,0:T(8,128)(2,1)}, bf16[192,384]{1,0:T(8,128)(2,1)}, u32[]{:S(2)}, u32[]{:S(2)}) collective-permute-start(bf16[192,384]{1,0:T(8,128)(2,1)} %param.25), channel_id=1, source_target_pairs={{0,2},{2,0},{4,6},{6,4},{1,3},{3,1},{5,7},{7,5},{8,10},{10,8},{12,... | collective-permute-start | bytes 442376 | tf_op jit(solution)/shard_map/ppermute | solution.py:30
  14.3 12.7 %collective-permute-start.4 = (bf16[192,1152]{1,0:T(8,128)(2,1)S(1)}, bf16[192,1152]{1,0:T(8,128)(2,1)}, u32[]{:S(2)}, u32[]{:S(2)}) collective-permute-start(bf16[192,1152]{1,0:T(8,128)(2,1)S(1)} %constant_dynamic-update-slice_fusion), channel_id=1, source_target_pairs={{0,4},{2,6},{4,0},{6,2},{1,5},{3,7},{5,1},{7,3},{8,12},{10,14},{12... | collective-permute-start | bytes 1327112 | tf_op jit(solution)/shard_map/ppermute | solution.py:30
  21.7 40.2 %collective-permute-start.26 = (bf16[192,1536]{1,0:T(8,128)(2,1)}, bf16[192,1536]{1,0:T(8,128)(2,1)}, u32[]{:S(2)}, u32[]{:S(2)}) collective-permute-start(bf16[192,1536]{1,0:T(8,128)(2,1)} %param.27), channel_id=1, source_target_pairs={{0,2},{2,0},{4,6},{6,4},{1,3},{3,1},{5,7},{7,5},{8,10},{10,8},{12,... | collective-permute-start | bytes 1769480 | tf_op jit(solution)/shard_map/ppermute | solution.py:30
  39.3 16.1 %collective-permute-start.16 = (bf16[192,1536]{1,0:T(8,128)(2,1)}, bf16[192,1536]{1,0:T(8,128)(2,1)S(1)}, u32[]{:S(2)}, u32[]{:S(2)}) collective-permute-start(bf16[192,1536]{1,0:T(8,128)(2,1)} %param.27), channel_id=1, source_target_pairs={{0,4},{2,6},{4,0},{6,2},{1,5},{3,7},{5,1},{7,3},{8,12},{10,14},{12... | collective-permute-start | bytes 1769480 | tf_op jit(solution)/shard_map/ppermute | solution.py:30
  56.6 20.1 %collective-permute-start.20 = (bf16[192,1536]{1,0:T(8,128)(2,1)S(1)}, bf16[192,1536]{1,0:T(8,128)(2,1)S(1)}, u32[]{:S(2)}, u32[]{:S(2)}) collective-permute-start(bf16[192,1536]{1,0:T(8,128)(2,1)S(1)} %copy-done.33), channel_id=1, source_target_pairs={{0,4},{2,6},{4,0},{6,2},{1,5},{3,7},{5,1},{7,3},{8,12},{10,14},{12... | collective-permute-start | bytes 1769480 | tf_op jit(solution)/shard_map/ppermute | solution.py:30
  58.4 15.7 %collective-permute-start.23 = (bf16[192,256]{1,0:T(8,128)(2,1)S(1)}, bf16[192,256]{1,0:T(8,128)(2,1)S(1)}, u32[]{:S(2)}, u32[]{:S(2)}) collective-permute-start(bf16[192,256]{1,0:T(8,128)(2,1)S(1)} %get-tuple-element.117), channel_id=1, source_target_pairs={{0,6},{2,4},{4,2},{6,0},{1,7},{3,5},{5,3},{7,1},{8,14},{10,12},{12... | collective-permute-start | bytes 294920 | tf_op jit(solution)/shard_map/ppermute | solution.py:30
  58.5 16.2 %collective-permute-start.22 = (bf16[192,256]{1,0:T(8,128)(2,1)S(1)}, bf16[192,256]{1,0:T(8,128)(2,1)S(1)}, u32[]{:S(2)}, u32[]{:S(2)}) collective-permute-start(bf16[192,256]{1,0:T(8,128)(2,1)S(1)} %get-tuple-element.118), channel_id=1, source_target_pairs={{0,2},{2,0},{4,6},{6,4},{1,3},{3,1},{5,7},{7,5},{8,10},{10,8},{12,... | collective-permute-start | bytes 294920 | tf_op jit(solution)/shard_map/ppermute | solution.py:30
  60.3 16.2 %collective-permute-start.19 = (bf16[768,256]{1,0:T(8,128)(2,1)S(1)}, bf16[768,256]{1,0:T(8,128)(2,1)S(1)}, u32[]{:S(2)}, u32[]{:S(2)}) collective-permute-start(bf16[768,256]{1,0:T(8,128)(2,1)S(1)} %convolution_convert_fusion.5), channel_id=1, source_target_pairs={{0,1},{1,0},{2,3},{3,2},{4,5},{5,4},{6,7},{7,6},{8,9},{9,8},{10,11... | collective-permute-start | bytes 1179656 | tf_op jit(solution)/shard_map/ppermute | solution.py:34
  61.9 14.5 %collective-permute-start.21 = (bf16[192,256]{1,0:T(8,128)(2,1)S(1)}, bf16[192,256]{1,0:T(8,128)(2,1)S(1)}, u32[]{:S(2)}, u32[]{:S(2)}) collective-permute-start(bf16[192,256]{1,0:T(8,128)(2,1)S(1)} %get-tuple-element.119), channel_id=1, source_target_pairs={{0,4},{2,6},{4,0},{6,2},{1,5},{3,7},{5,1},{7,3},{8,12},{10,14},{12... | collective-permute-start | bytes 294920 | tf_op jit(solution)/shard_map/ppermute | solution.py:30
  81.4 17.1 %collective-permute-start.29 = (bf16[384,1536]{1,0:T(8,128)(2,1)}, bf16[384,1536]{1,0:T(8,128)(2,1)}, u32[]{:S(2)}, u32[]{:S(2)}) collective-permute-start(bf16[384,1536]{1,0:T(8,128)(2,1)} %convolution_convert_fusion.2), channel_id=1, source_target_pairs={{0,2},{2,0},{4,6},{6,4},{1,3},{3,1},{5,7},{7,5},{8,10},{10,8},{12,... | collective-permute-start | bytes 3538952 | tf_op jit(solution)/shard_map/ppermute | solution.py:30
  85.9 11.4 %collective-permute-start.28 = (bf16[768,256]{1,0:T(8,128)(2,1)}, bf16[768,256]{1,0:T(8,128)(2,1)}, u32[]{:S(2)}, u32[]{:S(2)}) collective-permute-start(bf16[768,256]{1,0:T(8,128)(2,1)} %convolution_convert_fusion.4), channel_id=1, source_target_pairs={{0,1},{1,0},{2,3},{3,2},{4,5},{5,4},{6,7},{7,6},{8,9},{9,8},{10,11... | collective-permute-start | bytes 1179656 | tf_op jit(solution)/shard_map/ppermute | solution.py:34
  88.9 12.5 %collective-permute-start.30 = (bf16[384,1536]{1,0:T(8,128)(2,1)}, bf16[384,1536]{1,0:T(8,128)(2,1)}, u32[]{:S(2)}, u32[]{:S(2)}) collective-permute-start(bf16[384,1536]{1,0:T(8,128)(2,1)} %convolution_convert_fusion.1), channel_id=1, source_target_pairs={{0,2},{2,0},{4,6},{6,4},{1,3},{3,1},{5,7},{7,5},{8,10},{10,8},{12,... | collective-permute-start | bytes 3538952 | tf_op jit(solution)/shard_map/ppermute | solution.py:30
  106.1 10.2 %collective-permute-start.31 = (bf16[768,256]{1,0:T(8,128)(2,1)S(1)}, bf16[768,256]{1,0:T(8,128)(2,1)S(1)}, u32[]{:S(2)}, u32[]{:S(2)}) collective-permute-start(bf16[768,256]{1,0:T(8,128)(2,1)S(1)} %fusion.118), channel_id=1, source_target_pairs={{0,1},{1,0},{2,3},{3,2},{4,5},{5,4},{6,7},{7,6},{8,9},{9,8},{10,11... | collective-permute-start | bytes 1179656 | tf_op jit(solution)/shard_map/ppermute | solution.py:34
  107.6 16.3 %collective-permute-start.32 = (bf16[192,1536]{1,0:T(8,128)(2,1)S(1)}, bf16[192,1536]{1,0:T(8,128)(2,1)S(1)}, u32[]{:S(2)}, u32[]{:S(2)}) collective-permute-start(bf16[192,1536]{1,0:T(8,128)(2,1)S(1)} %add_convert_fusion.7), channel_id=1, source_target_pairs={{0,4},{2,6},{4,0},{6,2},{1,5},{3,7},{5,1},{7,3},{8,12},{10,14},{12... | collective-permute-start | bytes 1769480 | tf_op jit(solution)/shard_map/ppermute | solution.py:30
  109.3 25.2 %collective-permute-start.34 = (bf16[192,1536]{1,0:T(8,128)(2,1)}, bf16[192,1536]{1,0:T(8,128)(2,1)}, u32[]{:S(2)}, u32[]{:S(2)}) collective-permute-start(bf16[192,1536]{1,0:T(8,128)(2,1)} %add_convert_fusion.6), channel_id=1, source_target_pairs={{0,4},{2,6},{4,0},{6,2},{1,5},{3,7},{5,1},{7,3},{8,12},{10,14},{12... | collective-permute-start | bytes 1769480 | tf_op jit(solution)/shard_map/ppermute | solution.py:30
  122.4 14.5 %collective-permute-start.38 = (bf16[384,384]{1,0:T(8,128)(2,1)}, bf16[384,384]{1,0:T(8,128)(2,1)}, u32[]{:S(2)}, u32[]{:S(2)}) collective-permute-start(bf16[384,384]{1,0:T(8,128)(2,1)} %convolution_convert_fusion.6), channel_id=1, source_target_pairs={{0,2},{2,0},{4,6},{6,4},{1,3},{3,1},{5,7},{7,5},{8,10},{10,8},{12,... | collective-permute-start | bytes 884744 | tf_op jit(solution)/shard_map/ppermute | solution.py:30
  125.6 19.4 %collective-permute-start.33 = (bf16[192,1536]{1,0:T(8,128)(2,1)S(1)}, bf16[192,1536]{1,0:T(8,128)(2,1)S(1)}, u32[]{:S(2)}, u32[]{:S(2)}) collective-permute-start(bf16[192,1536]{1,0:T(8,128)(2,1)S(1)} %add_convert_fusion.5), channel_id=1, source_target_pairs={{0,8},{24,16},{1,9},{25,17},{2,10},{26,18},{3,11},{27,19},{4,12},{... | collective-permute-start | bytes 1769480 | tf_op jit(solution)/shard_map/ppermute | solution.py:73
  152.4 15.1 %collective-permute-start.37 = (bf16[192,1536]{1,0:T(8,128)(2,1)}, bf16[192,1536]{1,0:T(8,128)(2,1)S(1)}, u32[]{:S(2)}, u32[]{:S(2)}) collective-permute-start(bf16[192,1536]{1,0:T(8,128)(2,1)} %add_convert_fusion.3), channel_id=1, source_target_pairs={{0,8},{24,16},{1,9},{25,17},{2,10},{26,18},{3,11},{27,19},{4,12},{... | collective-permute-start | bytes 1769480 | tf_op jit(solution)/shard_map/ppermute | solution.py:73
  158.0 50.8 %collective-permute-start.51 = (bf16[384,1152]{1,0:T(8,128)(2,1)}, bf16[384,1152]{1,0:T(8,128)(2,1)}, u32[]{:S(2)}, u32[]{:S(2)}) collective-permute-start(bf16[384,1152]{1,0:T(8,128)(2,1)} %convolution_convert_fusion), channel_id=1, source_target_pairs={{0,2},{2,0},{4,6},{6,4},{1,3},{3,1},{5,7},{7,5},{8,10},{10,8},{12,... | collective-permute-start | bytes 2654216 | tf_op jit(solution)/shard_map/ppermute | solution.py:30
  172.9 31.1 %collective-permute-start.41 = (bf16[192,512]{1,0:T(8,128)(2,1)}, bf16[192,512]{1,0:T(8,128)(2,1)}, u32[]{:S(2)}, u32[]{:S(2)}) collective-permute-start(bf16[192,512]{1,0:T(8,128)(2,1)} %get-tuple-element.115), channel_id=1, source_target_pairs={{0,2},{2,0},{5,7},{7,5},{8,10},{10,8},{13,15},{15,13},{16,18},{18,... | collective-permute-start | bytes 589832 | tf_op jit(solution)/shard_map/ppermute | solution.py:138
  182.0 23.5 %collective-permute-start.42 = (bf16[192,512]{1,0:T(8,128)(2,1)}, bf16[192,512]{1,0:T(8,128)(2,1)}, u32[]{:S(2)}, u32[]{:S(2)}) collective-permute-start(bf16[192,512]{1,0:T(8,128)(2,1)} %get-tuple-element.114), channel_id=1, source_target_pairs={{0,6},{2,4},{5,3},{7,1},{8,14},{10,12},{13,11},{15,9},{16,22},{18,... | collective-permute-start | bytes 589832 | tf_op jit(solution)/shard_map/ppermute | solution.py:138
  185.1 21.0 %collective-permute-start.40 = (bf16[192,512]{1,0:T(8,128)(2,1)}, bf16[192,512]{1,0:T(8,128)(2,1)}, u32[]{:S(2)}, u32[]{:S(2)}) collective-permute-start(bf16[192,512]{1,0:T(8,128)(2,1)} %get-tuple-element.113), channel_id=1, source_target_pairs={{0,4},{2,6},{5,1},{7,3},{8,12},{10,14},{13,9},{15,11},{16,20},{18,... | collective-permute-start | bytes 589832 | tf_op jit(solution)/shard_map/ppermute | solution.py:138
  192.0 10.3 %collective-permute-start.56 = (bf16[192,384]{1,0:T(8,128)(2,1)S(1)}, bf16[192,384]{1,0:T(8,128)(2,1)}, u32[]{:S(2)}, u32[]{:S(2)}) collective-permute-start(bf16[192,384]{1,0:T(8,128)(2,1)S(1)} %copy-done.36), channel_id=1, source_target_pairs={{0,8},{24,16},{1,9},{25,17},{2,10},{26,18},{3,11},{27,19},{4,12},{... | collective-permute-start | bytes 442376 | tf_op jit(solution)/shard_map/ppermute | solution.py:73
  202.3 33.9 %collective-permute-start.59 = (bf16[192,1536]{1,0:T(8,128)(2,1)S(1)}, bf16[192,1536]{1,0:T(8,128)(2,1)S(1)}, u32[]{:S(2)}, u32[]{:S(2)}) collective-permute-start(bf16[192,1536]{1,0:T(8,128)(2,1)S(1)} %add_convert_fusion.1), channel_id=1, source_target_pairs={{8,16},{16,8},{9,17},{17,9},{10,18},{18,10},{11,19},{19,11},{12,20... | collective-permute-start | bytes 1769480 | tf_op jit(solution)/shard_map/ppermute | solution.py:78
  204.0 39.5 %collective-permute-start.61 = (bf16[192,1536]{1,0:T(8,128)(2,1)S(1)}, bf16[192,1536]{1,0:T(8,128)(2,1)S(1)}, u32[]{:S(2)}, u32[]{:S(2)}) collective-permute-start(bf16[192,1536]{1,0:T(8,128)(2,1)S(1)} %add_convert_fusion.2), channel_id=1, source_target_pairs={{8,0},{16,24},{9,1},{17,25},{10,2},{18,26},{11,3},{19,27},{12,4},{... | collective-permute-start | bytes 1769480 | tf_op jit(solution)/shard_map/ppermute | solution.py:91
  207.4 17.4 %collective-permute-start.58 = (bf16[192,384]{1,0:T(8,128)(2,1)S(1)}, bf16[192,384]{1,0:T(8,128)(2,1)S(1)}, u32[]{:S(2)}, u32[]{:S(2)}) collective-permute-start(bf16[192,384]{1,0:T(8,128)(2,1)S(1)} %add_convert_fusion.14), channel_id=1, source_target_pairs={{8,0},{16,24},{9,1},{17,25},{10,2},{18,26},{11,3},{19,27},{12,4},{... | collective-permute-start | bytes 442376 | tf_op jit(solution)/shard_map/ppermute | solution.py:91
  210.3 15.2 %collective-permute-start.52 = (bf16[192,1152]{1,0:T(8,128)(2,1)S(1)}, bf16[192,1152]{1,0:T(8,128)(2,1)S(1)}, u32[]{:S(2)}, u32[]{:S(2)}) collective-permute-start(bf16[192,1152]{1,0:T(8,128)(2,1)S(1)} %add_convert_fusion.11), channel_id=1, source_target_pairs={{0,4},{2,6},{4,0},{6,2},{1,5},{3,7},{5,1},{7,3},{8,12},{10,14},{12... | collective-permute-start | bytes 1327112 | tf_op jit(solution)/shard_map/ppermute | solution.py:30
  226.7 16.0 %collective-permute-start.53 = (bf16[192,1152]{1,0:T(8,128)(2,1)S(1)}, bf16[192,1152]{1,0:T(8,128)(2,1)S(1)}, u32[]{:S(2)}, u32[]{:S(2)}) collective-permute-start(bf16[192,1152]{1,0:T(8,128)(2,1)S(1)} %add_convert_fusion.10), channel_id=1, source_target_pairs={{0,8},{24,16},{1,9},{25,17},{2,10},{26,18},{3,11},{27,19},{4,12},{... | collective-permute-start | bytes 1327112 | tf_op jit(solution)/shard_map/ppermute | solution.py:73
  236.3 13.8 %collective-permute-start.60 = (bf16[192,1536]{1,0:T(8,128)(2,1)S(1)}, bf16[192,1536]{1,0:T(8,128)(2,1)S(1)}, u32[]{:S(2)}, u32[]{:S(2)}) collective-permute-start(bf16[192,1536]{1,0:T(8,128)(2,1)S(1)} %add_convert_fusion), channel_id=1, source_target_pairs={{8,0},{16,24},{9,1},{17,25},{10,2},{18,26},{11,3},{19,27},{12,4},{... | collective-permute-start | bytes 1769480 | tf_op jit(solution)/shard_map/ppermute | solution.py:91
  244.7 18.4 %collective-permute-start.55 = (bf16[192,1152]{1,0:T(8,128)(2,1)S(1)}, bf16[192,1152]{1,0:T(8,128)(2,1)S(1)}, u32[]{:S(2)}, u32[]{:S(2)}) collective-permute-start(bf16[192,1152]{1,0:T(8,128)(2,1)S(1)} %add_convert_fusion.8), channel_id=1, source_target_pairs={{8,0},{16,24},{9,1},{17,25},{10,2},{18,26},{11,3},{19,27},{12,4},{... | collective-permute-start | bytes 1327112 | tf_op jit(solution)/shard_map/ppermute | solution.py:91
  (123 other events, 773.9 us)

commit v5 on v4

--- a/solution.py
+++ b/solution.py
@@ -208,6 +208,7 @@
     local_tokens = latent_of(both_tokens, row, col)
     far_out = swap_row(after(w_out, far_joined), 2)
     far_up = swap_row(after(w_up, far_joined), 2)
+    local_tokens, far_out = lax.optimization_barrier((local_tokens, far_out))
     w_joined = gather_row(w_joined_own, far_joined)
     shift_attn, scale_attn, gate_attn, shift_mlp, scale_mlp, gate_mlp, bias_out, bias_down = (
         columns[:, i : i + 1] for i in range(8)
@@ -216,6 +217,7 @@
     x = local_tokens.astype(F32)
     normed_attn, inverse_attn = normalize(x)
     hidden_attn = (normed_attn * (1.0 + scale_attn) + shift_attn).astype(BF16)
+    hidden_attn, far_up = lax.optimization_barrier((hidden_attn, far_up))
     joined = contract(w_joined, hidden_attn, 0, 0)
 
     def split_heads(matrix):
@@ -230,7 +232,6 @@
     full_probs = exponent / jnp.sum(exponent, axis=-1, keepdims=True)
     probabilities = full_probs.astype(BF16)
     attended = contract_heads(values, probabilities, 2, 2).reshape(width_col, LEN).astype(BF16)
-    attended, far_out, far_up = lax.optimization_barrier((attended, far_out, far_up))
     w_out_all = gather_row(w_out, far_out)
     w_up_all = gather_row(w_up, far_up)
     far_down = swap_row(after(w_down, far_up), 2)
@@ -290,8 +291,8 @@
     grad_hidden = pair_sum(contract(w_joined, grad_joined, 1, 0))
     near_joined = near_sum(hidden_attn, grad_joined)
     grad_b_joined = jnp.sum(grad_joined.astype(F32), axis=1, keepdims=True)
-    grad_hidden, total_down, first_up, sum_out = lax.optimization_barrier(
-        (grad_hidden, total_down, first_up, sum_out)
+    grad_hidden, total_down, first_up, sum_out, near_joined = lax.optimization_barrier(
+        (grad_hidden, total_down, first_up, sum_out, near_joined)
     )
     sum_joined = far_sum(near_joined)
     grad_w_down = dp_third(total_down)
@@ -302,7 +303,10 @@
     grad_x = grad_residual + normalize_back(
         grad_hidden * (1.0 + scale_attn), normed_attn, inverse_attn
     )
-    spread = spread_out(jnp.concatenate([output, grad_x.astype(BF16)], axis=1), row, col)
+    both_out = jnp.concatenate([output, grad_x.astype(BF16)], axis=1)
+    both_out, sum_joined = lax.optimization_barrier((both_out, sum_joined))
+    first_joined = dp_first(sum_joined)
+    spread = spread_out(both_out, row, col)
     output = jnp.concatenate([part[:, :LEN] for part in spread], axis=1)
     grad_tokens = jnp.concatenate([part[:, LEN:] for part in spread], axis=1)
 
@@ -342,7 +346,9 @@
         ],
         axis=1,
     )
-    everyone = gather_dp(message)
+    everyone, first_joined, total_up = lax.optimization_barrier(
+        (gather_dp(message), first_joined, total_up)
+    )
     all_mod = everyone[:, : 6 * width_row]
     all_cond = everyone[:, 8 * width_row : 8 * width_row + width_col]
     grad_w_mod = contract(all_mod, all_cond, 0, 0).reshape(w_mod.shape)
@@ -354,7 +360,6 @@
     bias_sums = jnp.sum(bias_parts.reshape(-1, rows, bias_parts.shape[1]), axis=0).reshape(-1)
     hidden_width = grad_b_up.shape[0]
 
-    first_joined = dp_first(sum_joined)
     total_out = dp_second(first_out)
     grad_w_up = dp_third(total_up)
     total_joined = dp_second(first_joined)

time: 266 us -> 278 us (1.045)
  waiting for transfers between devices: 91.7 us -> 121 us
  starting transfers between devices: 77.5 us -> 68 us
  other arithmetic: 33.9 us -> 27.6 us
    ppermute x2, waiting for transfers between devices: 1.8 us -> 17.2 us  [gather_dp(): other = lax.ppermute(value, 'dp', [(i, i ^ step) for i in range(size)])]
    ppermute x4, starting transfers between devices: 23.2 us -> 15.1 us  [dp_first(): lax.ppermute(value, 'dp', dp_pairs()[0]).astype(F32)]
    ppermute x38, waiting for transfers between devices: 38.6 us -> 44.8 us  [swap_row(): return lax.ppermute(value, 'row', [(i, i ^ offset) for i in range(size)])]
    ppermute x7, waiting for transfers between devices: 11.8 us -> 16.9 us  [swap_col(): return lax.ppermute(value, 'col', [(0, 1), (1, 0)])]
    ppermute x3, waiting for transfers between devices: 0.01 us -> 3.06 us  [spread_out(): lax.ppermute(full[place * width:(place + 1) * width], ('row', 'col'), pairs)]
    convert_element_type x3 -> x4, other arithmetic: 3.6 us -> 6 us  [far_sum(): return (near[0] + swap_row(near[1], 2).astype(F32)).astype(BF16)]
    unnamed x197 -> x119, local copies, waits for them, and re-layouts: 9.95 us -> 9.66 us
  transfers between devices with their start and end apart: 62 -> 62, of which waited for: 23 -> 26; matrix products, arithmetic and copies ran while one was open for 30% -> 24% of each run, Pallas kernels for 0% -> 0%
where the time goes in v5:
time: 278 us; the launch traced here: 277 us
  waiting for transfers between devices  121 us (44%)
  starting transfers between devices  68 us (24%)
  matrix products  40.2 us (14%)
  other arithmetic  27.6 us (10%)
  local copies, waits for them, and re-layouts  17.7 us (6%)
    ppermute x38, waiting for transfers between devices, swap_row(): return lax.ppermute(value, 'row', [(i, i ^ offset) for i in range(size)])  44.8 us
    dot_general x23, matrix products, contract(): lax.dot_general(left, right, (((left_dim,), (right_dim,)), ((), ())), pre...  34.5 us
    ppermute x4, waiting for transfers between devices, dp_third(): back = lax.ppermute(total, 'dp', dp_pairs()[2])  29.5 us
    ppermute x38, starting transfers between devices, swap_row(): return lax.ppermute(value, 'row', [(i, i ^ offset) for i in range(size)])  27.4 us
    ppermute x2, waiting for transfers between devices, gather_dp(): other = lax.ppermute(value, 'dp', [(i, i ^ step) for i in range(size)])  17.2 us
    ppermute x7, waiting for transfers between devices, swap_col(): return lax.ppermute(value, 'col', [(0, 1), (1, 0)])  16.9 us
    ppermute x4, starting transfers between devices, dp_first(): lax.ppermute(value, 'dp', dp_pairs()[0]).astype(F32)  15.1 us
    ppermute x4, waiting for transfers between devices, dp_first(): lax.ppermute(value, 'dp', dp_pairs()[0]).astype(F32)  9.78 us
  transfers between devices with their start and end apart: 62, of which 26 were waited for; matrix products, arithmetic and copies ran while one was open for 24% of the time, Pallas kernels for 0%

profile of v5, /device:TPU:0, one launch (start us, length us, event | category | flops | bytes accessed | tf_op | source)
XLA Modules:
  0.0 276.8 jit_solution(6789722746461248947)
XLA Ops:
  1.5 2.5 collective-permute-start.2
  18.0 2.2 collective-permute-done.3
  21.2 5.7 %collective-permute-done.4 = bf16[192,1152]{1,0:T(8,128)(2,1)} collective-permute-done((bf16[192,1152]{1,0:T(8,128)(2,1)}, bf16[192,1152]{1,0:T(8,128)(2,1)}, u32[]{:S(2)}, u32[]{:S(2)}) %collective-permute-start.4) | collective-permute-done | bytes 442400 | tf_op jit(solution)/shard_map/ppermute | solution.py:30
  34.8 2.1 collective-permute-done.7
  42.3 10.2 %collective-permute-done.18 = bf16[192,1536]{1,0:T(8,128)(2,1)S(1)} collective-permute-done((bf16[192,1536]{1,0:T(8,128)(2,1)S(1)}, bf16[192,1536]{1,0:T(8,128)(2,1)S(1)}, u32[]{:S(2)}, u32[]{:S(2)}) %collective-permute-start.18) | collective-permute-done | bytes 589856 | tf_op jit(solution)/shard_map/ppermute | solution.py:30
  53.3 2.1 fusion.36
  66.4 11.9 %collective-permute-done.23 = bf16[192,256]{1,0:T(8,128)(2,1)S(1)} collective-permute-done((bf16[192,256]{1,0:T(8,128)(2,1)S(1)}, bf16[192,256]{1,0:T(8,128)(2,1)S(1)}, u32[]{:S(2)}, u32[]{:S(2)}) %collective-permute-start.23) | collective-permute-done | bytes 98336 | tf_op jit(solution)/shard_map/ppermute | solution.py:30
  90.7 2.6 fusion.108
  93.3 7.0 %collective-permute-done.28 = bf16[768,256]{1,0:T(8,128)(2,1)} collective-permute-done((bf16[768,256]{1,0:T(8,128)(2,1)}, bf16[768,256]{1,0:T(8,128)(2,1)}, u32[]{:S(2)}, u32[]{:S(2)}) %collective-permute-start.28) | collective-permute-done | bytes 393248 | tf_op jit(solution)/shard_map/ppermute | solution.py:34
  104.7 2.4 convert_add_fusion.1
  107.1 2.3 add_convert_fusion.6
  112.3 7.7 %collective-permute-done.31 = bf16[768,256]{1,0:T(8,128)(2,1)S(1)} collective-permute-done((bf16[768,256]{1,0:T(8,128)(2,1)S(1)}, bf16[768,256]{1,0:T(8,128)(2,1)S(1)}, u32[]{:S(2)}, u32[]{:S(2)}) %collective-permute-start.31) | collective-permute-done | bytes 393248 | tf_op jit(solution)/shard_map/ppermute | solution.py:34
  128.6 3.8 %collective-permute-start.33 = (bf16[192,1536]{1,0:T(8,128)(2,1)}, bf16[192,1536]{1,0:T(8,128)(2,1)S(1)}, u32[]{:S(2)}, u32[]{:S(2)}) collective-permute-start(bf16[192,1536]{1,0:T(8,128)(2,1)} %add_convert_fusion.5), channel_id=1, source_target_pairs={{0,8},{24,16},{1,9},{25,17},{2,10},{26,18},{3,11},{27,19},{4,12},{... | collective-permute-start | bytes 1769480 | tf_op jit(solution)/shard_map/ppermute | solution.py:73
  132.4 4.6 %collective-permute-done.34 = bf16[192,1536]{1,0:T(8,128)(2,1)} collective-permute-done((bf16[192,1536]{1,0:T(8,128)(2,1)}, bf16[192,1536]{1,0:T(8,128)(2,1)}, u32[]{:S(2)}, u32[]{:S(2)}) %collective-permute-start.34) | collective-permute-done | bytes 589856 | tf_op jit(solution)/shard_map/ppermute | solution.py:30
  137.0 2.3 add_convert_fusion.3
  142.3 2.4 multiply_convert_fusion
  148.8 2.6 convolution_convert_fusion.3
  155.9 5.5 %collective-permute-start.37 = (bf16[192,1536]{1,0:T(8,128)(2,1)}, bf16[192,1536]{1,0:T(8,128)(2,1)S(1)}, u32[]{:S(2)}, u32[]{:S(2)}) collective-permute-start(bf16[192,1536]{1,0:T(8,128)(2,1)} %add_convert_fusion.3), channel_id=1, source_target_pairs={{0,8},{24,16},{1,9},{25,17},{2,10},{26,18},{3,11},{27,19},{4,12},{... | collective-permute-start | bytes 1769480 | tf_op jit(solution)/shard_map/ppermute | solution.py:73
  164.4 7.0 %collective-permute-done.37 = bf16[192,1536]{1,0:T(8,128)(2,1)S(1)} collective-permute-done((bf16[192,1536]{1,0:T(8,128)(2,1)}, bf16[192,1536]{1,0:T(8,128)(2,1)S(1)}, u32[]{:S(2)}, u32[]{:S(2)}) %collective-permute-start.37) | collective-permute-done | bytes 589856 | tf_op jit(solution)/shard_map/ppermute | solution.py:73
  172.6 2.3 convolution_add_fusion.2
  174.9 2.2 fusion.2
  183.5 2.0 collective-permute-done.47
  190.3 4.3 %collective-permute-start.57 = (bf16[192,384]{1,0:T(8,128)(2,1)S(1)}, bf16[192,384]{1,0:T(8,128)(2,1)S(1)}, u32[]{:S(2)}, u32[]{:S(2)}) collective-permute-start(bf16[192,384]{1,0:T(8,128)(2,1)S(1)} %copy-done.28), channel_id=1, source_target_pairs={{0,8},{24,16},{1,9},{25,17},{2,10},{26,18},{3,11},{27,19},{4,12},{... | collective-permute-start | bytes 442376 | tf_op jit(solution)/shard_map/ppermute | solution.py:73
  195.9 2.7 collective-permute-start.51
  199.2 13.1 %collective-permute-done.51 = bf16[4,2496]{1,0:T(4,128)(2,1)S(1)} collective-permute-done((bf16[4,2496]{1,0:T(4,128)(2,1)S(1)}, bf16[4,2496]{1,0:T(4,128)(2,1)S(1)}, u32[]{:S(2)}, u32[]{:S(2)}) %collective-permute-start.51) | collective-permute-done | bytes 20000 | tf_op jit(solution)/shard_map/ppermute | solution.py:100
  213.2 4.2 %collective-permute-done.52 = bf16[8,2496]{1,0:T(8,128)(2,1)S(1)} collective-permute-done((bf16[8,2496]{1,0:T(8,128)(2,1)S(1)}, bf16[8,2496]{1,0:T(8,128)(2,1)S(1)}, u32[]{:S(2)}, u32[]{:S(2)}) %collective-permute-start.52) | collective-permute-done | bytes 39968 | tf_op jit(solution)/shard_map/ppermute | solution.py:100
  218.7 7.1 %collective-permute-done.59 = bf16[192,384]{1,0:T(8,128)(2,1)S(1)} collective-permute-done((bf16[192,384]{1,0:T(8,128)(2,1)S(1)}, bf16[192,384]{1,0:T(8,128)(2,1)S(1)}, u32[]{:S(2)}, u32[]{:S(2)}) %collective-permute-start.59) | collective-permute-done | bytes 147488 | tf_op jit(solution)/shard_map/ppermute | solution.py:91
  231.0 2.3 collective-permute-start.42
  237.1 3.1 %collective-permute-done.42 = bf16[192,512]{1,0:T(8,128)(2,1)S(1)} collective-permute-done((bf16[192,512]{1,0:T(8,128)(2,1)S(1)}, bf16[192,512]{1,0:T(8,128)(2,1)S(1)}, u32[]{:S(2)}, u32[]{:S(2)}) %collective-permute-start.42) | collective-permute-done | bytes 196640 | tf_op jit(solution)/shard_map/ppermute | solution.py:138
  241.7 2.8 %collective-permute-done.53 = bf16[192,1152]{1,0:T(8,128)(2,1)S(1)} collective-permute-done((bf16[192,1152]{1,0:T(8,128)(2,1)S(1)}, bf16[192,1152]{1,0:T(8,128)(2,1)S(1)}, u32[]{:S(2)}, u32[]{:S(2)}) %collective-permute-start.53) | collective-permute-done | bytes 442400 | tf_op jit(solution)/shard_map/ppermute | solution.py:73
  252.3 15.6 %collective-permute-done.60 = bf16[192,1536]{1,0:T(8,128)(2,1)S(1)} collective-permute-done((bf16[192,1536]{1,0:T(8,128)(2,1)S(1)}, bf16[192,1536]{1,0:T(8,128)(2,1)S(1)}, u32[]{:S(2)}, u32[]{:S(2)}) %collective-permute-start.60) | collective-permute-done | bytes 589856 | tf_op jit(solution)/shard_map/ppermute | solution.py:91
  269.0 6.8 %collective-permute-done.56 = bf16[192,1152]{1,0:T(8,128)(2,1)S(1)} collective-permute-done((bf16[192,1152]{1,0:T(8,128)(2,1)S(1)}, bf16[192,1152]{1,0:T(8,128)(2,1)S(1)}, u32[]{:S(2)}, u32[]{:S(2)}) %collective-permute-start.56) | collective-permute-done | bytes 442400 | tf_op jit(solution)/shard_map/ppermute | solution.py:91
  (356 shorter events, 119.4 us)
Async XLA Ops:
  1.5 10.2 %collective-permute-start.2 = (bf16[1,384]{1,0:T(2,128)(2,1)S(1)}, bf16[1,384]{1,0:T(2,128)(2,1)S(1)}, u32[]{:S(2)}, u32[]{:S(2)}) collective-permute-start(bf16[1,384]{1,0:T(2,128)(2,1)S(1)} %multiply_convert_fusion.4), channel_id=1, source_target_pairs={{0,6},{2,4},{4,2},{6,0},{1,7},{3,5},{5,3},{7,1},{8,14},{10,12},{12... | collective-permute-start | bytes 2312 | tf_op jit(solution)/shard_map/ppermute | solution.py:30
  4.7 15.4 %collective-permute-start.5 = (bf16[192,512]{1,0:T(8,128)(2,1)}, bf16[192,512]{1,0:T(8,128)(2,1)S(1)}, u32[]{:S(2)}, u32[]{:S(2)}) collective-permute-start(bf16[192,512]{1,0:T(8,128)(2,1)} %param.16), channel_id=1, source_target_pairs={{0,1},{1,0},{2,3},{3,2},{4,5},{5,4},{6,7},{7,6},{8,9},{9,8},{10,11... | collective-permute-start | bytes 589832 | tf_op jit(solution)/shard_map/ppermute | solution.py:34
  6.7 34.0 %collective-permute-start.14 = (bf16[192,384]{1,0:T(8,128)(2,1)}, bf16[192,384]{1,0:T(8,128)(2,1)}, u32[]{:S(2)}, u32[]{:S(2)}) collective-permute-start(bf16[192,384]{1,0:T(8,128)(2,1)} %param.25), channel_id=1, source_target_pairs={{0,2},{2,0},{4,6},{6,4},{1,3},{3,1},{5,7},{7,5},{8,10},{10,8},{12,... | collective-permute-start | bytes 442376 | tf_op jit(solution)/shard_map/ppermute | solution.py:30
  14.1 12.9 %collective-permute-start.4 = (bf16[192,1152]{1,0:T(8,128)(2,1)}, bf16[192,1152]{1,0:T(8,128)(2,1)}, u32[]{:S(2)}, u32[]{:S(2)}) collective-permute-start(bf16[192,1152]{1,0:T(8,128)(2,1)} %constant_dynamic-update-slice_fusion), channel_id=1, source_target_pairs={{0,4},{2,6},{4,0},{6,2},{1,5},{3,7},{5,1},{7,3},{8,12},{10,14},{12... | collective-permute-start | bytes 1327112 | tf_op jit(solution)/shard_map/ppermute | solution.py:30
  34.3 18.2 %collective-permute-start.16 = (bf16[192,1152]{1,0:T(8,128)(2,1)}, bf16[192,1152]{1,0:T(8,128)(2,1)S(1)}, u32[]{:S(2)}, u32[]{:S(2)}) collective-permute-start(bf16[192,1152]{1,0:T(8,128)(2,1)} %constant_dynamic-update-slice_fusion), channel_id=1, source_target_pairs={{0,2},{2,0},{4,6},{6,4},{1,3},{3,1},{5,7},{7,5},{8,10},{10,8},{12,... | collective-permute-start | bytes 1327112 | tf_op jit(solution)/shard_map/ppermute | solution.py:30
  34.6 18.6 %collective-permute-start.17 = (bf16[192,1152]{1,0:T(8,128)(2,1)}, bf16[192,1152]{1,0:T(8,128)(2,1)S(1)}, u32[]{:S(2)}, u32[]{:S(2)}) collective-permute-start(bf16[192,1152]{1,0:T(8,128)(2,1)} %collective-permute-done.4), channel_id=1, source_target_pairs={{0,2},{2,0},{4,6},{6,4},{1,3},{3,1},{5,7},{7,5},{8,10},{10,8},{12,... | collective-permute-start | bytes 1327112 | tf_op jit(solution)/shard_map/ppermute | solution.py:30
  36.9 15.5 %collective-permute-start.18 = (bf16[192,1536]{1,0:T(8,128)(2,1)S(1)}, bf16[192,1536]{1,0:T(8,128)(2,1)S(1)}, u32[]{:S(2)}, u32[]{:S(2)}) collective-permute-start(bf16[192,1536]{1,0:T(8,128)(2,1)S(1)} %copy-done.24), channel_id=1, source_target_pairs={{0,4},{2,6},{4,0},{6,2},{1,5},{3,7},{5,1},{7,3},{8,12},{10,14},{12... | collective-permute-start | bytes 1769480 | tf_op jit(solution)/shard_map/ppermute | solution.py:30
  40.7 23.1 %collective-permute-start.26 = (bf16[192,1536]{1,0:T(8,128)(2,1)S(1)}, bf16[192,1536]{1,0:T(8,128)(2,1)}, u32[]{:S(2)}, u32[]{:S(2)}) collective-permute-start(bf16[192,1536]{1,0:T(8,128)(2,1)S(1)} %copy-done.24), channel_id=1, source_target_pairs={{0,2},{2,0},{4,6},{6,4},{1,3},{3,1},{5,7},{7,5},{8,10},{10,8},{12,... | collective-permute-start | bytes 1769480 | tf_op jit(solution)/shard_map/ppermute | solution.py:30
  59.8 20.5 %collective-permute-start.19 = (bf16[768,256]{1,0:T(8,128)(2,1)S(1)}, bf16[768,256]{1,0:T(8,128)(2,1)S(1)}, u32[]{:S(2)}, u32[]{:S(2)}) collective-permute-start(bf16[768,256]{1,0:T(8,128)(2,1)S(1)} %convolution_convert_fusion.5), channel_id=1, source_target_pairs={{0,1},{1,0},{2,3},{3,2},{4,5},{5,4},{6,7},{7,6},{8,9},{9,8},{10,11... | collective-permute-start | bytes 1179656 | tf_op jit(solution)/shard_map/ppermute | solution.py:34
  61.5 18.9 %collective-permute-start.20 = (bf16[192,1536]{1,0:T(8,128)(2,1)S(1)}, bf16[192,1536]{1,0:T(8,128)(2,1)S(1)}, u32[]{:S(2)}, u32[]{:S(2)}) collective-permute-start(bf16[192,1536]{1,0:T(8,128)(2,1)S(1)} %copy-done.25), channel_id=1, source_target_pairs={{0,4},{2,6},{4,0},{6,2},{1,5},{3,7},{5,1},{7,3},{8,12},{10,14},{12... | collective-permute-start | bytes 1769480 | tf_op jit(solution)/shard_map/ppermute | solution.py:30
  62.9 15.3 %collective-permute-start.23 = (bf16[192,256]{1,0:T(8,128)(2,1)S(1)}, bf16[192,256]{1,0:T(8,128)(2,1)S(1)}, u32[]{:S(2)}, u32[]{:S(2)}) collective-permute-start(bf16[192,256]{1,0:T(8,128)(2,1)S(1)} %get-tuple-element.133), channel_id=1, source_target_pairs={{0,6},{2,4},{4,2},{6,0},{1,7},{3,5},{5,3},{7,1},{8,14},{10,12},{12... | collective-permute-start | bytes 294920 | tf_op jit(solution)/shard_map/ppermute | solution.py:30
  63.0 15.9 %collective-permute-start.22 = (bf16[192,256]{1,0:T(8,128)(2,1)S(1)}, bf16[192,256]{1,0:T(8,128)(2,1)S(1)}, u32[]{:S(2)}, u32[]{:S(2)}) collective-permute-start(bf16[192,256]{1,0:T(8,128)(2,1)S(1)} %get-tuple-element.134), channel_id=1, source_target_pairs={{0,2},{2,0},{4,6},{6,4},{1,3},{3,1},{5,7},{7,5},{8,10},{10,8},{12,... | collective-permute-start | bytes 294920 | tf_op jit(solution)/shard_map/ppermute | solution.py:30
  63.8 16.3 %collective-permute-start.21 = (bf16[192,256]{1,0:T(8,128)(2,1)S(1)}, bf16[192,256]{1,0:T(8,128)(2,1)S(1)}, u32[]{:S(2)}, u32[]{:S(2)}) collective-permute-start(bf16[192,256]{1,0:T(8,128)(2,1)S(1)} %get-tuple-element.135), channel_id=1, source_target_pairs={{0,4},{2,6},{4,0},{6,2},{1,5},{3,7},{5,1},{7,3},{8,12},{10,14},{12... | collective-permute-start | bytes 294920 | tf_op jit(solution)/shard_map/ppermute | solution.py:30
  84.5 17.1 %collective-permute-start.29 = (bf16[384,1536]{1,0:T(8,128)(2,1)}, bf16[384,1536]{1,0:T(8,128)(2,1)}, u32[]{:S(2)}, u32[]{:S(2)}) collective-permute-start(bf16[384,1536]{1,0:T(8,128)(2,1)} %convolution_convert_fusion.2), channel_id=1, source_target_pairs={{0,2},{2,0},{4,6},{6,4},{1,3},{3,1},{5,7},{7,5},{8,10},{10,8},{12,... | collective-permute-start | bytes 3538952 | tf_op jit(solution)/shard_map/ppermute | solution.py:30
  88.7 11.7 %collective-permute-start.28 = (bf16[768,256]{1,0:T(8,128)(2,1)}, bf16[768,256]{1,0:T(8,128)(2,1)}, u32[]{:S(2)}, u32[]{:S(2)}) collective-permute-start(bf16[768,256]{1,0:T(8,128)(2,1)} %convolution_convert_fusion.4), channel_id=1, source_target_pairs={{0,1},{1,0},{2,3},{3,2},{4,5},{5,4},{6,7},{7,6},{8,9},{9,8},{10,11... | collective-permute-start | bytes 1179656 | tf_op jit(solution)/shard_map/ppermute | solution.py:34
  90.6 14.1 %collective-permute-start.30 = (bf16[384,1536]{1,0:T(8,128)(2,1)}, bf16[384,1536]{1,0:T(8,128)(2,1)}, u32[]{:S(2)}, u32[]{:S(2)}) collective-permute-start(bf16[384,1536]{1,0:T(8,128)(2,1)} %convolution_convert_fusion.1), channel_id=1, source_target_pairs={{0,2},{2,0},{4,6},{6,4},{1,3},{3,1},{5,7},{7,5},{8,10},{10,8},{12,... | collective-permute-start | bytes 3538952 | tf_op jit(solution)/shard_map/ppermute | solution.py:30
  109.3 10.6 %collective-permute-start.31 = (bf16[768,256]{1,0:T(8,128)(2,1)S(1)}, bf16[768,256]{1,0:T(8,128)(2,1)S(1)}, u32[]{:S(2)}, u32[]{:S(2)}) collective-permute-start(bf16[768,256]{1,0:T(8,128)(2,1)S(1)} %fusion.108), channel_id=1, source_target_pairs={{0,1},{1,0},{2,3},{3,2},{4,5},{5,4},{6,7},{7,6},{8,9},{9,8},{10,11... | collective-permute-start | bytes 1179656 | tf_op jit(solution)/shard_map/ppermute | solution.py:34
  109.7 16.3 %collective-permute-start.32 = (bf16[192,1536]{1,0:T(8,128)(2,1)S(1)}, bf16[192,1536]{1,0:T(8,128)(2,1)S(1)}, u32[]{:S(2)}, u32[]{:S(2)}) collective-permute-start(bf16[192,1536]{1,0:T(8,128)(2,1)S(1)} %add_convert_fusion.7), channel_id=1, source_target_pairs={{0,4},{2,6},{4,0},{6,2},{1,5},{3,7},{5,1},{7,3},{8,12},{10,14},{12... | collective-permute-start | bytes 1769480 | tf_op jit(solution)/shard_map/ppermute | solution.py:30
  111.5 25.5 %collective-permute-start.34 = (bf16[192,1536]{1,0:T(8,128)(2,1)}, bf16[192,1536]{1,0:T(8,128)(2,1)}, u32[]{:S(2)}, u32[]{:S(2)}) collective-permute-start(bf16[192,1536]{1,0:T(8,128)(2,1)} %add_convert_fusion.6), channel_id=1, source_target_pairs={{0,4},{2,6},{4,0},{6,2},{1,5},{3,7},{5,1},{7,3},{8,12},{10,14},{12... | collective-permute-start | bytes 1769480 | tf_op jit(solution)/shard_map/ppermute | solution.py:30
  125.8 13.6 %collective-permute-start.38 = (bf16[384,384]{1,0:T(8,128)(2,1)}, bf16[384,384]{1,0:T(8,128)(2,1)}, u32[]{:S(2)}, u32[]{:S(2)}) collective-permute-start(bf16[384,384]{1,0:T(8,128)(2,1)} %convolution_convert_fusion.6), channel_id=1, source_target_pairs={{0,2},{2,0},{4,6},{6,4},{1,3},{3,1},{5,7},{7,5},{8,10},{10,8},{12,... | collective-permute-start | bytes 884744 | tf_op jit(solution)/shard_map/ppermute | solution.py:30
  128.6 18.8 %collective-permute-start.33 = (bf16[192,1536]{1,0:T(8,128)(2,1)}, bf16[192,1536]{1,0:T(8,128)(2,1)S(1)}, u32[]{:S(2)}, u32[]{:S(2)}) collective-permute-start(bf16[192,1536]{1,0:T(8,128)(2,1)} %add_convert_fusion.5), channel_id=1, source_target_pairs={{0,8},{24,16},{1,9},{25,17},{2,10},{26,18},{3,11},{27,19},{4,12},{... | collective-permute-start | bytes 1769480 | tf_op jit(solution)/shard_map/ppermute | solution.py:73
  151.4 10.5 %collective-permute-start.35 = (bf16[768,256]{1,0:T(8,128)(2,1)}, bf16[768,256]{1,0:T(8,128)(2,1)}, u32[]{:S(2)}, u32[]{:S(2)}) collective-permute-start(bf16[768,256]{1,0:T(8,128)(2,1)} %convolution_convert_fusion.3), channel_id=1, source_target_pairs={{0,1},{1,0},{2,3},{3,2},{4,5},{5,4},{6,7},{7,6},{8,9},{9,8},{10,11... | collective-permute-start | bytes 1179656 | tf_op jit(solution)/shard_map/ppermute | solution.py:34
  155.9 15.5 %collective-permute-start.37 = (bf16[192,1536]{1,0:T(8,128)(2,1)}, bf16[192,1536]{1,0:T(8,128)(2,1)S(1)}, u32[]{:S(2)}, u32[]{:S(2)}) collective-permute-start(bf16[192,1536]{1,0:T(8,128)(2,1)} %add_convert_fusion.3), channel_id=1, source_target_pairs={{0,8},{24,16},{1,9},{25,17},{2,10},{26,18},{3,11},{27,19},{4,12},{... | collective-permute-start | bytes 1769480 | tf_op jit(solution)/shard_map/ppermute | solution.py:73
  161.4 11.2 %collective-permute-start.40 = (bf16[384,1152]{1,0:T(8,128)(2,1)}, bf16[384,1152]{1,0:T(8,128)(2,1)}, u32[]{:S(2)}, u32[]{:S(2)}) collective-permute-start(bf16[384,1152]{1,0:T(8,128)(2,1)} %convolution_convert_fusion), channel_id=1, source_target_pairs={{0,2},{2,0},{4,6},{6,4},{1,3},{3,1},{5,7},{7,5},{8,10},{10,8},{12,... | collective-permute-start | bytes 2654216 | tf_op jit(solution)/shard_map/ppermute | solution.py:30
  177.6 49.0 %collective-permute-start.41 = (bf16[192,1152]{1,0:T(8,128)(2,1)}, bf16[192,1152]{1,0:T(8,128)(2,1)}, u32[]{:S(2)}, u32[]{:S(2)}) collective-permute-start(bf16[192,1152]{1,0:T(8,128)(2,1)} %fusion.2), channel_id=1, source_target_pairs={{0,4},{2,6},{4,0},{6,2},{1,5},{3,7},{5,1},{7,3},{8,12},{10,14},{12... | collective-permute-start | bytes 1327112 | tf_op jit(solution)/shard_map/ppermute | solution.py:30
  181.7 54.2 %collective-permute-start.54 = (bf16[192,1536]{1,0:T(8,128)(2,1)S(1)}, bf16[192,1536]{1,0:T(8,128)(2,1)}, u32[]{:S(2)}, u32[]{:S(2)}) collective-permute-start(bf16[192,1536]{1,0:T(8,128)(2,1)S(1)} %add_convert_fusion.1), channel_id=1, source_target_pairs={{8,16},{16,8},{9,17},{17,9},{10,18},{18,10},{11,19},{19,11},{12,20... | collective-permute-start | bytes 1769480 | tf_op jit(solution)/shard_map/ppermute | solution.py:78
  190.3 22.2 %collective-permute-start.57 = (bf16[192,384]{1,0:T(8,128)(2,1)S(1)}, bf16[192,384]{1,0:T(8,128)(2,1)S(1)}, u32[]{:S(2)}, u32[]{:S(2)}) collective-permute-start(bf16[192,384]{1,0:T(8,128)(2,1)S(1)} %copy-done.28), channel_id=1, source_target_pairs={{0,8},{24,16},{1,9},{25,17},{2,10},{26,18},{3,11},{27,19},{4,12},{... | collective-permute-start | bytes 442376 | tf_op jit(solution)/shard_map/ppermute | solution.py:73
  194.6 38.7 %collective-permute-start.61 = (bf16[192,1536]{1,0:T(8,128)(2,1)S(1)}, bf16[192,1536]{1,0:T(8,128)(2,1)S(1)}, u32[]{:S(2)}, u32[]{:S(2)}) collective-permute-start(bf16[192,1536]{1,0:T(8,128)(2,1)S(1)} %add_convert_fusion.2), channel_id=1, source_target_pairs={{8,0},{16,24},{9,1},{17,25},{10,2},{18,26},{11,3},{19,27},{12,4},{... | collective-permute-start | bytes 1769480 | tf_op jit(solution)/shard_map/ppermute | solution.py:91
  195.9 16.4 %collective-permute-start.51 = (bf16[4,2496]{1,0:T(4,128)(2,1)S(1)}, bf16[4,2496]{1,0:T(4,128)(2,1)S(1)}, u32[]{:S(2)}, u32[]{:S(2)}) collective-permute-start(bf16[4,2496]{1,0:T(4,128)(2,1)S(1)} %pad_maximum_fusion.11), channel_id=1, source_target_pairs={{0,8},{8,0},{16,24},{24,16},{1,9},{9,1},{17,25},{25,17},{2,10},{10... | collective-permute-start | bytes 59912 | tf_op jit(solution)/shard_map/ppermute | solution.py:100
  233.3 11.3 %collective-permute-start.53 = (bf16[192,1152]{1,0:T(8,128)(2,1)S(1)}, bf16[192,1152]{1,0:T(8,128)(2,1)S(1)}, u32[]{:S(2)}, u32[]{:S(2)}) collective-permute-start(bf16[192,1152]{1,0:T(8,128)(2,1)S(1)} %add_convert_fusion.10), channel_id=1, source_target_pairs={{0,8},{24,16},{1,9},{25,17},{2,10},{26,18},{3,11},{27,19},{4,12},{... | collective-permute-start | bytes 1327112 | tf_op jit(solution)/shard_map/ppermute | solution.py:73
  247.1 20.8 %collective-permute-start.60 = (bf16[192,1536]{1,0:T(8,128)(2,1)S(1)}, bf16[192,1536]{1,0:T(8,128)(2,1)S(1)}, u32[]{:S(2)}, u32[]{:S(2)}) collective-permute-start(bf16[192,1536]{1,0:T(8,128)(2,1)S(1)} %add_convert_fusion), channel_id=1, source_target_pairs={{8,0},{16,24},{9,1},{17,25},{10,2},{18,26},{11,3},{19,27},{12,4},{... | collective-permute-start | bytes 1769480 | tf_op jit(solution)/shard_map/ppermute | solution.py:91
  251.0 24.8 %collective-permute-start.56 = (bf16[192,1152]{1,0:T(8,128)(2,1)S(1)}, bf16[192,1152]{1,0:T(8,128)(2,1)S(1)}, u32[]{:S(2)}, u32[]{:S(2)}) collective-permute-start(bf16[192,1152]{1,0:T(8,128)(2,1)S(1)} %add_convert_fusion.8), channel_id=1, source_target_pairs={{8,0},{16,24},{9,1},{17,25},{10,2},{18,26},{11,3},{19,27},{12,4},{... | collective-permute-start | bytes 1327112 | tf_op jit(solution)/shard_map/ppermute | solution.py:91
  (84 other events, 526.4 us)
